TPU v7x, 256 devices: a whole 4x4x8 slice. The times are simulated.
256 devices in a mesh: corpus: 32 (over x, y, core), qbatch: 8 (over z).
Axes of the slice: x: 4, y: 4, z: 8, core: 2. Of those that a mesh axis runs over, the one named last changes fastest.
Arguments:
- query_tokens: bfloat16 [4096, 32, 128], P(('corpus', 'qbatch')), may hold values from -6 to 6
- visit_owner: int32 [4096, 8], P(('corpus', 'qbatch')), may hold values from 0 to 255, as said below
- visit_passages: int32 [4096, 8, 8], P(('corpus', 'qbatch')), may hold values from 0 to 63
- passage_tokens: bfloat16 [16384, 128, 128], P(('corpus', 'qbatch')), may hold values from -0.015625 to 0.015625
- passage_lengths: int32 [16384], P(('corpus', 'qbatch')), may hold values from 16 to 128
Outputs:
- scores: float32 [4096, 64], P(('corpus', 'qbatch'))
Inputs may be any that keep to these rules, and one draw needn't show every extreme that they name: `visit_owner`: the 8 owners of one query differ. The 128 queries of the devices that share a corpus index visit exactly half of the 256 owners, each of them exactly 8 times; some owners are visited so by every such group.
All inputs are finite; a program needn't handle non-finite values.
Results may differ from a plain program's by a relative error of at most 0.0003.
Values may be sent and summed in bfloat16 or wider, within the bound.
No kernel may reach another device: no remote copies, remote signals or barrier semaphores. Data moves between devices by JAX's collectives and lax.ppermute only.
A program may use at most 64 MiB of HBM per device.

v0:
```python
import jax
import jax.numpy as jnp
from jax import lax
from jax.sharding import PartitionSpec as P

slot_block = 32


def exclusive_count(flags):
    length = flags.shape[0]
    positions = jnp.arange(length, dtype=jnp.int32)
    lower = (positions[:, None] > positions[None, :]).astype(jnp.float32)
    return jnp.dot(lower, flags.astype(jnp.float32), precision=lax.Precision.HIGHEST).astype(
        jnp.int32
    )


def score_group(flat_tokens, cand_ids, passage_tokens, passage_lengths, query_len):
    slots_here = flat_tokens.shape[0]
    per_visit = cand_ids.shape[1]
    local_passages, passage_len, feature_width = passage_tokens.shape
    queries = flat_tokens.reshape(slots_here, query_len, feature_width)
    passage_index = jnp.arange(local_passages, dtype=jnp.int32)
    picks = cand_ids.reshape(-1)[:, None] == passage_index[None, :]
    picked = jnp.dot(
        picks.astype(jnp.bfloat16),
        passage_tokens.reshape(local_passages, passage_len * feature_width),
        preferred_element_type=jnp.float32,
    )
    passages = picked.astype(jnp.bfloat16).reshape(
        slots_here, per_visit, passage_len, feature_width
    )
    lengths = jnp.sum(jnp.where(picks, passage_lengths[None, :], 0), axis=1).reshape(
        slots_here, per_visit
    )
    similarity = jnp.einsum("sid,skjd->skij", queries, passages, preferred_element_type=jnp.float32)
    token_index = jnp.arange(passage_len, dtype=jnp.int32)
    in_length = token_index[None, None, None, :] < lengths[:, :, None, None]
    best_match = jnp.max(jnp.where(in_length, similarity, -1e30), axis=3)
    return jnp.where(cand_ids >= 0, jnp.sum(best_match, axis=2), 0.0)


def score_slots(flat_tokens, cand_ids, passage_tokens, passage_lengths, query_len):
    slots_total = flat_tokens.shape[0]
    per_visit = cand_ids.shape[1]
    rounds = -(-slots_total // slot_block)
    padded_len = rounds * slot_block
    tokens_pad = flat_tokens.reshape(rounds, slot_block, flat_tokens.shape[1])
    cands_pad = cand_ids.reshape(rounds, slot_block, per_visit)

    def one_block(pieces):
        return score_group(pieces[0], pieces[1], passage_tokens, passage_lengths, query_len)

    results = lax.map(one_block, (tokens_pad, cands_pad))
    return results.reshape(padded_len, per_visit)


def shards(query_tokens, visit_owner, visit_passages, passage_tokens, passage_lengths):
    corpus_count = lax.axis_size("corpus")
    batch_count = lax.axis_size("qbatch")
    my_row = lax.axis_index("qbatch")
    local_queries, query_len, feature_width = query_tokens.shape
    visit_count = visit_owner.shape[1]
    per_visit = visit_passages.shape[2]
    capacity = 2 * local_queries * visit_count // corpus_count
    slot_count = corpus_count * capacity
    token_row = query_len * feature_width
    group_tokens, group_owner, group_cands = (
        lax.all_gather(query_tokens, "qbatch", axis=0, tiled=True),
        lax.all_gather(visit_owner, "qbatch", axis=0, tiled=True),
        lax.all_gather(visit_passages, "qbatch", axis=0, tiled=True),
    )
    group_size = group_tokens.shape[0]
    flat_owner = group_owner.reshape(-1)
    visit_total = flat_owner.shape[0]
    target_column = flat_owner // batch_count
    is_mine = flat_owner % batch_count == my_row
    column_hits = (
        (target_column[:, None] == jnp.arange(corpus_count, dtype=jnp.int32)[None, :])
        & is_mine[:, None]
    ).astype(jnp.int32)
    earlier = exclusive_count(column_hits)
    visit_rank = jnp.sum(earlier * column_hits, axis=1)
    visit_slot = jnp.where(is_mine, target_column * capacity + visit_rank, slot_count)
    slot_match = visit_slot[None, :] == jnp.arange(slot_count, dtype=jnp.int32)[:, None]
    slot_live = jnp.any(slot_match, axis=1)
    query_pick = jnp.any(slot_match.reshape(slot_count, group_size, visit_count), axis=2)
    flat_group = group_tokens.reshape(group_size, token_row)
    send_tokens = jnp.dot(
        query_pick.astype(jnp.bfloat16), flat_group, preferred_element_type=jnp.float32
    ).astype(jnp.bfloat16)
    match_float = slot_match.astype(jnp.float32)
    picked_cands = jnp.dot(
        match_float,
        group_cands.reshape(visit_total, per_visit).astype(jnp.float32),
        precision=lax.Precision.HIGHEST,
    ).astype(jnp.int32)
    send_cands = jnp.where(slot_live[:, None], picked_cands, -1)
    send_tokens = send_tokens.reshape(corpus_count, capacity, token_row)
    send_cands = send_cands.reshape(corpus_count, capacity, per_visit)
    got_tokens = lax.all_to_all(send_tokens, "corpus", split_axis=0, concat_axis=0, tiled=True)
    got_cands = lax.all_to_all(send_cands, "corpus", split_axis=0, concat_axis=0, tiled=True)
    item_count = got_tokens.shape[1]
    scored = score_slots(
        got_tokens.reshape(-1, token_row),
        got_cands.reshape(-1, per_visit),
        passage_tokens,
        passage_lengths,
        query_len,
    )
    returned = lax.all_to_all(
        scored.reshape(corpus_count, item_count, per_visit),
        "corpus",
        split_axis=0,
        concat_axis=0,
        tiled=True,
    )
    slot_scores = returned.reshape(slot_count, per_visit)
    visit_scores = jnp.dot(match_float.T, slot_scores, precision=lax.Precision.HIGHEST)
    group_scores = visit_scores.reshape(group_size, visit_count * per_visit)
    final_scores = lax.psum_scatter(group_scores, "qbatch", scatter_dimension=0, tiled=True)
    return final_scores


def solution(mesh):
    placed = (
        P(("corpus", "qbatch"), None, None),
        P(("corpus", "qbatch"), None),
        P(("corpus", "qbatch"), None, None),
        P(("corpus", "qbatch"), None, None),
        P(("corpus", "qbatch")),
    )
    return jax.shard_map(
        shards, mesh=mesh, in_specs=placed, out_specs=P(("corpus", "qbatch"), None), check_vma=False
    )
```

profile of v0, /device:TPU:2, one launch (start us, length us, event | category | flops | bytes accessed | tf_op | source)
XLA Modules:
  0.0 223.4 jit_solution(1819615360569038757)
XLA Ops:
  7.3 28.2 %all-gather = s32[8,16,8]{1,2,0:T(8,128)S(1)} all-gather(s32[1,16,8]{1,2,0:T(8,128)} %bitcast.59), channel_id=1, replica_groups=mesh['corpus'=32,'qbatch'=8] {'qbatch'}, dimensions={0}, use_global_device_ids=true | all-gather | bytes 4608 | tf_op jit(solution)/shard_map/all_gather | solution.py:70
  36.5 25.5 %all_gather.10 = s32[128,8,8]{2,1,0:T(8,128)S(1)} all-gather(s32[16,8,8]{2,1,0:T(8,128)S(1)} %copy.54), channel_id=1, replica_groups=mesh['corpus'=32,'qbatch'=8] {'qbatch'}, dimensions={0}, use_global_device_ids=true | all-gather | bytes 36864 | tf_op jit(solution)/shard_map/all_gather | solution.py:71
  62.7 1.2 fusion.14
  65.6 8.0 %all-to-all-start = ((s32[32,8,8]{1,2,0:T(8,128)}), s32[32,8,8]{1,2,0:T(8,128)S(1)}, u32[]{:S(2)}, u32[]{:S(2)}) async-start(s32[32,8,8]{1,2,0:T(8,128)} %copy.57), calls=%async_computation | async-start | bytes 262144 | tf_op jit(solution)/shard_map/all_to_all | solution.py:102
  74.3 3.3 %fusion.10 = bf16[32,8,4096]{2,1,0:T(8,128)(2,1)} fusion(pred[256,128]{1,0:T(8,128)(4,1)S(1)} %fusion.20, bf16[16,8,32,128]{3,2,1,0:T(8,128)(2,1)} %bitcast.56), kind=kOutput, calls=%fused_computation.17 | convolution fusion | flops 269484032 | bytes 3178496 | tf_op jit(solution)/shard_map/dot_general | solution.py:89
  77.6 2.7 %all-to-all-done = s32[32,8,8]{1,2,0:T(8,128)S(1)} async-done(((s32[32,8,8]{1,2,0:T(8,128)}), s32[32,8,8]{1,2,0:T(8,128)S(1)}, u32[]{:S(2)}, u32[]{:S(2)}) %all-to-all-start) | async-done | bytes 8224 | tf_op jit(solution)/shard_map/all_to_all | solution.py:102
  80.3 5.8 %all-to-all-start.1 = ((bf16[32,8,4096]{2,1,0:T(8,128)(2,1)}), bf16[32,8,4096]{2,1,0:T(8,128)(2,1)}, u32[]{:S(2)}, u32[]{:S(2)}) async-start(bf16[32,8,4096]{2,1,0:T(8,128)(2,1)} %fusion.10), calls=%async_computation.1 | async-start | bytes 4194304 | tf_op jit(solution)/shard_map/all_to_all | solution.py:101
  86.3 25.8 %all-to-all-done.1 = bf16[32,8,4096]{2,1,0:T(8,128)(2,1)} async-done(((bf16[32,8,4096]{2,1,0:T(8,128)(2,1)}), bf16[32,8,4096]{2,1,0:T(8,128)(2,1)}, u32[]{:S(2)}, u32[]{:S(2)}) %all-to-all-start.1) | async-done | bytes 2097184 | tf_op jit(solution)/shard_map/all_to_all | solution.py:101
  112.1 56.8 %while.10 = (s32[]{:T(128)}, f32[8,32,8]{2,1,0:T(8,128)S(1)}, s32[8,32,8]{2,1,0:T(8,128)S(1)}, s32[64]{0:T(128)S(1)}, bf16[64,128,128]{2,1,0:T(8,128)(2,1)S(1)},...) while((s32[]{:T(128)}, f32[8,32,8]{2,1,0:T(8,128)S(1)}, s32[8,32,8]{2,1,0:T(8,128)S(1)}, ...), condition=%wide.region_7.8_spmd, body=%wide.region_3.7_spmd.sunk | while | flops 811696128 | bytes 20376940 | solution.py:54
  112.5 1.0 dynamic-slice_bitcast_fusion.2
  113.6 2.4 %fusion.51 = bf16[32,8,128,128]{3,1,2,0:T(8,128)(2,1)S(1)} fusion(bf16[8,8,128,128]{3,2,1,0:T(8,128)(2,1)S(1)} %bitcast.54, s32[256]{0:T(256)S(1)} %eq.170), kind=kOutput, calls=%fused_computation.3.clone.1 | convolution fusion | flops 541081600 | bytes 10486784 | tf_op jit(solution)/shard_map/while/body/eval_jaxpr/dot_general | solution.py:25
  116.0 3.1 %select_reduce_fusion.5 = f32[32,8,32]{2,1,0:T(8,128)S(1)} fusion(pred[32,8,128]{2,1,0:T(8,128)(4,1)S(1)} %iota_compare_fusion.18, bf16[32,8,128,128]{3,1,2,0:T(8,128)(2,1)S(1)} %fusion.51, bf16[32,32,128,1]{2,1,0,3:T(8,128)(2,1)S(1)} %bitcast.55), kind=kOutput, calls=%fused_computation.4.clone.1 | convolution fusion | flops 270524416 | bytes 8716288 | tf_op jit(solution)/shard_map/while/body/eval_jaxpr/sid,skjd->skij/dot_general | solution.py:36
  119.6 1.0 dynamic-slice_bitcast_fusion.2
  120.7 2.4 %fusion.51 = bf16[32,8,128,128]{3,1,2,0:T(8,128)(2,1)S(1)} fusion(bf16[8,8,128,128]{3,2,1,0:T(8,128)(2,1)S(1)} %bitcast.54, s32[256]{0:T(256)S(1)} %eq.170), kind=kOutput, calls=%fused_computation.3.clone.1 | convolution fusion | flops 541081600 | bytes 10486784 | tf_op jit(solution)/shard_map/while/body/eval_jaxpr/dot_general | solution.py:25
  123.1 3.1 %select_reduce_fusion.5 = f32[32,8,32]{2,1,0:T(8,128)S(1)} fusion(pred[32,8,128]{2,1,0:T(8,128)(4,1)S(1)} %iota_compare_fusion.18, bf16[32,8,128,128]{3,1,2,0:T(8,128)(2,1)S(1)} %fusion.51, bf16[32,32,128,1]{2,1,0,3:T(8,128)(2,1)S(1)} %bitcast.55), kind=kOutput, calls=%fused_computation.4.clone.1 | convolution fusion | flops 270524416 | bytes 8716288 | tf_op jit(solution)/shard_map/while/body/eval_jaxpr/sid,skjd->skij/dot_general | solution.py:36
  126.7 1.0 dynamic-slice_bitcast_fusion.2
  127.8 2.4 %fusion.51 = bf16[32,8,128,128]{3,1,2,0:T(8,128)(2,1)S(1)} fusion(bf16[8,8,128,128]{3,2,1,0:T(8,128)(2,1)S(1)} %bitcast.54, s32[256]{0:T(256)S(1)} %eq.170), kind=kOutput, calls=%fused_computation.3.clone.1 | convolution fusion | flops 541081600 | bytes 10486784 | tf_op jit(solution)/shard_map/while/body/eval_jaxpr/dot_general | solution.py:25
  130.2 3.1 %select_reduce_fusion.5 = f32[32,8,32]{2,1,0:T(8,128)S(1)} fusion(pred[32,8,128]{2,1,0:T(8,128)(4,1)S(1)} %iota_compare_fusion.18, bf16[32,8,128,128]{3,1,2,0:T(8,128)(2,1)S(1)} %fusion.51, bf16[32,32,128,1]{2,1,0,3:T(8,128)(2,1)S(1)} %bitcast.55), kind=kOutput, calls=%fused_computation.4.clone.1 | convolution fusion | flops 270524416 | bytes 8716288 | tf_op jit(solution)/shard_map/while/body/eval_jaxpr/sid,skjd->skij/dot_general | solution.py:36
  133.9 1.0 dynamic-slice_bitcast_fusion.2
  134.9 2.4 %fusion.51 = bf16[32,8,128,128]{3,1,2,0:T(8,128)(2,1)S(1)} fusion(bf16[8,8,128,128]{3,2,1,0:T(8,128)(2,1)S(1)} %bitcast.54, s32[256]{0:T(256)S(1)} %eq.170), kind=kOutput, calls=%fused_computation.3.clone.1 | convolution fusion | flops 541081600 | bytes 10486784 | tf_op jit(solution)/shard_map/while/body/eval_jaxpr/dot_general | solution.py:25
  137.3 3.1 %select_reduce_fusion.5 = f32[32,8,32]{2,1,0:T(8,128)S(1)} fusion(pred[32,8,128]{2,1,0:T(8,128)(4,1)S(1)} %iota_compare_fusion.18, bf16[32,8,128,128]{3,1,2,0:T(8,128)(2,1)S(1)} %fusion.51, bf16[32,32,128,1]{2,1,0,3:T(8,128)(2,1)S(1)} %bitcast.55), kind=kOutput, calls=%fused_computation.4.clone.1 | convolution fusion | flops 270524416 | bytes 8716288 | tf_op jit(solution)/shard_map/while/body/eval_jaxpr/sid,skjd->skij/dot_general | solution.py:36
  141.0 1.0 dynamic-slice_bitcast_fusion.2
  142.0 2.4 %fusion.51 = bf16[32,8,128,128]{3,1,2,0:T(8,128)(2,1)S(1)} fusion(bf16[8,8,128,128]{3,2,1,0:T(8,128)(2,1)S(1)} %bitcast.54, s32[256]{0:T(256)S(1)} %eq.170), kind=kOutput, calls=%fused_computation.3.clone.1 | convolution fusion | flops 541081600 | bytes 10486784 | tf_op jit(solution)/shard_map/while/body/eval_jaxpr/dot_general | solution.py:25
  144.4 3.1 %select_reduce_fusion.5 = f32[32,8,32]{2,1,0:T(8,128)S(1)} fusion(pred[32,8,128]{2,1,0:T(8,128)(4,1)S(1)} %iota_compare_fusion.18, bf16[32,8,128,128]{3,1,2,0:T(8,128)(2,1)S(1)} %fusion.51, bf16[32,32,128,1]{2,1,0,3:T(8,128)(2,1)S(1)} %bitcast.55), kind=kOutput, calls=%fused_computation.4.clone.1 | convolution fusion | flops 270524416 | bytes 8716288 | tf_op jit(solution)/shard_map/while/body/eval_jaxpr/sid,skjd->skij/dot_general | solution.py:36
  149.1 2.4 %fusion.51 = bf16[32,8,128,128]{3,1,2,0:T(8,128)(2,1)S(1)} fusion(bf16[8,8,128,128]{3,2,1,0:T(8,128)(2,1)S(1)} %bitcast.54, s32[256]{0:T(256)S(1)} %eq.170), kind=kOutput, calls=%fused_computation.3.clone.1 | convolution fusion | flops 541081600 | bytes 10486784 | tf_op jit(solution)/shard_map/while/body/eval_jaxpr/dot_general | solution.py:25
  151.5 3.1 %select_reduce_fusion.5 = f32[32,8,32]{2,1,0:T(8,128)S(1)} fusion(pred[32,8,128]{2,1,0:T(8,128)(4,1)S(1)} %iota_compare_fusion.18, bf16[32,8,128,128]{3,1,2,0:T(8,128)(2,1)S(1)} %fusion.51, bf16[32,32,128,1]{2,1,0,3:T(8,128)(2,1)S(1)} %bitcast.55), kind=kOutput, calls=%fused_computation.4.clone.1 | convolution fusion | flops 270524416 | bytes 8716288 | tf_op jit(solution)/shard_map/while/body/eval_jaxpr/sid,skjd->skij/dot_general | solution.py:36
  156.2 2.4 %fusion.51 = bf16[32,8,128,128]{3,1,2,0:T(8,128)(2,1)S(1)} fusion(bf16[8,8,128,128]{3,2,1,0:T(8,128)(2,1)S(1)} %bitcast.54, s32[256]{0:T(256)S(1)} %eq.170), kind=kOutput, calls=%fused_computation.3.clone.1 | convolution fusion | flops 541081600 | bytes 10486784 | tf_op jit(solution)/shard_map/while/body/eval_jaxpr/dot_general | solution.py:25
  158.7 3.1 %select_reduce_fusion.5 = f32[32,8,32]{2,1,0:T(8,128)S(1)} fusion(pred[32,8,128]{2,1,0:T(8,128)(4,1)S(1)} %iota_compare_fusion.18, bf16[32,8,128,128]{3,1,2,0:T(8,128)(2,1)S(1)} %fusion.51, bf16[32,32,128,1]{2,1,0,3:T(8,128)(2,1)S(1)} %bitcast.55), kind=kOutput, calls=%fused_computation.4.clone.1 | convolution fusion | flops 270524416 | bytes 8716288 | tf_op jit(solution)/shard_map/while/body/eval_jaxpr/sid,skjd->skij/dot_general | solution.py:36
  163.3 2.4 %fusion.51 = bf16[32,8,128,128]{3,1,2,0:T(8,128)(2,1)S(1)} fusion(bf16[8,8,128,128]{3,2,1,0:T(8,128)(2,1)S(1)} %bitcast.54, s32[256]{0:T(256)S(1)} %eq.170), kind=kOutput, calls=%fused_computation.3.clone.1 | convolution fusion | flops 541081600 | bytes 10486784 | tf_op jit(solution)/shard_map/while/body/eval_jaxpr/dot_general | solution.py:25
  165.8 3.1 %select_reduce_fusion.5 = f32[32,8,32]{2,1,0:T(8,128)S(1)} fusion(pred[32,8,128]{2,1,0:T(8,128)(4,1)S(1)} %iota_compare_fusion.18, bf16[32,8,128,128]{3,1,2,0:T(8,128)(2,1)S(1)} %fusion.51, bf16[32,32,128,1]{2,1,0,3:T(8,128)(2,1)S(1)} %bitcast.55), kind=kOutput, calls=%fused_computation.4.clone.1 | convolution fusion | flops 270524416 | bytes 8716288 | tf_op jit(solution)/shard_map/while/body/eval_jaxpr/sid,skjd->skij/dot_general | solution.py:36
  169.1 12.7 %all_to_all.15 = f32[32,8,8]{1,2,0:T(8,128)S(1)} all-to-all(f32[32,8,8]{1,2,0:T(8,128)S(1)} %copy.63), channel_id=1, replica_groups=mesh['corpus'=32,'qbatch'=8] {'corpus'}, dimensions={0} | all-to-all | bytes 16384 | tf_op jit(solution)/shard_map/all_to_all | solution.py:111
  183.4 33.2 %reduce-scatter.2.cloned.1.call-done = f32[16,64]{1,0:T(8,128)} async-done(((f32[128,64]{1,0:T(8,128)}), f32[16,64]{1,0:T(8,128)}) %reduce-scatter.2.cloned.1.call-update) | async-done | bytes 4112 | tf_op jit(solution)/shard_map/reduce_scatter | solution.py:121
  (103 shorter events, 13.9 us)
Async XLA Ops:
  6.5 67.8 %all-gather.3.cloned.1.call-start = ((), (), s32[]{:S(2)}) async-start(), calls=%async_computation.4 | async-start | bytes 1179648 | tf_op jit(solution)/shard_map/all_gather | solution.py:69
  64.9 47.2 %copy-start = (bf16[64,128,128]{2,1,0:T(8,128)(2,1)S(1)}, bf16[64,128,128]{2,1,0:T(8,128)(2,1)}, u32[]{:S(2)}) copy-start(bf16[64,128,128]{2,1,0:T(8,128)(2,1)} %param.10) | copy-start | bytes 6291460
  64.9 47.2 %copy-start.1 = (s32[64]{0:T(128)S(1)}, s32[64]{0:T(128)}, u32[]{:S(2)}) copy-start(s32[64]{0:T(128)} %param.11) | copy-start | bytes 772
  65.6 14.6 %all-to-all-start = ((s32[32,8,8]{1,2,0:T(8,128)}), s32[32,8,8]{1,2,0:T(8,128)S(1)}, u32[]{:S(2)}, u32[]{:S(2)}) async-start(s32[32,8,8]{1,2,0:T(8,128)} %copy.57), calls=%async_computation | async-start | bytes 262144 | tf_op jit(solution)/shard_map/all_to_all | solution.py:102
  80.3 31.8 %all-to-all-start.1 = ((bf16[32,8,4096]{2,1,0:T(8,128)(2,1)}), bf16[32,8,4096]{2,1,0:T(8,128)(2,1)}, u32[]{:S(2)}, u32[]{:S(2)}) async-start(bf16[32,8,4096]{2,1,0:T(8,128)(2,1)} %fusion.10), calls=%async_computation.1 | async-start | bytes 4194304 | tf_op jit(solution)/shard_map/all_to_all | solution.py:101
  86.1 130.5 %reduce-scatter.2.cloned.1.call-start = ((), (), s32[]{:S(2)}) async-start(), calls=%async_computation.5 | async-start | bytes 73728 | tf_op jit(solution)/shard_map/reduce_scatter | solution.py:121
Sparse Core Ops, SparseCore 0:
  9.1 41.9 all-gather.2
  183.5 33.0 reduce-scatter.1
where the time goes:
time: 224 us; the launch traced here: 223 us
  blocking collectives  66.4 us (30%)
  waiting for transfers between devices  62.5 us (28%)
  matrix products  49.8 us (22%)
  starting transfers between devices  13.9 us (6%)
  between operations  13.6 us (6%)
  local copies, waits for them, and re-layouts  13.5 us (6%)
  other arithmetic  3.29 us (1%)
    reduce_scatter x1, waiting for transfers between devices, shards(): lax.psum_scatter(group_scores, 'qbatch', scatter_dimension=0, tiled=True)  33.2 us
    all_gather x1, blocking collectives, shards(): lax.all_gather(visit_owner, 'qbatch', axis=0, tiled=True)  28.2 us
    all_to_all x1, waiting for transfers between devices, shards(): lax.all_to_all(send_tokens, 'corpus', split_axis=0, concat_axis=0, tiled=...  25.8 us
    all_gather x1, blocking collectives, shards(): lax.all_gather(visit_passages, 'qbatch', axis=0, tiled=True)  25.5 us
    dot_general x8, matrix products, score_group(): jnp.einsum('sid,skjd->skij', queries, passages, preferred_element_type=jn...  24.5 us
    dot_general x8, matrix products, score_group(): jnp.dot(picks.astype(jnp.bfloat16), passage_tokens.reshape(local_passages...  19.5 us
    all_to_all x1, blocking collectives, shards(): lax.all_to_all(scored.reshape(corpus_count, item_count, per_visit), 'corp...  12.7 us
    while x16, local copies, waits for them, and re-layouts  8.15 us
  transfers between devices with their start and end apart: 4, of which 3 were waited for; matrix products, arithmetic and copies ran while one was open for 4% of the time, Pallas kernels for 0%

commit v1 on v0

v1 whole, which is shorter than its diff:
```python
import jax
import jax.numpy as jnp
from jax import lax
from jax.experimental import pallas as pl
from jax.experimental.pallas import tpu as pltpu
from jax.sharding import PartitionSpec as P

f32, bf16, i32 = jnp.float32, jnp.bfloat16, jnp.int32
TOK = 32
FEAT = 128
PLEN = 128
LOCAL = 64
VIS = 8
QDEV = 16
ROWS = 8
COLS = 32
GROUP = QDEV * ROWS
SLOTS = COLS * VIS
BLOCK = QDEV * TOK + QDEV
CELL = VIS * TOK + QDEV
TILE = 8
UNROLL = 8
PLANES = SLOTS // TILE + UNROLL
VMEM_LIMIT = 48 * 1024 * 1024


def iota(shape, dim):
    return lax.broadcasted_iota(i32, shape, dim)


def dot_t(a, b, precision=None):
    return lax.dot_general(
        a, b, (((1,), (1,)), ((), ())), precision=precision, preferred_element_type=f32
    )


def dot_n(a, b, precision=None):
    return lax.dot_general(
        a, b, (((1,), (0,)), ((), ())), precision=precision, preferred_element_type=f32
    )


def fill_kernel(length_ref, tokens_ref, out_ref):
    token = iota((PLEN, FEAT), 0)

    def one(p, _):
        tokens = tokens_ref[p].astype(f32)
        out_ref[p] = jnp.where(token < length_ref[p], tokens, tokens[0:1, :]).astype(bf16)
        return 0

    lax.fori_loop(0, LOCAL, one, 0)


def build_kernel(row_ref, *refs):
    blocks = refs[:ROWS]
    send_ref, back_ref, buf, idx_v, idx_s, sems, idx_sem = refs[ROWS:]
    row = row_ref[0]
    copies = []
    for s, (block, step) in enumerate(zip(blocks, STEPS)):
        copy = pltpu.make_async_copy(block, buf.at[lax.rem(row + step, ROWS)], sems.at[s])
        copy.start()
        copies.append(copy)
    for copy in copies:
        copy.wait()
    lists = jnp.concatenate([buf[z, QDEV * TOK : BLOCK, :] for z in range(ROWS)], 0)
    eye = (iota((GROUP, FEAT), 0) == iota((GROUP, FEAT), 1)).astype(bf16)
    owners = dot_t(eye[0:QDEV], lists)
    wanted = (iota((COLS, GROUP), 0) * ROWS + (row + 1)).astype(f32)
    hit = jnp.zeros((COLS, GROUP), f32)
    for v in range(VIS):
        hit = jnp.where(owners[v : v + 1, :] == wanted, 1.0, hit)
    before = (iota((GROUP, GROUP), 0) < iota((GROUP, GROUP), 1)).astype(bf16)
    rank = dot_n(hit.astype(bf16), before)
    rank = jnp.where(hit > 0.5, rank, -1.0)
    place = iota((COLS, QDEV, GROUP), 1).astype(f32)
    pick = jnp.where(rank[:, None, :] == place, 1.0, 0.0)
    chosen = pick.reshape(COLS * QDEV, GROUP).astype(bf16)
    number = iota((QDEV, GROUP), 1).astype(bf16)
    idx_v[...] = dot_t(number, chosen)[0:8, :].astype(i32)
    to_scalar = pltpu.make_async_copy(idx_v, idx_s, idx_sem)
    to_scalar.start()
    send_ref[:, VIS * TOK : CELL, :] = (
        dot_n(chosen, lists).astype(bf16).reshape(COLS, QDEV, FEAT)
    )
    slots = pick[:, 0:VIS, :].reshape(SLOTS, GROUP).astype(bf16)
    back_ref[...] = dot_t(eye, slots)
    to_scalar.wait()

    def one(c, _):
        for s in range(VIS):
            q = idx_s[0, c * QDEV + s]
            start = pl.multiple_of((q & (QDEV - 1)) * TOK, TOK)
            send_ref[c, s * TOK : (s + 1) * TOK, :] = buf[q >> 4, pl.ds(start, TOK), :]
        return 0

    lax.fori_loop(0, COLS, one, 0)


def score_kernel(me_ref, got_ref, lists_ref, passage_ref, out_ref, plan_v, plan_s, best, plan_sem):
    me = me_ref[0].astype(f32)
    lists = lists_ref[...].astype(f32)[:, 0:VIS, :].reshape(SLOTS, FEAT)
    lane = iota((SLOTS, FEAT), 1)
    visit = jnp.where((lists == me) & (lane < VIS), 1.0, 0.0).astype(bf16)
    low, high = iota((FEAT, FEAT), 0), iota((FEAT, FEAT), 1)
    spread = ((high >= VIS) & (low == (high >> 3) - 1)).astype(bf16)
    mine = dot_n(visit, spread)
    kept = (lists * mine).astype(bf16)
    k16, l16 = iota((16, FEAT), 0), iota((16, FEAT), 1)
    fold = ((l16 >= VIS) & (l16 < VIS + VIS * VIS) & ((l16 & 7) == k16)).astype(bf16)
    cands = dot_t(fold, kept)

    wide = (LOCAL, SLOTS)
    passage = (iota(wide, 0) + 1).astype(f32)
    slot = iota(wide, 1)
    hit = jnp.zeros(wide, f32)
    for k in range(VIS):
        hit = jnp.where(cands[k : k + 1, :] == passage, 1.0, hit)
    before = (iota((SLOTS, SLOTS), 0) < iota((SLOTS, SLOTS), 1)).astype(bf16)
    rank = dot_n(hit.astype(bf16), before).astype(i32)
    count = jnp.sum(hit, axis=1, keepdims=True).astype(i32)
    tiles = (count + (TILE - 1)) >> 3
    tiles_wide = jnp.broadcast_to(tiles, (LOCAL, FEAT)).astype(f32)
    earlier = (iota((LOCAL, LOCAL), 1) < iota((LOCAL, LOCAL), 0)).astype(bf16)
    first = dot_n(earlier, tiles_wide.astype(bf16))[:, 0:1].astype(i32)
    total = jnp.sum(tiles_wide[:, 0:1], axis=0, keepdims=True).astype(i32)
    deepest = jnp.max(tiles_wide[:, 0:1], axis=0, keepdims=True).astype(i32)

    shift = slot - rank
    start = slot * 2 + (slot >> 3)
    x = jnp.where(hit > 0.5, shift * 1024 + start + 1, 0)
    for b in range(8):
        moves = ((x >> (10 + b)) & 1) == 1
        x = jnp.where(moves, 0, x) + pltpu.roll(jnp.where(moves, x, 0), SLOTS - (1 << b), 1)
    plan_v[0:LOCAL, :] = jnp.maximum((x & 1023) - 1, 0)
    for half in range(2):
        t = slot + half * SLOTS
        begun = first <= t
        which = jnp.sum(jnp.where(begun, 1.0, 0.0), axis=0, keepdims=True).astype(i32) - 1
        since = jnp.max(jnp.where(begun, first, 0).astype(f32), axis=0, keepdims=True).astype(i32)
        plan_v[LOCAL + half : LOCAL + half + 1, :] = which * 64 + jnp.minimum(t[0:1, :] - since, 63)
    plan_v[LOCAL + 2 : LOCAL + 3, :] = jnp.broadcast_to(total, (1, SLOTS))
    plan_v[LOCAL + 3 : LOCAL + 4, :] = jnp.broadcast_to(deepest, (1, SLOTS))
    to_scalar = pltpu.make_async_copy(plan_v, plan_s, plan_sem)
    to_scalar.start()
    to_scalar.wait()

    def tile_steps(step, _):
        for u in range(UNROLL):
            t = step * UNROLL + u
            word = plan_s[LOCAL + (step >> 5), t & (SLOTS - 1)]
            p = word >> 6
            j = word & 63
            base = jnp.minimum(j, SLOTS // TILE - 1) * TILE
            queries = jnp.concatenate(
                [
                    got_ref[pl.ds(pl.multiple_of(plan_s[p, base + r] * 16, 16), TOK), :]
                    for r in range(TILE)
                ],
                0,
            )
            similarity = dot_t(passage_ref[p], queries)
            best[j, pl.ds(p, 1), :] = jnp.max(similarity, axis=0, keepdims=True)
        return 0

    steps = (plan_s[LOCAL + 2, 0] + (UNROLL - 1)) >> 3
    lax.fori_loop(0, steps, tile_steps, 0)

    adder = ((iota((SLOTS, FEAT), 0) >> 5) == (iota((SLOTS, FEAT), 1) & 7)).astype(f32)

    def gather_plane(j, acc):
        sums = dot_n(best[j], adder, lax.Precision.HIGHEST)
        both = jnp.concatenate([sums, sums], 1)
        return jnp.where((slot >> 3) == j, both, acc)

    y = lax.fori_loop(0, plan_s[LOCAL + 3, 0], gather_plane, jnp.zeros(wide, f32))
    y = jnp.where(slot < count, y, 0.0)
    x = x >> 10
    for b in (7, 6, 5, 4, 3, 2, 1, 0):
        moves = ((x >> b) & 1) == 1
        y = jnp.where(moves, 0.0, y) + pltpu.roll(jnp.where(moves, y, 0.0), 1 << b, 1)
        x = jnp.where(moves, 0, x) + pltpu.roll(jnp.where(moves, x, 0), 1 << b, 1)
    scores = jnp.concatenate(
        [
            jnp.sum(jnp.where(cands[k : k + 1, :] == passage, y, 0.0), axis=0, keepdims=True)
            for k in range(VIS)
        ],
        0,
    )
    k8, l8 = iota((VIS, FEAT), 0), iota((VIS, FEAT), 1)
    repeat = ((l8 & 7) == k8).astype(f32)
    spread_back = ((high < VIS * VIS) & (low == (high >> 3))).astype(bf16)
    by_slot = lax.dot_general(
        scores,
        repeat,
        (((0,), (0,)), ((), ())),
        precision=lax.Precision.HIGHEST,
        preferred_element_type=f32,
    )
    out_ref[...] = by_slot * dot_n(visit, spread_back)


def return_kernel(back_ref, got_ref, out_ref):
    out_ref[...] = dot_n(back_ref[...], got_ref[...], lax.Precision.HIGHEST)


VM = pl.BlockSpec(memory_space=pltpu.VMEM)
SM = pl.BlockSpec(memory_space=pltpu.SMEM)
ANY = pl.BlockSpec(memory_space=pl.ANY)
PARAMS = pltpu.CompilerParams(vmem_limit_bytes=VMEM_LIMIT)
STEPS = (0, 7, 1, 6, 2, 5, 3, 4)


def fill(lengths, tokens):
    return pl.pallas_call(
        fill_kernel,
        out_shape=jax.ShapeDtypeStruct((LOCAL, PLEN, FEAT), bf16),
        in_specs=[SM, VM],
        out_specs=VM,
        compiler_params=PARAMS,
        cost_estimate=pl.CostEstimate(flops=1 << 22, bytes_accessed=1 << 22, transcendentals=0),
    )(lengths, tokens)


def build(row, blocks):
    return pl.pallas_call(
        build_kernel,
        out_shape=(
            jax.ShapeDtypeStruct((COLS, CELL, FEAT), bf16),
            jax.ShapeDtypeStruct((GROUP, SLOTS), f32),
        ),
        in_specs=[SM] + [ANY] * ROWS,
        out_specs=(VM, VM),
        scratch_shapes=[
            pltpu.VMEM((ROWS, BLOCK, FEAT), bf16),
            pltpu.VMEM((8, COLS * QDEV), i32),
            pltpu.SMEM((8, COLS * QDEV), i32),
            pltpu.SemaphoreType.DMA((ROWS,)),
            pltpu.SemaphoreType.DMA,
        ],
        compiler_params=PARAMS,
    )(row, *blocks)


def score(me, got, passages):
    lists = got[:, VIS * TOK : CELL, :]
    return pl.pallas_call(
        score_kernel,
        out_shape=jax.ShapeDtypeStruct((SLOTS, FEAT), f32),
        in_specs=[SM, VM, VM, VM],
        out_specs=VM,
        scratch_shapes=[
            pltpu.VMEM((LOCAL + 8, SLOTS), i32),
            pltpu.SMEM((LOCAL + 8, SLOTS), i32),
            pltpu.VMEM((PLANES, LOCAL, SLOTS), f32),
            pltpu.SemaphoreType.DMA,
        ],
        compiler_params=PARAMS,
    )(me, got.reshape(COLS * CELL, FEAT), lists, passages)


def hand_back(back, got):
    return pl.pallas_call(
        return_kernel,
        out_shape=jax.ShapeDtypeStruct((GROUP, FEAT), f32),
        in_specs=[VM, VM],
        out_specs=VM,
        compiler_params=PARAMS,
    )(back, got)


def shards(query_tokens, visit_owner, visit_passages, passage_tokens, passage_lengths):
    row = lax.axis_index("qbatch").astype(i32)
    me = lax.axis_index("corpus").astype(i32) * ROWS + row + 1
    lists = jnp.concatenate(
        [
            visit_owner + 1,
            visit_passages.reshape(QDEV, VIS * VIS) + 1,
            jnp.zeros((QDEV, FEAT - VIS - VIS * VIS), i32),
        ],
        1,
    ).astype(bf16)
    own = jnp.concatenate([query_tokens.reshape(QDEV * TOK, FEAT), lists], 0)
    up = [(i, (i + 1) % ROWS) for i in range(ROWS)]
    down = [(i, (i + ROWS - 1) % ROWS) for i in range(ROWS)]
    blocks = [own]
    left = right = own
    for step in range(1, ROWS // 2 + 1):
        left = lax.ppermute(left, "qbatch", up)
        blocks.append(left)
        if step < ROWS // 2:
            right = lax.ppermute(right, "qbatch", down)
            blocks.append(right)
    passages = fill(passage_lengths, passage_tokens)
    send, back = build(row[None], blocks)
    got = lax.all_to_all(send, "corpus", split_axis=0, concat_axis=0, tiled=True)
    scored = score(me[None], got, passages)
    returned = lax.all_to_all(
        scored.reshape(COLS, VIS, FEAT), "corpus", split_axis=0, concat_axis=0, tiled=True
    )
    mine = hand_back(back, returned.reshape(SLOTS, FEAT))
    parts = lax.all_to_all(
        mine.reshape(ROWS, QDEV, FEAT), "qbatch", split_axis=0, concat_axis=0, tiled=True
    )
    return jnp.sum(parts, axis=0)[:, 0 : VIS * VIS]


def solution(mesh):
    placed = (
        P(("corpus", "qbatch"), None, None),
        P(("corpus", "qbatch"), None),
        P(("corpus", "qbatch"), None, None),
        P(("corpus", "qbatch"), None, None),
        P(("corpus", "qbatch")),
    )
    return jax.shard_map(
        shards, mesh=mesh, in_specs=placed, out_specs=P(("corpus", "qbatch"), None), check_vma=False
    )
```

time: 224 us -> 122 us (0.54)
  the two profiles are of different devices: /device:TPU:2 before, /device:TPU:1 now
where the time goes in v1:
time: 122 us; the launch traced here: 121 us
  waiting for transfers between devices  38.6 us (32%)
  blocking collectives  32.3 us (26%)
  starting transfers between devices  23.8 us (20%)
  Pallas kernels  17.7 us (15%)
  local copies, waits for them, and re-layouts  6.69 us (5%)
  other arithmetic  2.37 us (2%)
    all_to_all x1, waiting for transfers between devices, shards(): lax.all_to_all(send, 'corpus', split_axis=0, concat_axis=0, tiled=True)  25.5 us
    all_to_all x1, blocking collectives, shards(): lax.all_to_all(scored.reshape(COLS, VIS, FEAT), 'corpus', split_axis=0, c...  17.7 us
    all_to_all x1, blocking collectives, shards(): lax.all_to_all(mine.reshape(ROWS, QDEV, FEAT), 'qbatch', split_axis=0, co...  14.6 us
    ppermute x4, waiting for transfers between devices, shards(): left = lax.ppermute(left, 'qbatch', up)  13.1 us
    pallas_call x1, Pallas kernels, score(): pl.pallas_call(score_kernel, out_shape=jax.ShapeDtypeStruct((SLOTS, FEAT)...  12.3 us
    all_to_all x1, starting transfers between devices, shards(): lax.all_to_all(send, 'corpus', split_axis=0, concat_axis=0, tiled=True)  11.9 us
    ppermute x3, starting transfers between devices, shards(): right = lax.ppermute(right, 'qbatch', down)  9.38 us
    unnamed x11, local copies, waits for them, and re-layouts  6.6 us
  transfers between devices with their start and end apart: 8, of which 5 were waited for; matrix products, arithmetic and copies ran while one was open for 0% of the time, Pallas kernels for 1%

profile of v1, /device:TPU:1, one launch (start us, length us, event | category | flops | bytes accessed | tf_op | source)
XLA Modules:
  0.0 121.5 jit_solution(8968626766102572241)
XLA Ops:
  0.0 0.8 copy.10
  0.8 0.8 fusion
  1.5 0.1 copy.12
  1.6 1.0 maximum_maximum_fusion.refs_0_
  2.6 2.5 %collective-permute-start = (bf16[528,128]{1,0:T(8,128)(2,1)S(1)}, bf16[528,128]{1,0:T(8,128)(2,1)S(1)}, u32[]{:S(2)}, u32[]{:S(2)}) collective-permute-start(bf16[528,128]{1,0:T(8,128)(2,1)S(1)} %maximum_maximum_fusion.refs_0_), channel_id=1, source_target_pairs={{0,1},{1,2},{2,3},{3,4},{4,5},{5,6},{6,7},{7,0},{8,9},{9,10},{10,1... | collective-permute-start | bytes 405512 | tf_op jit(solution)/shard_map/ppermute | solution.py:288
  5.1 4.0 %collective-permute-start.1 = (bf16[528,128]{1,0:T(8,128)(2,1)S(1)}, bf16[528,128]{1,0:T(8,128)(2,1)S(1)}, u32[]{:S(2)}, u32[]{:S(2)}) collective-permute-start(bf16[528,128]{1,0:T(8,128)(2,1)S(1)} %maximum_maximum_fusion.refs_0_), channel_id=1, source_target_pairs={{0,7},{1,0},{2,1},{3,2},{4,3},{5,4},{6,5},{7,6},{8,15},{9,8},{10,9... | collective-permute-start | bytes 405512 | tf_op jit(solution)/shard_map/ppermute | solution.py:291
  9.1 3.2 %collective-permute-done.refs_1_ = bf16[528,128]{1,0:T(8,128)(2,1)S(1)} collective-permute-done((bf16[528,128]{1,0:T(8,128)(2,1)S(1)}, bf16[528,128]{1,0:T(8,128)(2,1)S(1)}, u32[]{:S(2)}, u32[]{:S(2)}) %collective-permute-start) | collective-permute-done | bytes 135200 | tf_op jit(solution)/shard_map/ppermute | solution.py:288
  12.3 0.0 collective-permute-start.2
  12.3 0.0 collective-permute-done.1.refs_2_
  12.3 2.7 %collective-permute-start.3 = (bf16[528,128]{1,0:T(8,128)(2,1)S(1)}, bf16[528,128]{1,0:T(8,128)(2,1)S(1)}, u32[]{:S(2)}, u32[]{:S(2)}) collective-permute-start(bf16[528,128]{1,0:T(8,128)(2,1)S(1)} %collective-permute-done.1.refs_2_), channel_id=1, source_target_pairs={{0,7},{1,0},{2,1},{3,2},{4,3},{5,4},{6,5},{7,6},{8,15},{9,8},{10,9... | collective-permute-start | bytes 405512 | tf_op jit(solution)/shard_map/ppermute | solution.py:291
  15.0 2.4 %collective-permute-done.2.refs_3_ = bf16[528,128]{1,0:T(8,128)(2,1)S(1)} collective-permute-done((bf16[528,128]{1,0:T(8,128)(2,1)S(1)}, bf16[528,128]{1,0:T(8,128)(2,1)S(1)}, u32[]{:S(2)}, u32[]{:S(2)}) %collective-permute-start.2) | collective-permute-done | bytes 135200 | tf_op jit(solution)/shard_map/ppermute | solution.py:288
  17.4 0.0 collective-permute-start.4
  17.4 0.0 collective-permute-done.3.refs_4_
  17.4 2.7 %collective-permute-start.5 = (bf16[528,128]{1,0:T(8,128)(2,1)S(1)}, bf16[528,128]{1,0:T(8,128)(2,1)S(1)}, u32[]{:S(2)}, u32[]{:S(2)}) collective-permute-start(bf16[528,128]{1,0:T(8,128)(2,1)S(1)} %collective-permute-done.3.refs_4_), channel_id=1, source_target_pairs={{0,7},{1,0},{2,1},{3,2},{4,3},{5,4},{6,5},{7,6},{8,15},{9,8},{10,9... | collective-permute-start | bytes 405512 | tf_op jit(solution)/shard_map/ppermute | solution.py:291
  20.1 2.4 %collective-permute-done.4.refs_5_ = bf16[528,128]{1,0:T(8,128)(2,1)S(1)} collective-permute-done((bf16[528,128]{1,0:T(8,128)(2,1)S(1)}, bf16[528,128]{1,0:T(8,128)(2,1)S(1)}, u32[]{:S(2)}, u32[]{:S(2)}) %collective-permute-start.4) | collective-permute-done | bytes 135200 | tf_op jit(solution)/shard_map/ppermute | solution.py:288
  22.5 0.0 collective-permute-start.6
  22.5 0.0 collective-permute-done.5.refs_6_
  22.5 5.1 %collective-permute-done.6.refs_7_ = bf16[528,128]{1,0:T(8,128)(2,1)S(1)} collective-permute-done((bf16[528,128]{1,0:T(8,128)(2,1)S(1)}, bf16[528,128]{1,0:T(8,128)(2,1)S(1)}, u32[]{:S(2)}, u32[]{:S(2)}) %collective-permute-start.6) | collective-permute-done | bytes 135200 | tf_op jit(solution)/shard_map/ppermute | solution.py:288
  27.6 3.8 %shard_map.55 = (bf16[32,272,128]{2,1,0:T(8,128)(2,1)S(1)}, f32[128,256]{1,0:T(8,128)S(1)}) custom-call(s32[1]{0:T(128)} %bitcast.row_ref, bf16[528,128]{1,0:T(8,128)(2,1)S(1)} %maximum_maximum_fusion.refs_0_, bf16[528,128]{1,0:T(8,128)(2,1)S(1)} %collective-permute-done.refs_1_, bf16[528,128]{1,0:T(8,128)(2,1)S(1)} %collective-permute-done.1.refs_2_, ...), custom_call_target="tpu_custom_call" | custom-call | tf_op jit(solution)/shard_map/pallas_call | solution.py:225
  31.4 1.4 %copy-done.2 = bf16[32,272,128]{2,1,0:T(8,128)(2,1)} copy-done((bf16[32,272,128]{2,1,0:T(8,128)(2,1)}, bf16[32,272,128]{2,1,0:T(8,128)(2,1)S(1)}, u32[]{:S(2)}) %copy-start.2) | copy-done | bytes 2228248
  32.8 11.9 %all-to-all-start = ((bf16[32,272,128]{2,1,0:T(8,128)(2,1)}), bf16[32,272,128]{2,1,0:T(8,128)(2,1)S(1)}, u32[]{:S(2)}, u32[]{:S(2)}) async-start(bf16[32,272,128]{2,1,0:T(8,128)(2,1)} %copy-done.2), calls=%async_computation | async-start | bytes 4456448 | tf_op jit(solution)/shard_map/all_to_all | solution.py:295
  44.7 0.0 copy-start.3
  44.7 1.6 %copy-done.3 = bf16[64,128,128]{2,1,0:T(8,128)(2,1)S(1)} copy-done((bf16[64,128,128]{2,1,0:T(8,128)(2,1)S(1)}, bf16[64,128,128]{2,1,0:T(8,128)(2,1)}, u32[]{:S(2)}) %copy-start.3) | copy-done | bytes 2097176
  46.3 1.2 %shard_map.56.passage_ref = bf16[64,128,128]{2,1,0:T(8,128)(2,1)S(1)} custom-call(s32[64]{0:T(128)S(1)} %copy-done.4, bf16[64,128,128]{2,1,0:T(8,128)(2,1)S(1)} %copy-done.3), custom_call_target="tpu_custom_call" | custom-call | flops 4194304 | bytes 4194304 | tf_op jit(solution)/shard_map/pallas_call | solution.py:214
  47.6 1.3 %copy-done = bf16[64,128,128]{2,1,0:T(8,128)(2,1)} copy-done((bf16[64,128,128]{2,1,0:T(8,128)(2,1)}, bf16[64,128,128]{2,1,0:T(8,128)(2,1)S(1)}, u32[]{:S(2)}) %copy-start) | copy-done | bytes 2097176
  48.9 25.5 %all-to-all-done = bf16[32,272,128]{2,1,0:T(8,128)(2,1)S(1)} async-done(((bf16[32,272,128]{2,1,0:T(8,128)(2,1)}), bf16[32,272,128]{2,1,0:T(8,128)(2,1)S(1)}, u32[]{:S(2)}, u32[]{:S(2)}) %all-to-all-start) | async-done | bytes 2228256 | tf_op jit(solution)/shard_map/all_to_all | solution.py:295
  74.4 1.6 %copy-done.1 = bf16[64,128,128]{2,1,0:T(8,128)(2,1)S(1)} copy-done((bf16[64,128,128]{2,1,0:T(8,128)(2,1)S(1)}, bf16[64,128,128]{2,1,0:T(8,128)(2,1)}, u32[]{:S(2)}) %copy-start.1) | copy-done | bytes 2097176
  76.0 12.3 %shard_map.57 = f32[256,128]{1,0:T(8,128)S(1)} custom-call(s32[1]{0:T(128)} %bitcast.3.me_ref, bf16[8704,128]{1,0:T(8,128)(2,1)S(1)} %bitcast.10, bf16[32,16,128]{2,1,0:T(8,128)(2,1)S(1)} %slice.8.lists_ref, bf16[64,128,128]{2,1,0:T(8,128)(2,1)S(1)} %copy-done.1), custom_call_target="tpu_custom_call" | custom-call | tf_op jit(solution)/shard_map/pallas_call | solution.py:246
  88.3 17.7 %all_to_all.15 = f32[32,8,128]{2,1,0:T(8,128)S(1)} all-to-all(f32[32,8,128]{2,1,0:T(8,128)S(1)} %bitcast.11), channel_id=1, replica_groups=mesh['corpus'=32,'qbatch'=8] {'corpus'}, dimensions={0} | all-to-all | bytes 262144 | tf_op jit(solution)/shard_map/all_to_all | solution.py:297
  106.0 0.3 shard_map.58
  106.2 14.6 %all_to_all.16 = f32[8,16,128]{2,1,0:T(8,128)S(1)} all-to-all(f32[8,16,128]{2,1,0:T(8,128)S(1)} %bitcast.13), channel_id=1, replica_groups=mesh['corpus'=32,'qbatch'=8] {'qbatch'}, dimensions={0} | all-to-all | bytes 131072 | tf_op jit(solution)/shard_map/all_to_all | solution.py:301
  120.9 0.6 reduce_sum.9
  (8 shorter events, 0.0 us)
Async XLA Ops:
  2.6 9.7 %collective-permute-start = (bf16[528,128]{1,0:T(8,128)(2,1)S(1)}, bf16[528,128]{1,0:T(8,128)(2,1)S(1)}, u32[]{:S(2)}, u32[]{:S(2)}) collective-permute-start(bf16[528,128]{1,0:T(8,128)(2,1)S(1)} %maximum_maximum_fusion.refs_0_), channel_id=1, source_target_pairs={{0,1},{1,2},{2,3},{3,4},{4,5},{5,6},{6,7},{7,0},{8,9},{9,10},{10,1... | collective-permute-start | bytes 405512 | tf_op jit(solution)/shard_map/ppermute | solution.py:288
  5.1 7.3 %collective-permute-start.1 = (bf16[528,128]{1,0:T(8,128)(2,1)S(1)}, bf16[528,128]{1,0:T(8,128)(2,1)S(1)}, u32[]{:S(2)}, u32[]{:S(2)}) collective-permute-start(bf16[528,128]{1,0:T(8,128)(2,1)S(1)} %maximum_maximum_fusion.refs_0_), channel_id=1, source_target_pairs={{0,7},{1,0},{2,1},{3,2},{4,3},{5,4},{6,5},{7,6},{8,15},{9,8},{10,9... | collective-permute-start | bytes 405512 | tf_op jit(solution)/shard_map/ppermute | solution.py:291
  12.3 5.1 %collective-permute-start.2 = (bf16[528,128]{1,0:T(8,128)(2,1)S(1)}, bf16[528,128]{1,0:T(8,128)(2,1)S(1)}, u32[]{:S(2)}, u32[]{:S(2)}) collective-permute-start(bf16[528,128]{1,0:T(8,128)(2,1)S(1)} %collective-permute-done.refs_1_), channel_id=1, source_target_pairs={{0,1},{1,2},{2,3},{3,4},{4,5},{5,6},{6,7},{7,0},{8,9},{9,10},{10,1... | collective-permute-start | bytes 405512 | tf_op jit(solution)/shard_map/ppermute | solution.py:288
  12.3 5.1 %collective-permute-start.3 = (bf16[528,128]{1,0:T(8,128)(2,1)S(1)}, bf16[528,128]{1,0:T(8,128)(2,1)S(1)}, u32[]{:S(2)}, u32[]{:S(2)}) collective-permute-start(bf16[528,128]{1,0:T(8,128)(2,1)S(1)} %collective-permute-done.1.refs_2_), channel_id=1, source_target_pairs={{0,7},{1,0},{2,1},{3,2},{4,3},{5,4},{6,5},{7,6},{8,15},{9,8},{10,9... | collective-permute-start | bytes 405512 | tf_op jit(solution)/shard_map/ppermute | solution.py:291
  17.4 5.1 %collective-permute-start.4 = (bf16[528,128]{1,0:T(8,128)(2,1)S(1)}, bf16[528,128]{1,0:T(8,128)(2,1)S(1)}, u32[]{:S(2)}, u32[]{:S(2)}) collective-permute-start(bf16[528,128]{1,0:T(8,128)(2,1)S(1)} %collective-permute-done.2.refs_3_), channel_id=1, source_target_pairs={{0,1},{1,2},{2,3},{3,4},{4,5},{5,6},{6,7},{7,0},{8,9},{9,10},{10,1... | collective-permute-start | bytes 405512 | tf_op jit(solution)/shard_map/ppermute | solution.py:288
  17.4 5.1 %collective-permute-start.5 = (bf16[528,128]{1,0:T(8,128)(2,1)S(1)}, bf16[528,128]{1,0:T(8,128)(2,1)S(1)}, u32[]{:S(2)}, u32[]{:S(2)}) collective-permute-start(bf16[528,128]{1,0:T(8,128)(2,1)S(1)} %collective-permute-done.3.refs_4_), channel_id=1, source_target_pairs={{0,7},{1,0},{2,1},{3,2},{4,3},{5,4},{6,5},{7,6},{8,15},{9,8},{10,9... | collective-permute-start | bytes 405512 | tf_op jit(solution)/shard_map/ppermute | solution.py:291
  22.5 5.1 %collective-permute-start.6 = (bf16[528,128]{1,0:T(8,128)(2,1)S(1)}, bf16[528,128]{1,0:T(8,128)(2,1)S(1)}, u32[]{:S(2)}, u32[]{:S(2)}) collective-permute-start(bf16[528,128]{1,0:T(8,128)(2,1)S(1)} %collective-permute-done.4.refs_5_), channel_id=1, source_target_pairs={{0,1},{1,2},{2,3},{3,4},{4,5},{5,6},{6,7},{7,0},{8,9},{9,10},{10,1... | collective-permute-start | bytes 405512 | tf_op jit(solution)/shard_map/ppermute | solution.py:288
  31.4 1.4 %copy-start.2 = (bf16[32,272,128]{2,1,0:T(8,128)(2,1)}, bf16[32,272,128]{2,1,0:T(8,128)(2,1)S(1)}, u32[]{:S(2)}) copy-start(bf16[32,272,128]{2,1,0:T(8,128)(2,1)S(1)} %get-tuple-element.8) | copy-start | bytes 6684676
  32.8 11.9 %copy-start.4 = (s32[64]{0:T(128)S(1)}, s32[64]{0:T(128)}, u32[]{:S(2)}) copy-start(s32[64]{0:T(128)} %length_ref.1) | copy-start | bytes 772
  32.8 41.6 %all-to-all-start = ((bf16[32,272,128]{2,1,0:T(8,128)(2,1)}), bf16[32,272,128]{2,1,0:T(8,128)(2,1)S(1)}, u32[]{:S(2)}, u32[]{:S(2)}) async-start(bf16[32,272,128]{2,1,0:T(8,128)(2,1)} %copy-done.2), calls=%async_computation | async-start | bytes 4456448 | tf_op jit(solution)/shard_map/all_to_all | solution.py:295
  44.7 1.6 %copy-start.3 = (bf16[64,128,128]{2,1,0:T(8,128)(2,1)S(1)}, bf16[64,128,128]{2,1,0:T(8,128)(2,1)}, u32[]{:S(2)}) copy-start(bf16[64,128,128]{2,1,0:T(8,128)(2,1)} %tokens_ref.1) | copy-start | bytes 6291460
  47.5 1.3 %copy-start = (bf16[64,128,128]{2,1,0:T(8,128)(2,1)}, bf16[64,128,128]{2,1,0:T(8,128)(2,1)S(1)}, u32[]{:S(2)}) copy-start(bf16[64,128,128]{2,1,0:T(8,128)(2,1)S(1)} %shard_map.56.passage_ref) | copy-start | bytes 6291460
  74.4 1.6 %copy-start.1 = (bf16[64,128,128]{2,1,0:T(8,128)(2,1)S(1)}, bf16[64,128,128]{2,1,0:T(8,128)(2,1)}, u32[]{:S(2)}) copy-start(bf16[64,128,128]{2,1,0:T(8,128)(2,1)} %copy-done) | copy-start | bytes 6291460

commit v2 on v1

v2 whole, which is shorter than its diff:
```python
import jax
import jax.numpy as jnp
from jax import lax
from jax.experimental import pallas as pl
from jax.experimental.pallas import tpu as pltpu
from jax.sharding import PartitionSpec as P

f32, bf16, i32 = jnp.float32, jnp.bfloat16, jnp.int32
TOK = 32
FEAT = 128
PLEN = 128
LOCAL = 64
VIS = 8
QDEV = 16
ROWS = 8
COLS = 32
GROUP = QDEV * ROWS
SLOTS = COLS * VIS
PIECES = TOK + 1
CELL = VIS * 2 + 1
TILE = 8
TILES = 384
UNROLL = 16
PARTS = ((0, 8), (8, 16), (16, 24), (24, 30), (30, 32))
VMEM_LIMIT = 16 * 1024 * 1024


def iota(shape, dim):
    return lax.broadcasted_iota(i32, shape, dim)


def dot_t(a, b, precision=None):
    return lax.dot_general(
        a, b, (((1,), (1,)), ((), ())), precision=precision, preferred_element_type=f32
    )


def dot_n(a, b, precision=None):
    return lax.dot_general(
        a, b, (((1,), (0,)), ((), ())), precision=precision, preferred_element_type=f32
    )


def dot_tn(a, b, precision=None):
    return lax.dot_general(
        a, b, (((0,), (0,)), ((), ())), precision=precision, preferred_element_type=f32
    )


def fill_kernel(length_ref, tokens_ref, out_ref, filled, sem):
    token = iota((PLEN, FEAT), 0)

    def one(p, _):
        tokens = tokens_ref[p].astype(f32)
        filled[p] = jnp.where(token < length_ref[p], tokens, tokens[0:1, :]).astype(bf16)
        return 0

    lax.fori_loop(0, LOCAL, one, 0)
    copy = pltpu.make_async_copy(filled, out_ref, sem)
    copy.start()
    copy.wait()


def pack_kernel(tokens_ref, owner_ref, cand_ref, out_ref, owners, cands, sems):
    loads = [
        pltpu.make_async_copy(owner_ref, owners, sems.at[0]),
        pltpu.make_async_copy(cand_ref, cands, sems.at[1]),
        pltpu.make_async_copy(tokens_ref, out_ref.at[pl.ds(0, TOK)], sems.at[2]),
    ]
    for load in loads:
        load.start()
    loads[0].wait()
    loads[1].wait()
    rest = jnp.zeros((FEAT - VIS - VIS * VIS, QDEV), i32)
    lists = jnp.concatenate([owners[...] + 1, cands[...] + 1, rest], 0).astype(bf16)
    eye = (iota((FEAT, FEAT), 0) == iota((FEAT, FEAT), 1)).astype(bf16)
    out_ref[TOK] = dot_tn(lists, eye).astype(bf16)
    loads[2].wait()


def build_kernel(row_ref, *refs):
    blocks = refs[:ROWS]
    send_ref, back_ref, buf, out_v, idx_v, idx_s, sems, idx_sem, out_sems = refs[ROWS:]
    row = row_ref[0]
    copies = []
    for s, (block, step) in enumerate(zip(blocks, STEPS)):
        at = buf.at[pl.ds(lax.rem(row + step, ROWS) * PIECES, PIECES)]
        copy = pltpu.make_async_copy(block, at, sems.at[s])
        copy.start()
        copies.append(copy)
    for copy in copies:
        copy.wait()
    lists = jnp.concatenate([buf[z * PIECES + TOK] for z in range(ROWS)], 0)
    eye = (iota((GROUP, FEAT), 0) == iota((GROUP, FEAT), 1)).astype(bf16)
    owners = dot_t(eye[0:QDEV], lists)
    wanted = (iota((COLS, GROUP), 0) * ROWS + (row + 1)).astype(f32)
    hit = jnp.zeros((COLS, GROUP), f32)
    for v in range(VIS):
        hit = jnp.where(owners[v : v + 1, :] == wanted, 1.0, hit)
    before = (iota((GROUP, GROUP), 0) < iota((GROUP, GROUP), 1)).astype(bf16)
    rank = dot_n(hit.astype(bf16), before)
    rank = jnp.where(hit > 0.5, rank, -1.0)
    place = iota((COLS, QDEV, GROUP), 1).astype(f32)
    pick = jnp.where(rank[:, None, :] == place, 1.0, 0.0)
    chosen = pick.reshape(COLS * QDEV, GROUP).astype(bf16)
    number = iota((QDEV, GROUP), 1).astype(bf16)
    query = dot_t(number, chosen)[0:8, :].astype(i32)
    idx_v[...] = (query >> 4) * PIECES + (query & (QDEV - 1)) * 2
    to_scalar = pltpu.make_async_copy(idx_v, idx_s, idx_sem)
    to_scalar.start()
    out_v[:, VIS * 2] = dot_n(chosen, lists).astype(bf16).reshape(COLS, QDEV, FEAT)
    slots = pick[:, 0:VIS, :].reshape(SLOTS, GROUP).astype(bf16)
    back_ref[...] = dot_t(eye, slots)
    to_scalar.wait()

    def one(c, _):
        for s in range(VIS):
            out_v[c, 2 * s : 2 * s + 2] = buf[pl.ds(idx_s[0, c * QDEV + s], 2)]
        return 0

    outs = []
    for start, stop in PARTS:
        lax.fori_loop(start, stop, one, 0)
        some = pl.ds(start, stop - start)
        copy = pltpu.make_async_copy(out_v.at[some], send_ref.at[some], out_sems.at[len(outs)])
        copy.start()
        outs.append(copy)
    for copy in outs:
        copy.wait()


def split3(x):
    high = x.astype(bf16)
    x = x - high.astype(f32)
    mid = x.astype(bf16)
    return high, mid, (x - mid.astype(f32)).astype(bf16)


def score_kernel(
    me_ref, got, cells_ref, passage_ref, out_ref, held, plan_v, plan_s, best, sems
):
    load = pltpu.make_async_copy(passage_ref, held, sems.at[0])
    load.start()
    me = me_ref[0].astype(f32)
    lists = cells_ref[:, VIS * 2].astype(f32)[:, 0:VIS, :].reshape(SLOTS, FEAT)
    lane = iota((SLOTS, FEAT), 1)
    visit = jnp.where((lists == me) & (lane < VIS), 1.0, 0.0).astype(bf16)
    low, high = iota((FEAT, FEAT), 0), iota((FEAT, FEAT), 1)
    spread = ((high >= VIS) & (low == (high >> 3) - 1)).astype(bf16)
    mine = dot_n(visit, spread)
    kept = (lists * mine).astype(bf16)
    k16, l16 = iota((16, FEAT), 0), iota((16, FEAT), 1)
    fold = ((l16 >= VIS) & (l16 < VIS + VIS * VIS) & ((l16 & 7) == k16)).astype(bf16)
    cands = dot_t(fold, kept)

    wide = (LOCAL, SLOTS)
    passage = (iota(wide, 0) + 1).astype(f32)
    slot = iota(wide, 1)
    hit = jnp.zeros(wide, f32)
    for k in range(VIS):
        hit = jnp.where(cands[k : k + 1, :] == passage, 1.0, hit)
    hits = hit.astype(bf16)
    before = (iota((SLOTS, SLOTS), 0) < iota((SLOTS, SLOTS), 1)).astype(bf16)
    rank = dot_n(hits, before).astype(i32)
    count = jnp.sum(hit, axis=1, keepdims=True).astype(i32)
    tiles = (count + (TILE - 1)) >> 3
    tiles_wide = jnp.broadcast_to(tiles, (LOCAL, FEAT)).astype(bf16)
    earlier = (iota((LOCAL, LOCAL), 1) < iota((LOCAL, LOCAL), 0)).astype(bf16)
    first_wide = dot_n(earlier, tiles_wide).astype(i32)
    padded = jnp.concatenate([hits, jnp.zeros(wide, bf16)], 0)
    tiles_row = (dot_t(jnp.ones((16, SLOTS), bf16), padded).astype(i32) + (TILE - 1)) >> 3
    first_row = dot_n(tiles_row.astype(bf16), (low < high).astype(bf16)).astype(i32)
    total = first_row[0:1, FEAT - 1 : FEAT]

    shift = slot - rank
    x = jnp.where(hit > 0.5, shift * 512 + slot + 1, 0)
    for b in range(8):
        moves = ((x >> (9 + b)) & 1) == 1
        x = jnp.where(moves, 0, x) + pltpu.roll(jnp.where(moves, x, 0), SLOTS - (1 << b), 1)
    packed = jnp.maximum((x & 511) - 1, 0).astype(f32).astype(bf16)

    t = iota((TILES, FEAT), 0)
    own = (first_row[0:1] <= t) & (t < first_row[0:1] + tiles_row[0:1])
    own = jnp.where(own, 1.0, 0.0).astype(bf16)
    table = jnp.concatenate(
        [packed, (first_wide >> 4).astype(bf16), (first_wide & 15).astype(bf16)], 1
    )
    rows = dot_n(own[:, 0:LOCAL], table)
    begun = rows[:, SLOTS : SLOTS + FEAT].astype(i32) * 16
    depth = t - begun - rows[:, SLOTS + FEAT :].astype(i32)
    depth = jnp.concatenate([depth, depth], 1)
    here = ((iota((TILES, SLOTS), 1) >> 3) == depth) & (iota((TILES, SLOTS), 0) < total)
    chosen = jnp.where(here, rows[:, 0:SLOTS], 0.0).astype(bf16)
    k16, l16 = iota((16, SLOTS + FEAT), 0), iota((16, SLOTS + FEAT), 1)
    fold = jnp.where((l16 < SLOTS) & ((l16 & 7) == k16), 1.0, 0.0)
    fold = jnp.where((l16 >= SLOTS) & (k16 == TILE), (l16 - SLOTS).astype(f32), fold)
    plan = dot_t(fold.astype(bf16), jnp.concatenate([chosen, own], 1)).astype(i32)
    plan_v[0:TILE, :] = plan[0:TILE] * 2 + (plan[0:TILE] >> 3)
    plan_v[TILE : TILE + 1, :] = plan[TILE : TILE + 1]
    plan_v[TILE + 1 : TILE + 2, :] = jnp.broadcast_to(total, (1, TILES))
    to_scalar = pltpu.make_async_copy(plan_v, plan_s, sems.at[1])
    to_scalar.start()
    to_scalar.wait()
    load.wait()

    def tile_steps(step, _):
        for half in range(UNROLL // 8):
            found = []
            for u in range(8):
                t = step * UNROLL + half * 8 + u
                queries = jnp.concatenate(
                    [got[pl.ds(plan_s[r, t], 2)].reshape(TOK, FEAT) for r in range(TILE)], 0
                )
                similarity = dot_t(held[plan_s[TILE, t]], queries)
                found.append(jnp.max(similarity, axis=0, keepdims=True))
            at = pl.multiple_of(step * UNROLL + half * 8, 8)
            best[pl.ds(at, 8), :] = jnp.concatenate(found, 0)
        return 0

    lax.fori_loop(0, (plan_s[TILE + 1, 0] + (UNROLL - 1)) // UNROLL, tile_steps, 0)

    adder = ((iota((SLOTS, FEAT), 0) >> 5) == (iota((SLOTS, FEAT), 1) & 7)).astype(bf16)
    sums = dot_n(jnp.concatenate(split3(best[...]), 1), jnp.concatenate([adder] * 3, 0))
    sums = jnp.where(here, jnp.concatenate([sums, sums], 1), 0.0)
    first = first_wide[:, 0:1]
    t = iota((LOCAL, TILES), 1)
    owned = jnp.where((first <= t) & (t < first + tiles), 1.0, 0.0).astype(bf16)
    y = dot_n(jnp.concatenate([owned] * 3, 1), jnp.concatenate(split3(sums), 0))
    y = jnp.where(slot < count, y, 0.0)
    x = x >> 9
    for b in (7, 6, 5, 4, 3, 2, 1, 0):
        moves = ((x >> b) & 1) == 1
        y = jnp.where(moves, 0.0, y) + pltpu.roll(jnp.where(moves, y, 0.0), 1 << b, 1)
        x = jnp.where(moves, 0, x) + pltpu.roll(jnp.where(moves, x, 0), 1 << b, 1)
    scores = jnp.concatenate(
        [
            jnp.sum(jnp.where(cands[k : k + 1, :] == passage, y, 0.0), axis=0, keepdims=True)
            for k in range(VIS)
        ],
        0,
    )
    k8, l8 = iota((VIS, FEAT), 0), iota((VIS, FEAT), 1)
    repeat = ((l8 & 7) == k8).astype(f32)
    spread_back = ((high < VIS * VIS) & (low == (high >> 3))).astype(bf16)
    by_slot = dot_tn(scores, repeat, lax.Precision.HIGHEST)
    out_ref[...] = by_slot * dot_n(visit, spread_back)


def return_kernel(back_ref, got_ref, out_ref):
    out_ref[...] = dot_n(back_ref[...], got_ref[...], lax.Precision.HIGHEST)


VM = pl.BlockSpec(memory_space=pltpu.VMEM)
SM = pl.BlockSpec(memory_space=pltpu.SMEM)
ANY = pl.BlockSpec(memory_space=pl.ANY)
PARAMS = pltpu.CompilerParams(vmem_limit_bytes=VMEM_LIMIT)
STEPS = (0, 7, 1, 6, 2, 5, 3, 4)


def in_hbm(x):
    return pltpu.with_memory_space_constraint(x, pltpu.HBM)


def fill(lengths, tokens):
    return pl.pallas_call(
        fill_kernel,
        out_shape=pltpu.HBM((LOCAL, PLEN, FEAT), bf16),
        in_specs=[SM, VM],
        out_specs=ANY,
        scratch_shapes=[pltpu.VMEM((LOCAL, PLEN, FEAT), bf16), pltpu.SemaphoreType.DMA],
        compiler_params=PARAMS,
        cost_estimate=pl.CostEstimate(flops=1 << 22, bytes_accessed=1 << 22, transcendentals=0),
    )(lengths, tokens)


def pack(tokens, owners, cands):
    return pl.pallas_call(
        pack_kernel,
        out_shape=jax.ShapeDtypeStruct((PIECES, 16, FEAT), bf16),
        in_specs=[ANY, ANY, ANY],
        out_specs=VM,
        scratch_shapes=[
            pltpu.VMEM((VIS, QDEV), i32),
            pltpu.VMEM((VIS * VIS, QDEV), i32),
            pltpu.SemaphoreType.DMA((3,)),
        ],
        compiler_params=PARAMS,
    )(in_hbm(tokens), in_hbm(owners), in_hbm(cands))


def build(row, blocks):
    return pl.pallas_call(
        build_kernel,
        out_shape=(
            pltpu.HBM((COLS, CELL, 16, FEAT), bf16),
            jax.ShapeDtypeStruct((GROUP, SLOTS), f32),
        ),
        in_specs=[SM] + [ANY] * ROWS,
        out_specs=(ANY, VM),
        scratch_shapes=[
            pltpu.VMEM((ROWS * PIECES, 16, FEAT), bf16),
            pltpu.VMEM((COLS, CELL, 16, FEAT), bf16),
            pltpu.VMEM((8, COLS * QDEV), i32),
            pltpu.SMEM((8, COLS * QDEV), i32),
            pltpu.SemaphoreType.DMA((ROWS,)),
            pltpu.SemaphoreType.DMA,
            pltpu.SemaphoreType.DMA((len(PARTS),)),
        ],
        compiler_params=PARAMS,
    )(row, *blocks)


def score(me, got, passages):
    return pl.pallas_call(
        score_kernel,
        out_shape=jax.ShapeDtypeStruct((SLOTS, FEAT), f32),
        in_specs=[SM, VM, VM, ANY],
        out_specs=VM,
        scratch_shapes=[
            pltpu.VMEM((LOCAL, PLEN, FEAT), bf16),
            pltpu.VMEM((16, TILES), i32),
            pltpu.SMEM((16, TILES), i32),
            pltpu.VMEM((TILES, SLOTS), f32),
            pltpu.SemaphoreType.DMA((2,)),
        ],
        compiler_params=PARAMS,
    )(me, got.reshape(COLS * CELL, 16, FEAT), got, in_hbm(passages))


def hand_back(back, got):
    return pl.pallas_call(
        return_kernel,
        out_shape=jax.ShapeDtypeStruct((GROUP, FEAT), f32),
        in_specs=[VM, VM],
        out_specs=VM,
        compiler_params=PARAMS,
    )(back, got)


def shards(query_tokens, visit_owner, visit_passages, passage_tokens, passage_lengths):
    row = lax.axis_index("qbatch").astype(i32)
    me = lax.axis_index("corpus").astype(i32) * ROWS + row + 1
    own = pack(
        query_tokens.reshape(TOK, 16, FEAT),
        visit_owner.T,
        jnp.transpose(visit_passages, (1, 2, 0)).reshape(VIS * VIS, QDEV),
    )
    up = [(i, (i + 1) % ROWS) for i in range(ROWS)]
    down = [(i, (i + ROWS - 1) % ROWS) for i in range(ROWS)]
    blocks = [own]
    left = right = own
    for step in range(1, ROWS // 2 + 1):
        left = lax.ppermute(left, "qbatch", up)
        blocks.append(left)
        if step < ROWS // 2:
            right = lax.ppermute(right, "qbatch", down)
            blocks.append(right)
    passages = fill(passage_lengths, passage_tokens)
    send, back = build(row[None], blocks)
    got = lax.all_to_all(send, "corpus", split_axis=0, concat_axis=0, tiled=True)
    scored = score(me[None], got, passages)
    returned = lax.all_to_all(
        scored.reshape(COLS, VIS, FEAT), "corpus", split_axis=0, concat_axis=0, tiled=True
    )
    mine = hand_back(back, returned.reshape(SLOTS, FEAT))
    parts = lax.all_to_all(
        mine.reshape(ROWS, QDEV, FEAT), "qbatch", split_axis=0, concat_axis=0, tiled=True
    )
    return jnp.sum(parts, axis=0)[:, 0 : VIS * VIS]


def solution(mesh):
    placed = (
        P(("corpus", "qbatch"), None, None),
        P(("corpus", "qbatch"), None),
        P(("corpus", "qbatch"), None, None),
        P(("corpus", "qbatch"), None, None),
        P(("corpus", "qbatch")),
    )
    return jax.shard_map(
        shards, mesh=mesh, in_specs=placed, out_specs=P(("corpus", "qbatch"), None), check_vma=False
    )
```

time: 122 us -> 108 us (0.89)
  local copies, waits for them, and re-layouts: 6.69 us -> 1.59 us
  blocking collectives: 32.3 us -> 27.2 us
  other arithmetic: 2.37 us -> 0.61 us
  Pallas kernels: 17.7 us -> 16.2 us
    all_to_all x1, blocking collectives: 17.7 us -> 12.2 us  [shards(): lax.all_to_all(scored.reshape(COLS, VIS, FEAT), 'corpus', split_axis=0, c...]
    unnamed x11 -> x4, local copies, waits for them, and re-layouts: 6.6 us -> 1.59 us
    pallas_call x1, Pallas kernels: 12.3 us -> 8.06 us  [score(): pl.pallas_call(score_kernel, out_shape=jax.ShapeDtypeStruct((SLOTS, FEAT)...]
    pallas_call x2 -> x3, Pallas kernels: 5.08 us -> 7.92 us  [the longest x1 4.33 us: build(): pl.pallas_call(build_kernel, out_shape=(pltpu.HBM((COLS, CELL, 16, FEAT),...]
  transfers between devices with their start and end apart: 8 -> 8, of which waited for: 5 -> 5; matrix products, arithmetic and copies ran while one was open for 0% -> 0% of each run, Pallas kernels for 1% -> 2%
where the time goes in v2:
time: 108 us
  waiting for transfers between devices  38.5 us (36%)
  blocking collectives  27.2 us (25%)
  starting transfers between devices  23.7 us (22%)
  Pallas kernels  16.2 us (15%)
  local copies, waits for them, and re-layouts  1.59 us (1%)
    all_to_all x1, waiting for transfers between devices, shards(): lax.all_to_all(send, 'corpus', split_axis=0, concat_axis=0, tiled=True)  25.5 us
    all_to_all x1, blocking collectives, shards(): lax.all_to_all(mine.reshape(ROWS, QDEV, FEAT), 'qbatch', split_axis=0, co...  15 us
    ppermute x4, waiting for transfers between devices, shards(): left = lax.ppermute(left, 'qbatch', up)  13.1 us
    all_to_all x1, blocking collectives, shards(): lax.all_to_all(scored.reshape(COLS, VIS, FEAT), 'corpus', split_axis=0, c...  12.2 us
    all_to_all x1, starting transfers between devices, shards(): lax.all_to_all(send, 'corpus', split_axis=0, concat_axis=0, tiled=True)  11.8 us
    ppermute x3, starting transfers between devices, shards(): right = lax.ppermute(right, 'qbatch', down)  9.38 us
    pallas_call x1, Pallas kernels, score(): pl.pallas_call(score_kernel, out_shape=jax.ShapeDtypeStruct((SLOTS, FEAT)...  8.06 us
    pallas_call x1, Pallas kernels, build(): pl.pallas_call(build_kernel, out_shape=(pltpu.HBM((COLS, CELL, 16, FEAT),...  4.33 us
  transfers between devices with their start and end apart: 8, of which 5 were waited for; matrix products, arithmetic and copies ran while one was open for 0% of the time, Pallas kernels for 2%

profile of v2, /device:TPU:1, one launch (start us, length us, event | category | flops | bytes accessed | tf_op | source)
XLA Modules:
  0.0 108.0 jit_solution(8149653819546756060)
XLA Ops:
  0.0 1.0 shard_map.55.refs_0_
  1.0 2.5 %collective-permute-start = (bf16[33,16,128]{2,1,0:T(8,128)(2,1)S(1)}, bf16[33,16,128]{2,1,0:T(8,128)(2,1)S(1)}, u32[]{:S(2)}, u32[]{:S(2)}) collective-permute-start(bf16[33,16,128]{2,1,0:T(8,128)(2,1)S(1)} %shard_map.55.refs_0_), channel_id=1, source_target_pairs={{0,1},{1,2},{2,3},{3,4},{4,5},{5,6},{6,7},{7,0},{8,9},{9,10},{10,1... | collective-permute-start | bytes 405512 | tf_op jit(solution)/shard_map/ppermute | solution.py:353
  3.5 4.0 %collective-permute-start.1 = (bf16[33,16,128]{2,1,0:T(8,128)(2,1)S(1)}, bf16[33,16,128]{2,1,0:T(8,128)(2,1)S(1)}, u32[]{:S(2)}, u32[]{:S(2)}) collective-permute-start(bf16[33,16,128]{2,1,0:T(8,128)(2,1)S(1)} %shard_map.55.refs_0_), channel_id=1, source_target_pairs={{0,7},{1,0},{2,1},{3,2},{4,3},{5,4},{6,5},{7,6},{8,15},{9,8},{10,9... | collective-permute-start | bytes 405512 | tf_op jit(solution)/shard_map/ppermute | solution.py:356
  7.6 3.2 %collective-permute-done.refs_1_ = bf16[33,16,128]{2,1,0:T(8,128)(2,1)S(1)} collective-permute-done((bf16[33,16,128]{2,1,0:T(8,128)(2,1)S(1)}, bf16[33,16,128]{2,1,0:T(8,128)(2,1)S(1)}, u32[]{:S(2)}, u32[]{:S(2)}) %collective-permute-start) | collective-permute-done | bytes 135200 | tf_op jit(solution)/shard_map/ppermute | solution.py:353
  10.8 0.0 collective-permute-start.2
  10.8 0.0 collective-permute-done.1.refs_2_
  10.8 2.7 %collective-permute-start.3 = (bf16[33,16,128]{2,1,0:T(8,128)(2,1)S(1)}, bf16[33,16,128]{2,1,0:T(8,128)(2,1)S(1)}, u32[]{:S(2)}, u32[]{:S(2)}) collective-permute-start(bf16[33,16,128]{2,1,0:T(8,128)(2,1)S(1)} %collective-permute-done.1.refs_2_), channel_id=1, source_target_pairs={{0,7},{1,0},{2,1},{3,2},{4,3},{5,4},{6,5},{7,6},{8,15},{9,8},{10,9... | collective-permute-start | bytes 405512 | tf_op jit(solution)/shard_map/ppermute | solution.py:356
  13.5 2.4 %collective-permute-done.2.refs_3_ = bf16[33,16,128]{2,1,0:T(8,128)(2,1)S(1)} collective-permute-done((bf16[33,16,128]{2,1,0:T(8,128)(2,1)S(1)}, bf16[33,16,128]{2,1,0:T(8,128)(2,1)S(1)}, u32[]{:S(2)}, u32[]{:S(2)}) %collective-permute-start.2) | collective-permute-done | bytes 135200 | tf_op jit(solution)/shard_map/ppermute | solution.py:353
  15.8 0.0 collective-permute-start.4
  15.9 0.0 collective-permute-done.3.refs_4_
  15.9 2.7 %collective-permute-start.5 = (bf16[33,16,128]{2,1,0:T(8,128)(2,1)S(1)}, bf16[33,16,128]{2,1,0:T(8,128)(2,1)S(1)}, u32[]{:S(2)}, u32[]{:S(2)}) collective-permute-start(bf16[33,16,128]{2,1,0:T(8,128)(2,1)S(1)} %collective-permute-done.3.refs_4_), channel_id=1, source_target_pairs={{0,7},{1,0},{2,1},{3,2},{4,3},{5,4},{6,5},{7,6},{8,15},{9,8},{10,9... | collective-permute-start | bytes 405512 | tf_op jit(solution)/shard_map/ppermute | solution.py:356
  18.5 2.4 %collective-permute-done.4.refs_5_ = bf16[33,16,128]{2,1,0:T(8,128)(2,1)S(1)} collective-permute-done((bf16[33,16,128]{2,1,0:T(8,128)(2,1)S(1)}, bf16[33,16,128]{2,1,0:T(8,128)(2,1)S(1)}, u32[]{:S(2)}, u32[]{:S(2)}) %collective-permute-start.4) | collective-permute-done | bytes 135200 | tf_op jit(solution)/shard_map/ppermute | solution.py:353
  20.9 0.0 collective-permute-start.6
  20.9 0.0 collective-permute-done.5.refs_6_
  20.9 5.1 %collective-permute-done.6.refs_7_ = bf16[33,16,128]{2,1,0:T(8,128)(2,1)S(1)} collective-permute-done((bf16[33,16,128]{2,1,0:T(8,128)(2,1)S(1)}, bf16[33,16,128]{2,1,0:T(8,128)(2,1)S(1)}, u32[]{:S(2)}, u32[]{:S(2)}) %collective-permute-start.6) | collective-permute-done | bytes 135200 | tf_op jit(solution)/shard_map/ppermute | solution.py:353
  26.0 4.3 %shard_map.56 = (bf16[32,17,16,128]{3,2,1,0:T(8,128)(2,1)}, f32[128,256]{1,0:T(8,128)S(1)}) custom-call(s32[1]{0:T(128)} %bitcast.row_ref, bf16[33,16,128]{2,1,0:T(8,128)(2,1)S(1)} %shard_map.55.refs_0_, bf16[33,16,128]{2,1,0:T(8,128)(2,1)S(1)} %collective-permute-done.refs_1_, bf16[33,16,128]{2,1,0:T(8,128)(2,1)S(1)} %collective-permute-done.1.refs_2_, ...), custom_call_target="tpu_custom_call" | custom-call | tf_op jit(solution)/shard_map/pallas_call | solution.py:292
  30.3 0.0 copy-start.1
  30.4 11.8 %all-to-all-start = ((bf16[32,17,16,128]{3,2,1,0:T(8,128)(2,1)}), bf16[32,17,16,128]{3,2,1,0:T(8,128)(2,1)S(1)}, u32[]{:S(2)}, u32[]{:S(2)}) async-start(bf16[32,17,16,128]{3,2,1,0:T(8,128)(2,1)} %get-tuple-element.8), calls=%async_computation | async-start | bytes 4456448 | tf_op jit(solution)/shard_map/all_to_all | solution.py:360
  42.1 0.0 copy-done.1
  42.1 0.0 copy-start
  42.2 1.6 %copy-done = bf16[64,128,128]{2,1,0:T(8,128)(2,1)S(1)} copy-done((bf16[64,128,128]{2,1,0:T(8,128)(2,1)S(1)}, bf16[64,128,128]{2,1,0:T(8,128)(2,1)}, u32[]{:S(2)}) %copy-start) | copy-done | bytes 2097176
  43.7 2.6 %shard_map.57.passage_ref = bf16[64,128,128]{2,1,0:T(8,128)(2,1)} custom-call(s32[64]{0:T(128)S(1)} %copy-done.1, bf16[64,128,128]{2,1,0:T(8,128)(2,1)S(1)} %copy-done), custom_call_target="tpu_custom_call" | custom-call | flops 4194304 | bytes 4194304 | tf_op jit(solution)/shard_map/pallas_call | solution.py:265
  46.4 25.5 %all-to-all-done.cells_ref = bf16[32,17,16,128]{3,2,1,0:T(8,128)(2,1)S(1)} async-done(((bf16[32,17,16,128]{3,2,1,0:T(8,128)(2,1)}), bf16[32,17,16,128]{3,2,1,0:T(8,128)(2,1)S(1)}, u32[]{:S(2)}, u32[]{:S(2)}) %all-to-all-start) | async-done | bytes 2228256 | tf_op jit(solution)/shard_map/all_to_all | solution.py:360
  71.8 8.1 %shard_map.58 = f32[256,128]{1,0:T(8,128)S(1)} custom-call(s32[1]{0:T(128)} %bitcast.5.me_ref, bf16[544,16,128]{2,1,0:T(8,128)(2,1)S(1)} %bitcast.12, bf16[32,17,16,128]{3,2,1,0:T(8,128)(2,1)S(1)} %all-to-all-done.cells_ref, bf16[64,128,128]{2,1,0:T(8,128)(2,1)} %shard_map.57.passage_ref), custom_call_target="tpu_custom_call" | custom-call | tf_op jit(solution)/shard_map/pallas_call | solution.py:314
  79.9 12.2 %all_to_all.15 = f32[32,8,128]{2,1,0:T(8,128)S(1)} all-to-all(f32[32,8,128]{2,1,0:T(8,128)S(1)} %bitcast.13), channel_id=1, replica_groups=mesh['corpus'=32,'qbatch'=8] {'corpus'}, dimensions={0} | all-to-all | bytes 262144 | tf_op jit(solution)/shard_map/all_to_all | solution.py:362
  92.1 0.3 shard_map.59
  92.4 15.0 %all_to_all.16 = f32[8,16,128]{2,1,0:T(8,128)S(1)} all-to-all(f32[8,16,128]{2,1,0:T(8,128)S(1)} %bitcast.15), channel_id=1, replica_groups=mesh['corpus'=32,'qbatch'=8] {'qbatch'}, dimensions={0} | all-to-all | bytes 131072 | tf_op jit(solution)/shard_map/all_to_all | solution.py:366
  107.4 0.6 reduce_sum.9
Async XLA Ops:
  1.0 9.8 %collective-permute-start = (bf16[33,16,128]{2,1,0:T(8,128)(2,1)S(1)}, bf16[33,16,128]{2,1,0:T(8,128)(2,1)S(1)}, u32[]{:S(2)}, u32[]{:S(2)}) collective-permute-start(bf16[33,16,128]{2,1,0:T(8,128)(2,1)S(1)} %shard_map.55.refs_0_), channel_id=1, source_target_pairs={{0,1},{1,2},{2,3},{3,4},{4,5},{5,6},{6,7},{7,0},{8,9},{9,10},{10,1... | collective-permute-start | bytes 405512 | tf_op jit(solution)/shard_map/ppermute | solution.py:353
  3.5 7.3 %collective-permute-start.1 = (bf16[33,16,128]{2,1,0:T(8,128)(2,1)S(1)}, bf16[33,16,128]{2,1,0:T(8,128)(2,1)S(1)}, u32[]{:S(2)}, u32[]{:S(2)}) collective-permute-start(bf16[33,16,128]{2,1,0:T(8,128)(2,1)S(1)} %shard_map.55.refs_0_), channel_id=1, source_target_pairs={{0,7},{1,0},{2,1},{3,2},{4,3},{5,4},{6,5},{7,6},{8,15},{9,8},{10,9... | collective-permute-start | bytes 405512 | tf_op jit(solution)/shard_map/ppermute | solution.py:356
  10.8 5.1 %collective-permute-start.2 = (bf16[33,16,128]{2,1,0:T(8,128)(2,1)S(1)}, bf16[33,16,128]{2,1,0:T(8,128)(2,1)S(1)}, u32[]{:S(2)}, u32[]{:S(2)}) collective-permute-start(bf16[33,16,128]{2,1,0:T(8,128)(2,1)S(1)} %collective-permute-done.refs_1_), channel_id=1, source_target_pairs={{0,1},{1,2},{2,3},{3,4},{4,5},{5,6},{6,7},{7,0},{8,9},{9,10},{10,1... | collective-permute-start | bytes 405512 | tf_op jit(solution)/shard_map/ppermute | solution.py:353
  10.8 5.1 %collective-permute-start.3 = (bf16[33,16,128]{2,1,0:T(8,128)(2,1)S(1)}, bf16[33,16,128]{2,1,0:T(8,128)(2,1)S(1)}, u32[]{:S(2)}, u32[]{:S(2)}) collective-permute-start(bf16[33,16,128]{2,1,0:T(8,128)(2,1)S(1)} %collective-permute-done.1.refs_2_), channel_id=1, source_target_pairs={{0,7},{1,0},{2,1},{3,2},{4,3},{5,4},{6,5},{7,6},{8,15},{9,8},{10,9... | collective-permute-start | bytes 405512 | tf_op jit(solution)/shard_map/ppermute | solution.py:356
  15.8 5.1 %collective-permute-start.4 = (bf16[33,16,128]{2,1,0:T(8,128)(2,1)S(1)}, bf16[33,16,128]{2,1,0:T(8,128)(2,1)S(1)}, u32[]{:S(2)}, u32[]{:S(2)}) collective-permute-start(bf16[33,16,128]{2,1,0:T(8,128)(2,1)S(1)} %collective-permute-done.2.refs_3_), channel_id=1, source_target_pairs={{0,1},{1,2},{2,3},{3,4},{4,5},{5,6},{6,7},{7,0},{8,9},{9,10},{10,1... | collective-permute-start | bytes 405512 | tf_op jit(solution)/shard_map/ppermute | solution.py:353
  15.9 5.1 %collective-permute-start.5 = (bf16[33,16,128]{2,1,0:T(8,128)(2,1)S(1)}, bf16[33,16,128]{2,1,0:T(8,128)(2,1)S(1)}, u32[]{:S(2)}, u32[]{:S(2)}) collective-permute-start(bf16[33,16,128]{2,1,0:T(8,128)(2,1)S(1)} %collective-permute-done.3.refs_4_), channel_id=1, source_target_pairs={{0,7},{1,0},{2,1},{3,2},{4,3},{5,4},{6,5},{7,6},{8,15},{9,8},{10,9... | collective-permute-start | bytes 405512 | tf_op jit(solution)/shard_map/ppermute | solution.py:356
  20.9 5.1 %collective-permute-start.6 = (bf16[33,16,128]{2,1,0:T(8,128)(2,1)S(1)}, bf16[33,16,128]{2,1,0:T(8,128)(2,1)S(1)}, u32[]{:S(2)}, u32[]{:S(2)}) collective-permute-start(bf16[33,16,128]{2,1,0:T(8,128)(2,1)S(1)} %collective-permute-done.4.refs_5_), channel_id=1, source_target_pairs={{0,1},{1,2},{2,3},{3,4},{4,5},{5,6},{6,7},{7,0},{8,9},{9,10},{10,1... | collective-permute-start | bytes 405512 | tf_op jit(solution)/shard_map/ppermute | solution.py:353
  30.3 11.8 %copy-start.1 = (s32[64]{0:T(128)S(1)}, s32[64]{0:T(128)}, u32[]{:S(2)}) copy-start(s32[64]{0:T(128)} %length_ref.1) | copy-start | bytes 772
  30.4 41.5 %all-to-all-start = ((bf16[32,17,16,128]{3,2,1,0:T(8,128)(2,1)}), bf16[32,17,16,128]{3,2,1,0:T(8,128)(2,1)S(1)}, u32[]{:S(2)}, u32[]{:S(2)}) async-start(bf16[32,17,16,128]{3,2,1,0:T(8,128)(2,1)} %get-tuple-element.8), calls=%async_computation | async-start | bytes 4456448 | tf_op jit(solution)/shard_map/all_to_all | solution.py:360
  42.1 1.6 %copy-start = (bf16[64,128,128]{2,1,0:T(8,128)(2,1)S(1)}, bf16[64,128,128]{2,1,0:T(8,128)(2,1)}, u32[]{:S(2)}) copy-start(bf16[64,128,128]{2,1,0:T(8,128)(2,1)} %tokens_ref.1) | copy-start | bytes 6291460

commit v3 on v2

--- a/solution.py
+++ b/solution.py
@@ -11,6 +11,7 @@
 PLEN = 128
 LOCAL = 64
 VIS = 8
+HV = VIS // 2
 QDEV = 16
 ROWS = 8
 COLS = 32
@@ -20,8 +21,7 @@
 CELL = VIS * 2 + 1
 TILE = 8
 TILES = 384
-UNROLL = 16
-PARTS = ((0, 8), (8, 16), (16, 24), (24, 30), (30, 32))
+UNROLL = 48
 VMEM_LIMIT = 16 * 1024 * 1024
 
 
@@ -45,20 +45,6 @@
     return lax.dot_general(
         a, b, (((0,), (0,)), ((), ())), precision=precision, preferred_element_type=f32
     )
-
-
-def fill_kernel(length_ref, tokens_ref, out_ref, filled, sem):
-    token = iota((PLEN, FEAT), 0)
-
-    def one(p, _):
-        tokens = tokens_ref[p].astype(f32)
-        filled[p] = jnp.where(token < length_ref[p], tokens, tokens[0:1, :]).astype(bf16)
-        return 0
-
-    lax.fori_loop(0, LOCAL, one, 0)
-    copy = pltpu.make_async_copy(filled, out_ref, sem)
-    copy.start()
-    copy.wait()
 
 
 def pack_kernel(tokens_ref, owner_ref, cand_ref, out_ref, owners, cands, sems):
@@ -78,19 +64,17 @@
     loads[2].wait()
 
 
-def build_kernel(row_ref, *refs):
+def build_kernel(*refs):
     blocks = refs[:ROWS]
-    send_ref, back_ref, buf, out_v, idx_v, idx_s, sems, idx_sem, out_sems = refs[ROWS:]
-    row = row_ref[0]
-    copies = []
-    for s, (block, step) in enumerate(zip(blocks, STEPS)):
-        at = buf.at[pl.ds(lax.rem(row + step, ROWS) * PIECES, PIECES)]
-        copy = pltpu.make_async_copy(block, at, sems.at[s])
-        copy.start()
-        copies.append(copy)
-    for copy in copies:
-        copy.wait()
-    lists = jnp.concatenate([buf[z * PIECES + TOK] for z in range(ROWS)], 0)
+    send_ref, back_ref, buf, idx_v, idx_s, idx_sem = refs[ROWS:]
+    row = lax.axis_index("qbatch").astype(i32)
+    lists = [
+        jnp.where(lax.rem(row + step, ROWS) == z, block[TOK].astype(f32), 0.0)
+        for z in range(ROWS)
+        for block, step in zip(blocks, STEPS)
+    ]
+    lists = [sum(lists[z * ROWS : z * ROWS + ROWS]) for z in range(ROWS)]
+    lists = jnp.concatenate(lists, 0).astype(bf16)
     eye = (iota((GROUP, FEAT), 0) == iota((GROUP, FEAT), 1)).astype(bf16)
     owners = dot_t(eye[0:QDEV], lists)
     wanted = (iota((COLS, GROUP), 0) * ROWS + (row + 1)).astype(f32)
@@ -108,25 +92,19 @@
     idx_v[...] = (query >> 4) * PIECES + (query & (QDEV - 1)) * 2
     to_scalar = pltpu.make_async_copy(idx_v, idx_s, idx_sem)
     to_scalar.start()
-    out_v[:, VIS * 2] = dot_n(chosen, lists).astype(bf16).reshape(COLS, QDEV, FEAT)
+    send_ref[:, VIS * 2] = dot_n(chosen, lists).astype(bf16).reshape(COLS, QDEV, FEAT)
     slots = pick[:, 0:VIS, :].reshape(SLOTS, GROUP).astype(bf16)
     back_ref[...] = dot_t(eye, slots)
+    for block, step in zip(blocks, STEPS):
+        buf[pl.ds(lax.rem(row + step, ROWS) * PIECES, PIECES)] = block[...]
     to_scalar.wait()
 
     def one(c, _):
         for s in range(VIS):
-            out_v[c, 2 * s : 2 * s + 2] = buf[pl.ds(idx_s[0, c * QDEV + s], 2)]
+            send_ref[c, 2 * s : 2 * s + 2] = buf[pl.ds(idx_s[0, c * QDEV + s], 2)]
         return 0
 
-    outs = []
-    for start, stop in PARTS:
-        lax.fori_loop(start, stop, one, 0)
-        some = pl.ds(start, stop - start)
-        copy = pltpu.make_async_copy(out_v.at[some], send_ref.at[some], out_sems.at[len(outs)])
-        copy.start()
-        outs.append(copy)
-    for copy in outs:
-        copy.wait()
+    lax.fori_loop(0, COLS, one, 0)
 
 
 def split3(x):
@@ -137,11 +115,14 @@
 
 
 def score_kernel(
-    me_ref, got, cells_ref, passage_ref, out_ref, held, plan_v, plan_s, best, sems
+    got, cells_ref, passage_ref, length_ref, out_ref, held, lengths, plan_v, plan_s, best, sems
 ):
     load = pltpu.make_async_copy(passage_ref, held, sems.at[0])
     load.start()
-    me = me_ref[0].astype(f32)
+    load_lengths = pltpu.make_async_copy(length_ref, lengths, sems.at[2])
+    load_lengths.start()
+    me = lax.axis_index("corpus") * ROWS + lax.axis_index("qbatch") + 1
+    me = me.astype(i32).astype(f32)
     lists = cells_ref[:, VIS * 2].astype(f32)[:, 0:VIS, :].reshape(SLOTS, FEAT)
     lane = iota((SLOTS, FEAT), 1)
     visit = jnp.where((lists == me) & (lane < VIS), 1.0, 0.0).astype(bf16)
@@ -201,7 +182,9 @@
     to_scalar = pltpu.make_async_copy(plan_v, plan_s, sems.at[1])
     to_scalar.start()
     to_scalar.wait()
+    load_lengths.wait()
     load.wait()
+    token = iota((PLEN, FEAT), 0)
 
     def tile_steps(step, _):
         for half in range(UNROLL // 8):
@@ -211,7 +194,10 @@
                 queries = jnp.concatenate(
                     [got[pl.ds(plan_s[r, t], 2)].reshape(TOK, FEAT) for r in range(TILE)], 0
                 )
-                similarity = dot_t(held[plan_s[TILE, t]], queries)
+                p = plan_s[TILE, t]
+                tokens = held[p].astype(f32)
+                tokens = jnp.where(token < lengths[p], tokens, tokens[0:1, :]).astype(bf16)
+                similarity = dot_t(tokens, queries)
                 found.append(jnp.max(similarity, axis=0, keepdims=True))
             at = pl.multiple_of(step * UNROLL + half * 8, 8)
             best[pl.ds(at, 8), :] = jnp.concatenate(found, 0)
@@ -243,15 +229,27 @@
     repeat = ((l8 & 7) == k8).astype(f32)
     spread_back = ((high < VIS * VIS) & (low == (high >> 3))).astype(bf16)
     by_slot = dot_tn(scores, repeat, lax.Precision.HIGHEST)
-    out_ref[...] = by_slot * dot_n(visit, spread_back)
+    by_slot = (by_slot * dot_n(visit, spread_back)).reshape(COLS, VIS, FEAT)
+    out_ref[...] = by_slot[:, 0:HV] + pltpu.roll(by_slot[:, HV:VIS], FEAT // 2, 2)
 
 
 def return_kernel(back_ref, got_ref, out_ref):
-    out_ref[...] = dot_n(back_ref[...], got_ref[...], lax.Precision.HIGHEST)
+    got = got_ref[...]
+    lower = iota((COLS, HV, FEAT), 2) < FEAT // 2
+    first = jnp.where(lower, got, 0.0)
+    second = jnp.where(lower, pltpu.roll(got, FEAT // 2, 2), 0.0)
+    by_slot = jnp.concatenate([first, second], 1).reshape(SLOTS, FEAT)
+    mine = dot_n(back_ref[...], by_slot, lax.Precision.HIGHEST).reshape(ROWS, QDEV, FEAT)
+    out_ref[...] = mine[:, 0:8] + pltpu.roll(mine[:, 8:QDEV], FEAT // 2, 2)
+
+
+def sum_kernel(parts_ref, out_ref):
+    total = jnp.sum(parts_ref[...], axis=0)
+    out_ref[0:8] = total[:, 0 : FEAT // 2]
+    out_ref[8:QDEV] = total[:, FEAT // 2 : FEAT]
 
 
 VM = pl.BlockSpec(memory_space=pltpu.VMEM)
-SM = pl.BlockSpec(memory_space=pltpu.SMEM)
 ANY = pl.BlockSpec(memory_space=pl.ANY)
 PARAMS = pltpu.CompilerParams(vmem_limit_bytes=VMEM_LIMIT)
 STEPS = (0, 7, 1, 6, 2, 5, 3, 4)
@@ -259,18 +257,6 @@
 
 def in_hbm(x):
     return pltpu.with_memory_space_constraint(x, pltpu.HBM)
-
-
-def fill(lengths, tokens):
-    return pl.pallas_call(
-        fill_kernel,
-        out_shape=pltpu.HBM((LOCAL, PLEN, FEAT), bf16),
-        in_specs=[SM, VM],
-        out_specs=ANY,
-        scratch_shapes=[pltpu.VMEM((LOCAL, PLEN, FEAT), bf16), pltpu.SemaphoreType.DMA],
-        compiler_params=PARAMS,
-        cost_estimate=pl.CostEstimate(flops=1 << 22, bytes_accessed=1 << 22, transcendentals=0),
-    )(lengths, tokens)
 
 
 def pack(tokens, owners, cands):
@@ -288,58 +274,64 @@
     )(in_hbm(tokens), in_hbm(owners), in_hbm(cands))
 
 
-def build(row, blocks):
+def build(blocks):
     return pl.pallas_call(
         build_kernel,
         out_shape=(
-            pltpu.HBM((COLS, CELL, 16, FEAT), bf16),
+            jax.ShapeDtypeStruct((COLS, CELL, 16, FEAT), bf16),
             jax.ShapeDtypeStruct((GROUP, SLOTS), f32),
         ),
-        in_specs=[SM] + [ANY] * ROWS,
-        out_specs=(ANY, VM),
+        in_specs=[VM] * ROWS,
+        out_specs=(VM, VM),
         scratch_shapes=[
             pltpu.VMEM((ROWS * PIECES, 16, FEAT), bf16),
-            pltpu.VMEM((COLS, CELL, 16, FEAT), bf16),
             pltpu.VMEM((8, COLS * QDEV), i32),
             pltpu.SMEM((8, COLS * QDEV), i32),
-            pltpu.SemaphoreType.DMA((ROWS,)),
             pltpu.SemaphoreType.DMA,
-            pltpu.SemaphoreType.DMA((len(PARTS),)),
         ],
         compiler_params=PARAMS,
-    )(row, *blocks)
-
-
-def score(me, got, passages):
+    )(*blocks)
+
+
+def score(got, passages, lengths):
     return pl.pallas_call(
         score_kernel,
-        out_shape=jax.ShapeDtypeStruct((SLOTS, FEAT), f32),
-        in_specs=[SM, VM, VM, ANY],
+        out_shape=jax.ShapeDtypeStruct((COLS, HV, FEAT), f32),
+        in_specs=[VM, VM, ANY, ANY],
         out_specs=VM,
         scratch_shapes=[
             pltpu.VMEM((LOCAL, PLEN, FEAT), bf16),
+            pltpu.SMEM((LOCAL,), i32),
             pltpu.VMEM((16, TILES), i32),
             pltpu.SMEM((16, TILES), i32),
             pltpu.VMEM((TILES, SLOTS), f32),
-            pltpu.SemaphoreType.DMA((2,)),
+            pltpu.SemaphoreType.DMA((3,)),
         ],
         compiler_params=PARAMS,
-    )(me, got.reshape(COLS * CELL, 16, FEAT), got, in_hbm(passages))
+    )(got.reshape(COLS * CELL, 16, FEAT), got, in_hbm(passages), in_hbm(lengths))
 
 
 def hand_back(back, got):
     return pl.pallas_call(
         return_kernel,
-        out_shape=jax.ShapeDtypeStruct((GROUP, FEAT), f32),
+        out_shape=jax.ShapeDtypeStruct((ROWS, 8, FEAT), f32),
         in_specs=[VM, VM],
         out_specs=VM,
         compiler_params=PARAMS,
     )(back, got)
 
 
+def add_up(parts):
+    return pl.pallas_call(
+        sum_kernel,
+        out_shape=jax.ShapeDtypeStruct((QDEV, VIS * VIS), f32),
+        in_specs=[VM],
+        out_specs=VM,
+        compiler_params=PARAMS,
+    )(parts)
+
+
 def shards(query_tokens, visit_owner, visit_passages, passage_tokens, passage_lengths):
-    row = lax.axis_index("qbatch").astype(i32)
-    me = lax.axis_index("corpus").astype(i32) * ROWS + row + 1
     own = pack(
         query_tokens.reshape(TOK, 16, FEAT),
         visit_owner.T,
@@ -355,18 +347,12 @@
         if step < ROWS // 2:
             right = lax.ppermute(right, "qbatch", down)
             blocks.append(right)
-    passages = fill(passage_lengths, passage_tokens)
-    send, back = build(row[None], blocks)
+    send, back = build(blocks)
     got = lax.all_to_all(send, "corpus", split_axis=0, concat_axis=0, tiled=True)
-    scored = score(me[None], got, passages)
-    returned = lax.all_to_all(
-        scored.reshape(COLS, VIS, FEAT), "corpus", split_axis=0, concat_axis=0, tiled=True
-    )
-    mine = hand_back(back, returned.reshape(SLOTS, FEAT))
-    parts = lax.all_to_all(
-        mine.reshape(ROWS, QDEV, FEAT), "qbatch", split_axis=0, concat_axis=0, tiled=True
-    )
-    return jnp.sum(parts, axis=0)[:, 0 : VIS * VIS]
+    scored = score(got, passage_tokens, passage_lengths)
+    returned = lax.all_to_all(scored, "corpus", split_axis=0, concat_axis=0, tiled=True)
+    mine = hand_back(back, returned)
+    return add_up(lax.all_to_all(mine, "qbatch", split_axis=0, concat_axis=0, tiled=True))
 
 
 def solution(mesh):

time: 108 us -> 104 us (0.963)
  blocking collectives: 27.2 us -> 66.4 us
  waiting for transfers between devices: 38.5 us -> 13.1 us
  starting transfers between devices: 23.7 us -> 11.9 us
  Pallas kernels: 16.2 us -> 12.4 us
  local copies, waits for them, and re-layouts: 1.59 us -> 0 us
    all_to_all x2 -> x3, blocking collectives: 27.2 us -> 66.4 us  [the longest x1 41.7 us: shards(): lax.all_to_all(send, 'corpus', split_axis=0, concat_axis=0, tiled=True)]
    all_to_all x1 -> x0, waiting for transfers between devices: 25.5 us -> none  [shards(): lax.all_to_all(send, 'corpus', split_axis=0, concat_axis=0, tiled=True)]
    all_to_all x1 -> x0, starting transfers between devices: 11.8 us -> none  [shards(): lax.all_to_all(send, 'corpus', split_axis=0, concat_axis=0, tiled=True)]
    pallas_call x4, Pallas kernels: 15.3 us -> 11.5 us  [the longest x1 8.31 us: score(): pl.pallas_call(score_kernel, out_shape=jax.ShapeDtypeStruct((COLS, HV, FE...]
    unnamed x4 -> x0, local copies, waits for them, and re-layouts: 1.59 us -> none
  transfers between devices with their start and end apart: 8 -> 7, of which waited for: 5 -> 4; matrix products, arithmetic and copies ran while one was open for 0% -> 0% of each run, Pallas kernels for 2% -> 0%
where the time goes in v3:
time: 104 us
  blocking collectives  66.4 us (64%)
  waiting for transfers between devices  13.1 us (13%)
  Pallas kernels  12.4 us (12%)
  starting transfers between devices  11.9 us (11%)
    all_to_all x1, blocking collectives, shards(): lax.all_to_all(send, 'corpus', split_axis=0, concat_axis=0, tiled=True)  41.7 us
    ppermute x4, waiting for transfers between devices, shards(): left = lax.ppermute(left, 'qbatch', up)  13.1 us
    all_to_all x1, blocking collectives, shards(): lax.all_to_all(scored, 'corpus', split_axis=0, concat_axis=0, tiled=True)  12.6 us
    all_to_all x1, blocking collectives, shards(): lax.all_to_all(mine, 'qbatch', split_axis=0, concat_axis=0, tiled=True)  12.1 us
    ppermute x3, starting transfers between devices, shards(): right = lax.ppermute(right, 'qbatch', down)  9.38 us
    pallas_call x1, Pallas kernels, score(): pl.pallas_call(score_kernel, out_shape=jax.ShapeDtypeStruct((COLS, HV, FE...  8.31 us
    ppermute x4, starting transfers between devices, shards(): left = lax.ppermute(left, 'qbatch', up)  2.55 us
  transfers between devices with their start and end apart: 7, of which 4 were waited for; matrix products, arithmetic and copies ran while one was open for 0% of the time, Pallas kernels for 0%

profile of v3, /device:TPU:1, one launch (start us, length us, event | category | flops | bytes accessed | tf_op | source)
XLA Modules:
  0.0 103.9 jit_solution(16455849955574040059)
XLA Ops:
  0.0 1.0 shard_map.55.refs_0_
  1.0 2.5 %collective-permute-start = (bf16[33,16,128]{2,1,0:T(8,128)(2,1)S(1)}, bf16[33,16,128]{2,1,0:T(8,128)(2,1)S(1)}, u32[]{:S(2)}, u32[]{:S(2)}) collective-permute-start(bf16[33,16,128]{2,1,0:T(8,128)(2,1)S(1)} %shard_map.55.refs_0_), channel_id=1, source_target_pairs={{0,1},{1,2},{2,3},{3,4},{4,5},{5,6},{6,7},{7,0},{8,9},{9,10},{10,1... | collective-permute-start | bytes 405512 | tf_op jit(solution)/shard_map/ppermute | solution.py:345
  3.5 4.0 %collective-permute-start.1 = (bf16[33,16,128]{2,1,0:T(8,128)(2,1)S(1)}, bf16[33,16,128]{2,1,0:T(8,128)(2,1)S(1)}, u32[]{:S(2)}, u32[]{:S(2)}) collective-permute-start(bf16[33,16,128]{2,1,0:T(8,128)(2,1)S(1)} %shard_map.55.refs_0_), channel_id=1, source_target_pairs={{0,7},{1,0},{2,1},{3,2},{4,3},{5,4},{6,5},{7,6},{8,15},{9,8},{10,9... | collective-permute-start | bytes 405512 | tf_op jit(solution)/shard_map/ppermute | solution.py:348
  7.6 3.2 %collective-permute-done.refs_1_ = bf16[33,16,128]{2,1,0:T(8,128)(2,1)S(1)} collective-permute-done((bf16[33,16,128]{2,1,0:T(8,128)(2,1)S(1)}, bf16[33,16,128]{2,1,0:T(8,128)(2,1)S(1)}, u32[]{:S(2)}, u32[]{:S(2)}) %collective-permute-start) | collective-permute-done | bytes 135200 | tf_op jit(solution)/shard_map/ppermute | solution.py:345
  10.8 0.0 collective-permute-start.2
  10.8 0.0 collective-permute-done.1.refs_2_
  10.8 2.7 %collective-permute-start.3 = (bf16[33,16,128]{2,1,0:T(8,128)(2,1)S(1)}, bf16[33,16,128]{2,1,0:T(8,128)(2,1)S(1)}, u32[]{:S(2)}, u32[]{:S(2)}) collective-permute-start(bf16[33,16,128]{2,1,0:T(8,128)(2,1)S(1)} %collective-permute-done.1.refs_2_), channel_id=1, source_target_pairs={{0,7},{1,0},{2,1},{3,2},{4,3},{5,4},{6,5},{7,6},{8,15},{9,8},{10,9... | collective-permute-start | bytes 405512 | tf_op jit(solution)/shard_map/ppermute | solution.py:348
  13.5 2.4 %collective-permute-done.2.refs_3_ = bf16[33,16,128]{2,1,0:T(8,128)(2,1)S(1)} collective-permute-done((bf16[33,16,128]{2,1,0:T(8,128)(2,1)S(1)}, bf16[33,16,128]{2,1,0:T(8,128)(2,1)S(1)}, u32[]{:S(2)}, u32[]{:S(2)}) %collective-permute-start.2) | collective-permute-done | bytes 135200 | tf_op jit(solution)/shard_map/ppermute | solution.py:345
  15.8 0.0 collective-permute-start.4
  15.9 0.0 collective-permute-done.3.refs_4_
  15.9 2.7 %collective-permute-start.5 = (bf16[33,16,128]{2,1,0:T(8,128)(2,1)S(1)}, bf16[33,16,128]{2,1,0:T(8,128)(2,1)S(1)}, u32[]{:S(2)}, u32[]{:S(2)}) collective-permute-start(bf16[33,16,128]{2,1,0:T(8,128)(2,1)S(1)} %collective-permute-done.3.refs_4_), channel_id=1, source_target_pairs={{0,7},{1,0},{2,1},{3,2},{4,3},{5,4},{6,5},{7,6},{8,15},{9,8},{10,9... | collective-permute-start | bytes 405512 | tf_op jit(solution)/shard_map/ppermute | solution.py:348
  18.5 2.4 %collective-permute-done.4.refs_5_ = bf16[33,16,128]{2,1,0:T(8,128)(2,1)S(1)} collective-permute-done((bf16[33,16,128]{2,1,0:T(8,128)(2,1)S(1)}, bf16[33,16,128]{2,1,0:T(8,128)(2,1)S(1)}, u32[]{:S(2)}, u32[]{:S(2)}) %collective-permute-start.4) | collective-permute-done | bytes 135200 | tf_op jit(solution)/shard_map/ppermute | solution.py:345
  20.9 0.0 collective-permute-start.6
  20.9 0.0 collective-permute-done.5.refs_6_
  20.9 5.1 %collective-permute-done.6.refs_7_ = bf16[33,16,128]{2,1,0:T(8,128)(2,1)S(1)} collective-permute-done((bf16[33,16,128]{2,1,0:T(8,128)(2,1)S(1)}, bf16[33,16,128]{2,1,0:T(8,128)(2,1)S(1)}, u32[]{:S(2)}, u32[]{:S(2)}) %collective-permute-start.6) | collective-permute-done | bytes 135200 | tf_op jit(solution)/shard_map/ppermute | solution.py:345
  26.0 2.1 %shard_map.56 = (bf16[32,17,16,128]{3,2,1,0:T(8,128)(2,1)S(1)}, f32[128,256]{1,0:T(8,128)S(1)}) custom-call(bf16[33,16,128]{2,1,0:T(8,128)(2,1)S(1)} %shard_map.55.refs_0_, bf16[33,16,128]{2,1,0:T(8,128)(2,1)S(1)} %collective-permute-done.refs_1_, bf16[33,16,128]{2,1,0:T(8,128)(2,1)S(1)} %collective-permute-done.1.refs_2_, ...), custom_call_target="tpu_custom_call" | custom-call | tf_op jit(solution)/shard_map/pallas_call | solution.py:278
  28.1 41.7 %all_to_all.15.cells_ref = bf16[32,17,16,128]{3,2,1,0:T(8,128)(2,1)S(1)} all-to-all(bf16[32,17,16,128]{3,2,1,0:T(8,128)(2,1)S(1)} %get-tuple-element.8), channel_id=1, replica_groups=mesh['corpus'=32,'qbatch'=8] {'corpus'}, dimensions={0} | all-to-all | bytes 4456448 | tf_op jit(solution)/shard_map/all_to_all | solution.py:351
  69.8 8.3 %shard_map.57 = f32[32,4,128]{2,1,0:T(4,128)S(1)} custom-call(bf16[544,16,128]{2,1,0:T(8,128)(2,1)S(1)} %bitcast.6, bf16[32,17,16,128]{3,2,1,0:T(8,128)(2,1)S(1)} %all_to_all.15.cells_ref, bf16[64,128,128]{2,1,0:T(8,128)(2,1)} %passage_ref.1, s32[64]{0:T(128)} %length_ref.1), custom_call_target="tpu_custom_call" | custom-call | tf_op jit(solution)/shard_map/pallas_call | solution.py:297
  78.1 12.6 %all_to_all.16.got_ref = f32[32,4,128]{2,1,0:T(4,128)S(1)} all-to-all(f32[32,4,128]{2,1,0:T(4,128)S(1)} %shard_map.57), channel_id=1, replica_groups=mesh['corpus'=32,'qbatch'=8] {'corpus'}, dimensions={0} | all-to-all | bytes 131072 | tf_op jit(solution)/shard_map/all_to_all | solution.py:353
  90.7 0.4 shard_map.58
  91.1 12.1 %all_to_all.17.parts_ref = f32[8,8,128]{2,1,0:T(8,128)S(1)} all-to-all(f32[8,8,128]{2,1,0:T(8,128)S(1)} %shard_map.58), channel_id=1, replica_groups=mesh['corpus'=32,'qbatch'=8] {'qbatch'}, dimensions={0} | all-to-all | bytes 65536 | tf_op jit(solution)/shard_map/all_to_all | solution.py:355
  103.2 0.7 shard_map.59
Async XLA Ops:
  1.0 9.8 %collective-permute-start = (bf16[33,16,128]{2,1,0:T(8,128)(2,1)S(1)}, bf16[33,16,128]{2,1,0:T(8,128)(2,1)S(1)}, u32[]{:S(2)}, u32[]{:S(2)}) collective-permute-start(bf16[33,16,128]{2,1,0:T(8,128)(2,1)S(1)} %shard_map.55.refs_0_), channel_id=1, source_target_pairs={{0,1},{1,2},{2,3},{3,4},{4,5},{5,6},{6,7},{7,0},{8,9},{9,10},{10,1... | collective-permute-start | bytes 405512 | tf_op jit(solution)/shard_map/ppermute | solution.py:345
  3.5 7.3 %collective-permute-start.1 = (bf16[33,16,128]{2,1,0:T(8,128)(2,1)S(1)}, bf16[33,16,128]{2,1,0:T(8,128)(2,1)S(1)}, u32[]{:S(2)}, u32[]{:S(2)}) collective-permute-start(bf16[33,16,128]{2,1,0:T(8,128)(2,1)S(1)} %shard_map.55.refs_0_), channel_id=1, source_target_pairs={{0,7},{1,0},{2,1},{3,2},{4,3},{5,4},{6,5},{7,6},{8,15},{9,8},{10,9... | collective-permute-start | bytes 405512 | tf_op jit(solution)/shard_map/ppermute | solution.py:348
  10.8 5.1 %collective-permute-start.2 = (bf16[33,16,128]{2,1,0:T(8,128)(2,1)S(1)}, bf16[33,16,128]{2,1,0:T(8,128)(2,1)S(1)}, u32[]{:S(2)}, u32[]{:S(2)}) collective-permute-start(bf16[33,16,128]{2,1,0:T(8,128)(2,1)S(1)} %collective-permute-done.refs_1_), channel_id=1, source_target_pairs={{0,1},{1,2},{2,3},{3,4},{4,5},{5,6},{6,7},{7,0},{8,9},{9,10},{10,1... | collective-permute-start | bytes 405512 | tf_op jit(solution)/shard_map/ppermute | solution.py:345
  10.8 5.1 %collective-permute-start.3 = (bf16[33,16,128]{2,1,0:T(8,128)(2,1)S(1)}, bf16[33,16,128]{2,1,0:T(8,128)(2,1)S(1)}, u32[]{:S(2)}, u32[]{:S(2)}) collective-permute-start(bf16[33,16,128]{2,1,0:T(8,128)(2,1)S(1)} %collective-permute-done.1.refs_2_), channel_id=1, source_target_pairs={{0,7},{1,0},{2,1},{3,2},{4,3},{5,4},{6,5},{7,6},{8,15},{9,8},{10,9... | collective-permute-start | bytes 405512 | tf_op jit(solution)/shard_map/ppermute | solution.py:348
  15.8 5.1 %collective-permute-start.4 = (bf16[33,16,128]{2,1,0:T(8,128)(2,1)S(1)}, bf16[33,16,128]{2,1,0:T(8,128)(2,1)S(1)}, u32[]{:S(2)}, u32[]{:S(2)}) collective-permute-start(bf16[33,16,128]{2,1,0:T(8,128)(2,1)S(1)} %collective-permute-done.2.refs_3_), channel_id=1, source_target_pairs={{0,1},{1,2},{2,3},{3,4},{4,5},{5,6},{6,7},{7,0},{8,9},{9,10},{10,1... | collective-permute-start | bytes 405512 | tf_op jit(solution)/shard_map/ppermute | solution.py:345
  15.9 5.1 %collective-permute-start.5 = (bf16[33,16,128]{2,1,0:T(8,128)(2,1)S(1)}, bf16[33,16,128]{2,1,0:T(8,128)(2,1)S(1)}, u32[]{:S(2)}, u32[]{:S(2)}) collective-permute-start(bf16[33,16,128]{2,1,0:T(8,128)(2,1)S(1)} %collective-permute-done.3.refs_4_), channel_id=1, source_target_pairs={{0,7},{1,0},{2,1},{3,2},{4,3},{5,4},{6,5},{7,6},{8,15},{9,8},{10,9... | collective-permute-start | bytes 405512 | tf_op jit(solution)/shard_map/ppermute | solution.py:348
  20.9 5.1 %collective-permute-start.6 = (bf16[33,16,128]{2,1,0:T(8,128)(2,1)S(1)}, bf16[33,16,128]{2,1,0:T(8,128)(2,1)S(1)}, u32[]{:S(2)}, u32[]{:S(2)}) collective-permute-start(bf16[33,16,128]{2,1,0:T(8,128)(2,1)S(1)} %collective-permute-done.4.refs_5_), channel_id=1, source_target_pairs={{0,1},{1,2},{2,3},{3,4},{4,5},{5,6},{6,7},{7,0},{8,9},{9,10},{10,1... | collective-permute-start | bytes 405512 | tf_op jit(solution)/shard_map/ppermute | solution.py:345

commit v4 on v3

--- a/solution.py
+++ b/solution.py
@@ -21,7 +21,7 @@
 CELL = VIS * 2 + 1
 TILE = 8
 TILES = 384
-UNROLL = 48
+UNROLL = 72
 VMEM_LIMIT = 16 * 1024 * 1024
 
 
@@ -92,7 +92,14 @@
     idx_v[...] = (query >> 4) * PIECES + (query & (QDEV - 1)) * 2
     to_scalar = pltpu.make_async_copy(idx_v, idx_s, idx_sem)
     to_scalar.start()
-    send_ref[:, VIS * 2] = dot_n(chosen, lists).astype(bf16).reshape(COLS, QDEV, FEAT)
+    rows = dot_n(chosen, lists)
+    lane = iota((COLS * QDEV, FEAT), 1)
+    target = ((iota((COLS * QDEV, FEAT), 0) >> 4) * ROWS + (row + 1)).astype(f32)
+    visit = jnp.where((rows == target) & (lane < VIS), 1.0, 0.0).astype(bf16)
+    low, high = iota((FEAT, FEAT), 0), iota((FEAT, FEAT), 1)
+    spread = ((high >= VIS) & (low == (high >> 3) - 1)).astype(bf16)
+    kept = (rows * dot_n(visit, spread)).astype(bf16)
+    send_ref[:, VIS * 2] = kept.reshape(COLS, QDEV, FEAT)
     slots = pick[:, 0:VIS, :].reshape(SLOTS, GROUP).astype(bf16)
     back_ref[...] = dot_t(eye, slots)
     for block, step in zip(blocks, STEPS):
@@ -121,18 +128,11 @@
     load.start()
     load_lengths = pltpu.make_async_copy(length_ref, lengths, sems.at[2])
     load_lengths.start()
-    me = lax.axis_index("corpus") * ROWS + lax.axis_index("qbatch") + 1
-    me = me.astype(i32).astype(f32)
-    lists = cells_ref[:, VIS * 2].astype(f32)[:, 0:VIS, :].reshape(SLOTS, FEAT)
-    lane = iota((SLOTS, FEAT), 1)
-    visit = jnp.where((lists == me) & (lane < VIS), 1.0, 0.0).astype(bf16)
+    kept = cells_ref[:, VIS * 2].astype(f32)[:, 0:VIS, :].reshape(SLOTS, FEAT)
     low, high = iota((FEAT, FEAT), 0), iota((FEAT, FEAT), 1)
-    spread = ((high >= VIS) & (low == (high >> 3) - 1)).astype(bf16)
-    mine = dot_n(visit, spread)
-    kept = (lists * mine).astype(bf16)
     k16, l16 = iota((16, FEAT), 0), iota((16, FEAT), 1)
     fold = ((l16 >= VIS) & (l16 < VIS + VIS * VIS) & ((l16 & 7) == k16)).astype(bf16)
-    cands = dot_t(fold, kept)
+    cands = dot_t(fold, kept.astype(bf16))
 
     wide = (LOCAL, SLOTS)
     passage = (iota(wide, 0) + 1).astype(f32)
@@ -181,6 +181,10 @@
     plan_v[TILE + 1 : TILE + 2, :] = jnp.broadcast_to(total, (1, TILES))
     to_scalar = pltpu.make_async_copy(plan_v, plan_s, sems.at[1])
     to_scalar.start()
+    adder = ((iota((SLOTS, FEAT), 0) >> 5) == (iota((SLOTS, FEAT), 1) & 7)).astype(bf16)
+    first = first_wide[:, 0:1]
+    t = iota((LOCAL, TILES), 1)
+    owned = jnp.where((first <= t) & (t < first + tiles), 1.0, 0.0).astype(bf16)
     to_scalar.wait()
     load_lengths.wait()
     load.wait()
@@ -205,12 +209,8 @@
 
     lax.fori_loop(0, (plan_s[TILE + 1, 0] + (UNROLL - 1)) // UNROLL, tile_steps, 0)
 
-    adder = ((iota((SLOTS, FEAT), 0) >> 5) == (iota((SLOTS, FEAT), 1) & 7)).astype(bf16)
     sums = dot_n(jnp.concatenate(split3(best[...]), 1), jnp.concatenate([adder] * 3, 0))
     sums = jnp.where(here, jnp.concatenate([sums, sums], 1), 0.0)
-    first = first_wide[:, 0:1]
-    t = iota((LOCAL, TILES), 1)
-    owned = jnp.where((first <= t) & (t < first + tiles), 1.0, 0.0).astype(bf16)
     y = dot_n(jnp.concatenate([owned] * 3, 1), jnp.concatenate(split3(sums), 0))
     y = jnp.where(slot < count, y, 0.0)
     x = x >> 9
@@ -227,9 +227,9 @@
     )
     k8, l8 = iota((VIS, FEAT), 0), iota((VIS, FEAT), 1)
     repeat = ((l8 & 7) == k8).astype(f32)
-    spread_back = ((high < VIS * VIS) & (low == (high >> 3))).astype(bf16)
     by_slot = dot_tn(scores, repeat, lax.Precision.HIGHEST)
-    by_slot = (by_slot * dot_n(visit, spread_back)).reshape(COLS, VIS, FEAT)
+    mine = pltpu.roll(kept, FEAT - VIS, 1) > 0.5
+    by_slot = jnp.where(mine, by_slot, 0.0).reshape(COLS, VIS, FEAT)
     out_ref[...] = by_slot[:, 0:HV] + pltpu.roll(by_slot[:, HV:VIS], FEAT // 2, 2)
 
 
@@ -341,12 +341,14 @@
     down = [(i, (i + ROWS - 1) % ROWS) for i in range(ROWS)]
     blocks = [own]
     left = right = own
-    for step in range(1, ROWS // 2 + 1):
+    for step in range(1, ROWS // 2):
         left = lax.ppermute(left, "qbatch", up)
-        blocks.append(left)
-        if step < ROWS // 2:
-            right = lax.ppermute(right, "qbatch", down)
-            blocks.append(right)
+        right = lax.ppermute(right, "qbatch", down)
+        if step == 1:
+            right, again = lax.optimization_barrier((right, own))
+            far = lax.ppermute(again, "qbatch", [(i, (i + ROWS // 2) % ROWS) for i in range(ROWS)])
+        blocks += [left, right]
+    blocks.append(far)
     send, back = build(blocks)
     got = lax.all_to_all(send, "corpus", split_axis=0, concat_axis=0, tiled=True)
     scored = score(got, passage_tokens, passage_lengths)

time: 104 us -> 103 us (level)
  starting transfers between devices: 11.9 us -> 14.6 us
  blocking collectives: 66.4 us -> 64.7 us
  Pallas kernels: 12.4 us -> 11.1 us
    ppermute x3, starting transfers between devices: 9.38 us -> 13 us  [shards(): right = lax.ppermute(right, 'qbatch', down)]
    ppermute x4 -> x3, waiting for transfers between devices: 13.1 us -> 10 us  [shards(): left = lax.ppermute(left, 'qbatch', up)]
    ppermute x3, waiting for transfers between devices: 0.01 us -> 2.89 us  [shards(): right = lax.ppermute(right, 'qbatch', down)]
    ppermute x4 -> x3, starting transfers between devices: 2.55 us -> 0.01 us  [shards(): left = lax.ppermute(left, 'qbatch', up)]
    ppermute x0 -> x1, starting transfers between devices: none -> 1.59 us  [shards(): lax.ppermute(again, 'qbatch', [(i, (i + ROWS // 2) % ROWS) for i in range...]
    all_to_all x1, blocking collectives: 41.7 us -> 40.2 us  [shards(): lax.all_to_all(send, 'corpus', split_axis=0, concat_axis=0, tiled=True)]
    pallas_call x1, Pallas kernels: 8.31 us -> 6.94 us  [score(): pl.pallas_call(score_kernel, out_shape=jax.ShapeDtypeStruct((COLS, HV, FE...]
  transfers between devices with their start and end apart: 7 -> 7, of which waited for: 4 -> 5; matrix products, arithmetic and copies ran while one was open for 0% -> 0% of each run, Pallas kernels for 0% -> 0%
where the time goes in v4:
time: 103 us
  blocking collectives  64.7 us (63%)
  starting transfers between devices  14.6 us (14%)
  waiting for transfers between devices  12.9 us (13%)
  Pallas kernels  11.1 us (11%)
    all_to_all x1, blocking collectives, shards(): lax.all_to_all(send, 'corpus', split_axis=0, concat_axis=0, tiled=True)  40.2 us
    all_to_all x1, blocking collectives, shards(): lax.all_to_all(scored, 'corpus', split_axis=0, concat_axis=0, tiled=True)  13.1 us
    ppermute x3, starting transfers between devices, shards(): right = lax.ppermute(right, 'qbatch', down)  13 us
    all_to_all x1, blocking collectives, shards(): lax.all_to_all(mine, 'qbatch', split_axis=0, concat_axis=0, tiled=True)  11.4 us
    ppermute x3, waiting for transfers between devices, shards(): left = lax.ppermute(left, 'qbatch', up)  10 us
    pallas_call x1, Pallas kernels, score(): pl.pallas_call(score_kernel, out_shape=jax.ShapeDtypeStruct((COLS, HV, FE...  6.94 us
    ppermute x3, waiting for transfers between devices, shards(): right = lax.ppermute(right, 'qbatch', down)  2.89 us
    pallas_call x1, Pallas kernels, build(): pl.pallas_call(build_kernel, out_shape=(jax.ShapeDtypeStruct((COLS, CELL,...  2.08 us
  transfers between devices with their start and end apart: 7, of which 5 were waited for; matrix products, arithmetic and copies ran while one was open for 0% of the time, Pallas kernels for 0%

profile of v4, /device:TPU:1, one launch (start us, length us, event | category | flops | bytes accessed | tf_op | source)
XLA Modules:
  0.0 103.3 jit_solution(9469272145011956708)
XLA Ops:
  0.0 1.0 shard_map.55.refs_0_
  1.0 6.5 %collective-permute-start.1 = (bf16[33,16,128]{2,1,0:T(8,128)(2,1)S(1)}, bf16[33,16,128]{2,1,0:T(8,128)(2,1)S(1)}, u32[]{:S(2)}, u32[]{:S(2)}) collective-permute-start(bf16[33,16,128]{2,1,0:T(8,128)(2,1)S(1)} %shard_map.55.refs_0_), channel_id=1, source_target_pairs={{0,7},{1,0},{2,1},{3,2},{4,3},{5,4},{6,5},{7,6},{8,15},{9,8},{10,9... | collective-permute-start | bytes 405512 | tf_op jit(solution)/shard_map/ppermute | solution.py:346
  7.5 0.0 collective-permute-start
  7.5 2.2 %collective-permute-done.1.refs_2_ = bf16[33,16,128]{2,1,0:T(8,128)(2,1)S(1)} collective-permute-done((bf16[33,16,128]{2,1,0:T(8,128)(2,1)S(1)}, bf16[33,16,128]{2,1,0:T(8,128)(2,1)S(1)}, u32[]{:S(2)}, u32[]{:S(2)}) %collective-permute-start.1) | collective-permute-done | bytes 135200 | tf_op jit(solution)/shard_map/ppermute | solution.py:346
  9.7 3.4 %collective-permute-start.3 = (bf16[33,16,128]{2,1,0:T(8,128)(2,1)S(1)}, bf16[33,16,128]{2,1,0:T(8,128)(2,1)S(1)}, u32[]{:S(2)}, u32[]{:S(2)}) collective-permute-start(bf16[33,16,128]{2,1,0:T(8,128)(2,1)S(1)} %collective-permute-done.1.refs_2_), channel_id=1, source_target_pairs={{0,7},{1,0},{2,1},{3,2},{4,3},{5,4},{6,5},{7,6},{8,15},{9,8},{10,9... | collective-permute-start | bytes 405512 | tf_op jit(solution)/shard_map/ppermute | solution.py:346
  13.1 0.0 collective-permute-done.refs_1_
  13.1 0.0 collective-permute-start.2
  13.1 1.6 %collective-permute-start.6 = (bf16[33,16,128]{2,1,0:T(8,128)(2,1)S(1)}, bf16[33,16,128]{2,1,0:T(8,128)(2,1)S(1)}, u32[]{:S(2)}, u32[]{:S(2)}) collective-permute-start(bf16[33,16,128]{2,1,0:T(8,128)(2,1)S(1)} %shard_map.55.refs_0_), channel_id=1, source_target_pairs={{0,4},{1,5},{2,6},{3,7},{4,0},{5,1},{6,2},{7,3},{8,12},{9,13},{10,... | collective-permute-start | bytes 405512 | tf_op jit(solution)/shard_map/ppermute | solution.py:349
  14.7 0.4 collective-permute-done.3.refs_4_
  15.1 3.1 %collective-permute-start.5 = (bf16[33,16,128]{2,1,0:T(8,128)(2,1)S(1)}, bf16[33,16,128]{2,1,0:T(8,128)(2,1)S(1)}, u32[]{:S(2)}, u32[]{:S(2)}) collective-permute-start(bf16[33,16,128]{2,1,0:T(8,128)(2,1)S(1)} %collective-permute-done.3.refs_4_), channel_id=1, source_target_pairs={{0,7},{1,0},{2,1},{3,2},{4,3},{5,4},{6,5},{7,6},{8,15},{9,8},{10,9... | collective-permute-start | bytes 405512 | tf_op jit(solution)/shard_map/ppermute | solution.py:346
  18.2 5.2 %collective-permute-done.2.refs_3_ = bf16[33,16,128]{2,1,0:T(8,128)(2,1)S(1)} collective-permute-done((bf16[33,16,128]{2,1,0:T(8,128)(2,1)S(1)}, bf16[33,16,128]{2,1,0:T(8,128)(2,1)S(1)}, u32[]{:S(2)}, u32[]{:S(2)}) %collective-permute-start.2) | collective-permute-done | bytes 135200 | tf_op jit(solution)/shard_map/ppermute | solution.py:345
  23.4 0.0 collective-permute-start.4
  23.4 0.0 collective-permute-done.6.refs_7_
  23.4 0.2 collective-permute-done.5.refs_6_
  23.6 4.8 %collective-permute-done.4.refs_5_ = bf16[33,16,128]{2,1,0:T(8,128)(2,1)S(1)} collective-permute-done((bf16[33,16,128]{2,1,0:T(8,128)(2,1)S(1)}, bf16[33,16,128]{2,1,0:T(8,128)(2,1)S(1)}, u32[]{:S(2)}, u32[]{:S(2)}) %collective-permute-start.4) | collective-permute-done | bytes 135200 | tf_op jit(solution)/shard_map/ppermute | solution.py:345
  28.5 2.1 %shard_map.56 = (bf16[32,17,16,128]{3,2,1,0:T(8,128)(2,1)S(1)}, f32[128,256]{1,0:T(8,128)S(1)}) custom-call(bf16[33,16,128]{2,1,0:T(8,128)(2,1)S(1)} %shard_map.55.refs_0_, bf16[33,16,128]{2,1,0:T(8,128)(2,1)S(1)} %collective-permute-done.refs_1_, bf16[33,16,128]{2,1,0:T(8,128)(2,1)S(1)} %collective-permute-done.1.refs_2_, ...), custom_call_target="tpu_custom_call" | custom-call | tf_op jit(solution)/shard_map/pallas_call | solution.py:278
  30.5 40.2 %all_to_all.15.cells_ref = bf16[32,17,16,128]{3,2,1,0:T(8,128)(2,1)S(1)} all-to-all(bf16[32,17,16,128]{3,2,1,0:T(8,128)(2,1)S(1)} %get-tuple-element.12), channel_id=1, replica_groups=mesh['corpus'=32,'qbatch'=8] {'corpus'}, dimensions={0} | all-to-all | bytes 4456448 | tf_op jit(solution)/shard_map/all_to_all | solution.py:353
  70.7 6.9 %shard_map.57 = f32[32,4,128]{2,1,0:T(4,128)S(1)} custom-call(bf16[544,16,128]{2,1,0:T(8,128)(2,1)S(1)} %bitcast.6, bf16[32,17,16,128]{3,2,1,0:T(8,128)(2,1)S(1)} %all_to_all.15.cells_ref, bf16[64,128,128]{2,1,0:T(8,128)(2,1)} %passage_ref.1, s32[64]{0:T(128)} %length_ref.1), custom_call_target="tpu_custom_call" | custom-call | tf_op jit(solution)/shard_map/pallas_call | solution.py:297
  77.7 13.1 %all_to_all.16.got_ref = f32[32,4,128]{2,1,0:T(4,128)S(1)} all-to-all(f32[32,4,128]{2,1,0:T(4,128)S(1)} %shard_map.57), channel_id=1, replica_groups=mesh['corpus'=32,'qbatch'=8] {'corpus'}, dimensions={0} | all-to-all | bytes 131072 | tf_op jit(solution)/shard_map/all_to_all | solution.py:355
  90.8 0.4 shard_map.58
  91.2 11.4 %all_to_all.17.parts_ref = f32[8,8,128]{2,1,0:T(8,128)S(1)} all-to-all(f32[8,8,128]{2,1,0:T(8,128)S(1)} %shard_map.58), channel_id=1, replica_groups=mesh['corpus'=32,'qbatch'=8] {'qbatch'}, dimensions={0} | all-to-all | bytes 65536 | tf_op jit(solution)/shard_map/all_to_all | solution.py:357
  102.6 0.7 shard_map.59
Async XLA Ops:
  1.0 8.7 %collective-permute-start.1 = (bf16[33,16,128]{2,1,0:T(8,128)(2,1)S(1)}, bf16[33,16,128]{2,1,0:T(8,128)(2,1)S(1)}, u32[]{:S(2)}, u32[]{:S(2)}) collective-permute-start(bf16[33,16,128]{2,1,0:T(8,128)(2,1)S(1)} %shard_map.55.refs_0_), channel_id=1, source_target_pairs={{0,7},{1,0},{2,1},{3,2},{4,3},{5,4},{6,5},{7,6},{8,15},{9,8},{10,9... | collective-permute-start | bytes 405512 | tf_op jit(solution)/shard_map/ppermute | solution.py:346
  7.5 5.7 %collective-permute-start = (bf16[33,16,128]{2,1,0:T(8,128)(2,1)S(1)}, bf16[33,16,128]{2,1,0:T(8,128)(2,1)S(1)}, u32[]{:S(2)}, u32[]{:S(2)}) collective-permute-start(bf16[33,16,128]{2,1,0:T(8,128)(2,1)S(1)} %shard_map.55.refs_0_), channel_id=1, source_target_pairs={{0,1},{1,2},{2,3},{3,4},{4,5},{5,6},{6,7},{7,0},{8,9},{9,10},{10,1... | collective-permute-start | bytes 405512 | tf_op jit(solution)/shard_map/ppermute | solution.py:345
  9.7 5.4 %collective-permute-start.3 = (bf16[33,16,128]{2,1,0:T(8,128)(2,1)S(1)}, bf16[33,16,128]{2,1,0:T(8,128)(2,1)S(1)}, u32[]{:S(2)}, u32[]{:S(2)}) collective-permute-start(bf16[33,16,128]{2,1,0:T(8,128)(2,1)S(1)} %collective-permute-done.1.refs_2_), channel_id=1, source_target_pairs={{0,7},{1,0},{2,1},{3,2},{4,3},{5,4},{6,5},{7,6},{8,15},{9,8},{10,9... | collective-permute-start | bytes 405512 | tf_op jit(solution)/shard_map/ppermute | solution.py:346
  13.1 10.3 %collective-permute-start.2 = (bf16[33,16,128]{2,1,0:T(8,128)(2,1)S(1)}, bf16[33,16,128]{2,1,0:T(8,128)(2,1)S(1)}, u32[]{:S(2)}, u32[]{:S(2)}) collective-permute-start(bf16[33,16,128]{2,1,0:T(8,128)(2,1)S(1)} %collective-permute-done.refs_1_), channel_id=1, source_target_pairs={{0,1},{1,2},{2,3},{3,4},{4,5},{5,6},{6,7},{7,0},{8,9},{9,10},{10,1... | collective-permute-start | bytes 405512 | tf_op jit(solution)/shard_map/ppermute | solution.py:345
  13.1 10.3 %collective-permute-start.6 = (bf16[33,16,128]{2,1,0:T(8,128)(2,1)S(1)}, bf16[33,16,128]{2,1,0:T(8,128)(2,1)S(1)}, u32[]{:S(2)}, u32[]{:S(2)}) collective-permute-start(bf16[33,16,128]{2,1,0:T(8,128)(2,1)S(1)} %shard_map.55.refs_0_), channel_id=1, source_target_pairs={{0,4},{1,5},{2,6},{3,7},{4,0},{5,1},{6,2},{7,3},{8,12},{9,13},{10,... | collective-permute-start | bytes 405512 | tf_op jit(solution)/shard_map/ppermute | solution.py:349
  15.1 8.5 %collective-permute-start.5 = (bf16[33,16,128]{2,1,0:T(8,128)(2,1)S(1)}, bf16[33,16,128]{2,1,0:T(8,128)(2,1)S(1)}, u32[]{:S(2)}, u32[]{:S(2)}) collective-permute-start(bf16[33,16,128]{2,1,0:T(8,128)(2,1)S(1)} %collective-permute-done.3.refs_4_), channel_id=1, source_target_pairs={{0,7},{1,0},{2,1},{3,2},{4,3},{5,4},{6,5},{7,6},{8,15},{9,8},{10,9... | collective-permute-start | bytes 405512 | tf_op jit(solution)/shard_map/ppermute | solution.py:346
  23.4 5.1 %collective-permute-start.4 = (bf16[33,16,128]{2,1,0:T(8,128)(2,1)S(1)}, bf16[33,16,128]{2,1,0:T(8,128)(2,1)S(1)}, u32[]{:S(2)}, u32[]{:S(2)}) collective-permute-start(bf16[33,16,128]{2,1,0:T(8,128)(2,1)S(1)} %collective-permute-done.2.refs_3_), channel_id=1, source_target_pairs={{0,1},{1,2},{2,3},{3,4},{4,5},{5,6},{6,7},{7,0},{8,9},{9,10},{10,1... | collective-permute-start | bytes 405512 | tf_op jit(solution)/shard_map/ppermute | solution.py:345

commit v5 on v4

--- a/solution.py
+++ b/solution.py
@@ -11,11 +11,11 @@
 PLEN = 128
 LOCAL = 64
 VIS = 8
-HV = VIS // 2
 QDEV = 16
 ROWS = 8
 COLS = 32
 GROUP = QDEV * ROWS
+OWNERS = COLS * ROWS
 SLOTS = COLS * VIS
 PIECES = TOK + 1
 CELL = VIS * 2 + 1
@@ -66,7 +66,7 @@
 
 def build_kernel(*refs):
     blocks = refs[:ROWS]
-    send_ref, back_ref, buf, idx_v, idx_s, idx_sem = refs[ROWS:]
+    send_ref, pick_ref, mask_ref, buf, idx_v, idx_s, idx_sem = refs[ROWS:]
     row = lax.axis_index("qbatch").astype(i32)
     lists = [
         jnp.where(lax.rem(row + step, ROWS) == z, block[TOK].astype(f32), 0.0)
@@ -100,8 +100,20 @@
     spread = ((high >= VIS) & (low == (high >> 3) - 1)).astype(bf16)
     kept = (rows * dot_n(visit, spread)).astype(bf16)
     send_ref[:, VIS * 2] = kept.reshape(COLS, QDEV, FEAT)
-    slots = pick[:, 0:VIS, :].reshape(SLOTS, GROUP).astype(bf16)
-    back_ref[...] = dot_t(eye, slots)
+    every = (iota((GROUP, OWNERS), 1) + 1).astype(f32)
+    theirs = lists.astype(f32)
+    visited = jnp.zeros((GROUP, OWNERS), f32)
+    for v in range(VIS):
+        visited = jnp.where(theirs[:, v : v + 1] == every, 1.0, visited)
+    earlier = (iota((QDEV, GROUP), 1) < iota((QDEV, GROUP), 0) + row * QDEV).astype(bf16)
+    places = dot_n(earlier, visited.astype(bf16))
+    ours = blocks[0][TOK].astype(f32)
+    lane = iota((QDEV, FEAT), 1)
+    for v in range(VIS):
+        at = jnp.where(ours[:, v : v + 1] == every[0:QDEV], 1.0, 0.0)
+        pick_ref[v * QDEV : (v + 1) * QDEV, :] = at.astype(bf16)
+        place = jnp.sum(at * places, axis=1, keepdims=True).astype(i32)
+        mask_ref[v * QDEV : (v + 1) * QDEV, :] = jnp.where((lane >> 3) == place, 1.0, 0.0)
     for block, step in zip(blocks, STEPS):
         buf[pl.ds(lax.rem(row + step, ROWS) * PIECES, PIECES)] = block[...]
     to_scalar.wait()
@@ -228,25 +240,21 @@
     k8, l8 = iota((VIS, FEAT), 0), iota((VIS, FEAT), 1)
     repeat = ((l8 & 7) == k8).astype(f32)
     by_slot = dot_tn(scores, repeat, lax.Precision.HIGHEST)
-    mine = pltpu.roll(kept, FEAT - VIS, 1) > 0.5
-    by_slot = jnp.where(mine, by_slot, 0.0).reshape(COLS, VIS, FEAT)
-    out_ref[...] = by_slot[:, 0:HV] + pltpu.roll(by_slot[:, HV:VIS], FEAT // 2, 2)
-
-
-def return_kernel(back_ref, got_ref, out_ref):
-    got = got_ref[...]
-    lower = iota((COLS, HV, FEAT), 2) < FEAT // 2
-    first = jnp.where(lower, got, 0.0)
-    second = jnp.where(lower, pltpu.roll(got, FEAT // 2, 2), 0.0)
-    by_slot = jnp.concatenate([first, second], 1).reshape(SLOTS, FEAT)
-    mine = dot_n(back_ref[...], by_slot, lax.Precision.HIGHEST).reshape(ROWS, QDEV, FEAT)
-    out_ref[...] = mine[:, 0:8] + pltpu.roll(mine[:, 8:QDEV], FEAT // 2, 2)
-
-
-def sum_kernel(parts_ref, out_ref):
-    total = jnp.sum(parts_ref[...], axis=0)
-    out_ref[0:8] = total[:, 0 : FEAT // 2]
-    out_ref[8:QDEV] = total[:, FEAT // 2 : FEAT]
+    lane = iota((SLOTS, FEAT), 1)
+    by_slot = jnp.where((lane >> 3) == (iota((SLOTS, FEAT), 0) & 7), by_slot, 0.0)
+    by_group = jnp.sum(by_slot.reshape(COLS, VIS, FEAT), axis=1, keepdims=True)
+    out_ref[...] = jnp.broadcast_to(by_group[:, None], (COLS, ROWS, 1, FEAT))
+
+
+def return_kernel(pick_ref, mask_ref, got_ref, out_ref):
+    pick = pick_ref[...]
+    found = dot_n(jnp.concatenate([pick] * 3, 1), jnp.concatenate(split3(got_ref[...]), 0))
+    found = jnp.where(mask_ref[...] > 0.5, found, 0.0)
+    for step in (8, 16, 32, 64):
+        found = found + pltpu.roll(found, step, 1)
+    shape = (QDEV * VIS, FEAT)
+    found = jnp.where((iota(shape, 1) >> 3) == (iota(shape, 0) >> 4), found, 0.0)
+    out_ref[...] = jnp.sum(found.reshape(VIS, QDEV, FEAT), axis=0)[:, 0 : VIS * VIS]
 
 
 VM = pl.BlockSpec(memory_space=pltpu.VMEM)
@@ -279,10 +287,11 @@
         build_kernel,
         out_shape=(
             jax.ShapeDtypeStruct((COLS, CELL, 16, FEAT), bf16),
-            jax.ShapeDtypeStruct((GROUP, SLOTS), f32),
+            jax.ShapeDtypeStruct((QDEV * VIS, OWNERS), bf16),
+            jax.ShapeDtypeStruct((QDEV * VIS, FEAT), f32),
         ),
         in_specs=[VM] * ROWS,
-        out_specs=(VM, VM),
+        out_specs=(VM, VM, VM),
         scratch_shapes=[
             pltpu.VMEM((ROWS * PIECES, 16, FEAT), bf16),
             pltpu.VMEM((8, COLS * QDEV), i32),
@@ -296,7 +305,7 @@
 def score(got, passages, lengths):
     return pl.pallas_call(
         score_kernel,
-        out_shape=jax.ShapeDtypeStruct((COLS, HV, FEAT), f32),
+        out_shape=jax.ShapeDtypeStruct((COLS, ROWS, 1, FEAT), f32),
         in_specs=[VM, VM, ANY, ANY],
         out_specs=VM,
         scratch_shapes=[
@@ -311,24 +320,14 @@
     )(got.reshape(COLS * CELL, 16, FEAT), got, in_hbm(passages), in_hbm(lengths))
 
 
-def hand_back(back, got):
+def hand_back(pick, mask, got):
     return pl.pallas_call(
         return_kernel,
-        out_shape=jax.ShapeDtypeStruct((ROWS, 8, FEAT), f32),
-        in_specs=[VM, VM],
+        out_shape=jax.ShapeDtypeStruct((QDEV, VIS * VIS), f32),
+        in_specs=[VM, VM, VM],
         out_specs=VM,
         compiler_params=PARAMS,
-    )(back, got)
-
-
-def add_up(parts):
-    return pl.pallas_call(
-        sum_kernel,
-        out_shape=jax.ShapeDtypeStruct((QDEV, VIS * VIS), f32),
-        in_specs=[VM],
-        out_specs=VM,
-        compiler_params=PARAMS,
-    )(parts)
+    )(pick, mask, got)
 
 
 def shards(query_tokens, visit_owner, visit_passages, passage_tokens, passage_lengths):
@@ -349,12 +348,13 @@
             far = lax.ppermute(again, "qbatch", [(i, (i + ROWS // 2) % ROWS) for i in range(ROWS)])
         blocks += [left, right]
     blocks.append(far)
-    send, back = build(blocks)
+    send, pick, mask = build(blocks)
     got = lax.all_to_all(send, "corpus", split_axis=0, concat_axis=0, tiled=True)
     scored = score(got, passage_tokens, passage_lengths)
-    returned = lax.all_to_all(scored, "corpus", split_axis=0, concat_axis=0, tiled=True)
-    mine = hand_back(back, returned)
-    return add_up(lax.all_to_all(mine, "qbatch", split_axis=0, concat_axis=0, tiled=True))
+    returned = lax.all_to_all(
+        scored.reshape(OWNERS, 1, FEAT), ("corpus", "qbatch"), split_axis=0, concat_axis=0, tiled=True
+    )
+    return hand_back(pick, mask, returned.reshape(OWNERS, FEAT))
 
 
 def solution(mesh):

time: 103 us -> 101 us (0.981)
  blocking collectives: 64.7 us -> 59 us
  Pallas kernels: 11.1 us -> 14.1 us
    all_to_all x2 -> x1, blocking collectives: 24.6 us -> 18.8 us  [shards(): lax.all_to_all(scored.reshape(OWNERS, 1, FEAT), ('corpus', 'qbatch'), spl...]
    pallas_call x3 -> x2, Pallas kernels: 8.03 us -> 11 us  [the longest x1 9.9 us: score(): pl.pallas_call(score_kernel, out_shape=jax.ShapeDtypeStruct((COLS, ROWS,...]
where the time goes in v5:
time: 101 us
  blocking collectives  59 us (58%)
  starting transfers between devices  14.6 us (14%)
  Pallas kernels  14.1 us (14%)
  waiting for transfers between devices  12.9 us (13%)
    all_to_all x1, blocking collectives, shards(): lax.all_to_all(send, 'corpus', split_axis=0, concat_axis=0, tiled=True)  40.2 us
    all_to_all x1, blocking collectives, shards(): lax.all_to_all(scored.reshape(OWNERS, 1, FEAT), ('corpus', 'qbatch'), spl...  18.8 us
    ppermute x3, starting transfers between devices, shards(): right = lax.ppermute(right, 'qbatch', down)  13 us
    ppermute x3, waiting for transfers between devices, shards(): left = lax.ppermute(left, 'qbatch', up)  10 us
    pallas_call x1, Pallas kernels, score(): pl.pallas_call(score_kernel, out_shape=jax.ShapeDtypeStruct((COLS, ROWS,...  9.9 us
    ppermute x3, waiting for transfers between devices, shards(): right = lax.ppermute(right, 'qbatch', down)  2.89 us
    pallas_call x1, Pallas kernels, build(): pl.pallas_call(build_kernel, out_shape=(jax.ShapeDtypeStruct((COLS, CELL,...  2.1 us
  transfers between devices with their start and end apart: 7, of which 5 were waited for; matrix products, arithmetic and copies ran while one was open for 0% of the time, Pallas kernels for 0%

profile of v5, /device:TPU:1, one launch (start us, length us, event | category | flops | bytes accessed | tf_op | source)
XLA Modules:
  0.0 100.5 jit_solution(642347520468916249)
XLA Ops:
  0.0 1.0 shard_map.55.refs_0_
  1.0 6.5 %collective-permute-start.1 = (bf16[33,16,128]{2,1,0:T(8,128)(2,1)S(1)}, bf16[33,16,128]{2,1,0:T(8,128)(2,1)S(1)}, u32[]{:S(2)}, u32[]{:S(2)}) collective-permute-start(bf16[33,16,128]{2,1,0:T(8,128)(2,1)S(1)} %shard_map.55.refs_0_), channel_id=1, source_target_pairs={{0,7},{1,0},{2,1},{3,2},{4,3},{5,4},{6,5},{7,6},{8,15},{9,8},{10,9... | collective-permute-start | bytes 405512 | tf_op jit(solution)/shard_map/ppermute | solution.py:345
  7.5 0.0 collective-permute-start
  7.5 2.2 %collective-permute-done.1.refs_2_ = bf16[33,16,128]{2,1,0:T(8,128)(2,1)S(1)} collective-permute-done((bf16[33,16,128]{2,1,0:T(8,128)(2,1)S(1)}, bf16[33,16,128]{2,1,0:T(8,128)(2,1)S(1)}, u32[]{:S(2)}, u32[]{:S(2)}) %collective-permute-start.1) | collective-permute-done | bytes 135200 | tf_op jit(solution)/shard_map/ppermute | solution.py:345
  9.7 3.4 %collective-permute-start.3 = (bf16[33,16,128]{2,1,0:T(8,128)(2,1)S(1)}, bf16[33,16,128]{2,1,0:T(8,128)(2,1)S(1)}, u32[]{:S(2)}, u32[]{:S(2)}) collective-permute-start(bf16[33,16,128]{2,1,0:T(8,128)(2,1)S(1)} %collective-permute-done.1.refs_2_), channel_id=1, source_target_pairs={{0,7},{1,0},{2,1},{3,2},{4,3},{5,4},{6,5},{7,6},{8,15},{9,8},{10,9... | collective-permute-start | bytes 405512 | tf_op jit(solution)/shard_map/ppermute | solution.py:345
  13.1 0.0 collective-permute-done.refs_1_
  13.1 0.0 collective-permute-start.2
  13.1 1.6 %collective-permute-start.6 = (bf16[33,16,128]{2,1,0:T(8,128)(2,1)S(1)}, bf16[33,16,128]{2,1,0:T(8,128)(2,1)S(1)}, u32[]{:S(2)}, u32[]{:S(2)}) collective-permute-start(bf16[33,16,128]{2,1,0:T(8,128)(2,1)S(1)} %shard_map.55.refs_0_), channel_id=1, source_target_pairs={{0,4},{1,5},{2,6},{3,7},{4,0},{5,1},{6,2},{7,3},{8,12},{9,13},{10,... | collective-permute-start | bytes 405512 | tf_op jit(solution)/shard_map/ppermute | solution.py:348
  14.7 0.4 collective-permute-done.3.refs_4_
  15.1 3.1 %collective-permute-start.5 = (bf16[33,16,128]{2,1,0:T(8,128)(2,1)S(1)}, bf16[33,16,128]{2,1,0:T(8,128)(2,1)S(1)}, u32[]{:S(2)}, u32[]{:S(2)}) collective-permute-start(bf16[33,16,128]{2,1,0:T(8,128)(2,1)S(1)} %collective-permute-done.3.refs_4_), channel_id=1, source_target_pairs={{0,7},{1,0},{2,1},{3,2},{4,3},{5,4},{6,5},{7,6},{8,15},{9,8},{10,9... | collective-permute-start | bytes 405512 | tf_op jit(solution)/shard_map/ppermute | solution.py:345
  18.2 5.2 %collective-permute-done.2.refs_3_ = bf16[33,16,128]{2,1,0:T(8,128)(2,1)S(1)} collective-permute-done((bf16[33,16,128]{2,1,0:T(8,128)(2,1)S(1)}, bf16[33,16,128]{2,1,0:T(8,128)(2,1)S(1)}, u32[]{:S(2)}, u32[]{:S(2)}) %collective-permute-start.2) | collective-permute-done | bytes 135200 | tf_op jit(solution)/shard_map/ppermute | solution.py:344
  23.4 0.0 collective-permute-start.4
  23.4 0.0 collective-permute-done.6.refs_7_
  23.4 0.2 collective-permute-done.5.refs_6_
  23.6 4.8 %collective-permute-done.4.refs_5_ = bf16[33,16,128]{2,1,0:T(8,128)(2,1)S(1)} collective-permute-done((bf16[33,16,128]{2,1,0:T(8,128)(2,1)S(1)}, bf16[33,16,128]{2,1,0:T(8,128)(2,1)S(1)}, u32[]{:S(2)}, u32[]{:S(2)}) %collective-permute-start.4) | collective-permute-done | bytes 135200 | tf_op jit(solution)/shard_map/ppermute | solution.py:344
  28.5 2.1 %shard_map.56 = (bf16[32,17,16,128]{3,2,1,0:T(8,128)(2,1)S(1)}, bf16[128,256]{1,0:T(8,128)(2,1)S(1)}, f32[128,128]{1,0:T(8,128)S(1)}) custom-call(bf16[33,16,128]{2,1,0:T(8,128)(2,1)S(1)} %shard_map.55.refs_0_, bf16[33,16,128]{2,1,0:T(8,128)(2,1)S(1)} %collective-permute-done.refs_1_, bf16[33,16,128]{2,1,0:T(8,128)(2,1)S(1)} %collective-permute-done.1.refs_2_, ...), custom_call_target="tpu_custom_call" | custom-call | tf_op jit(solution)/shard_map/pallas_call | solution.py:286
  30.6 40.2 %all_to_all.10.cells_ref = bf16[32,17,16,128]{3,2,1,0:T(8,128)(2,1)S(1)} all-to-all(bf16[32,17,16,128]{3,2,1,0:T(8,128)(2,1)S(1)} %get-tuple-element.14), channel_id=1, replica_groups=mesh['corpus'=32,'qbatch'=8] {'corpus'}, dimensions={0} | all-to-all | bytes 4456448 | tf_op jit(solution)/shard_map/all_to_all | solution.py:352
  70.7 9.9 %shard_map.57 = f32[32,8,1,128]{3,2,1,0:T(1,128)S(1)} custom-call(bf16[544,16,128]{2,1,0:T(8,128)(2,1)S(1)} %bitcast.10, bf16[32,17,16,128]{3,2,1,0:T(8,128)(2,1)S(1)} %all_to_all.10.cells_ref, bf16[64,128,128]{2,1,0:T(8,128)(2,1)} %passage_ref.1, s32[64]{0:T(128)} %length_ref.1), custom_call_target="tpu_custom_call" | custom-call | tf_op jit(solution)/shard_map/pallas_call | solution.py:306
  80.6 18.8 %all_to_all.11 = f32[256,1,128]{2,1,0:T(1,128)S(1)} all-to-all(f32[256,1,128]{2,1,0:T(1,128)S(1)} %bitcast.11), channel_id=1, replica_groups=mesh['corpus'=32,'qbatch'=8] {'corpus','qbatch'}, dimensions={0} | all-to-all | bytes 262144 | tf_op jit(solution)/shard_map/all_to_all | solution.py:354
  99.5 1.1 %shard_map.58 = f32[16,64]{1,0:T(8,128)} custom-call(bf16[128,256]{1,0:T(8,128)(2,1)S(1)} %get-tuple-element.12.pick_ref, f32[128,128]{1,0:T(8,128)S(1)} %get-tuple-element.13.mask_ref, f32[256,128]{1,0:T(8,128)S(1)} %bitcast.12), custom_call_target="tpu_custom_call" | custom-call | tf_op jit(solution)/shard_map/pallas_call | solution.py:324
Async XLA Ops:
  1.0 8.7 %collective-permute-start.1 = (bf16[33,16,128]{2,1,0:T(8,128)(2,1)S(1)}, bf16[33,16,128]{2,1,0:T(8,128)(2,1)S(1)}, u32[]{:S(2)}, u32[]{:S(2)}) collective-permute-start(bf16[33,16,128]{2,1,0:T(8,128)(2,1)S(1)} %shard_map.55.refs_0_), channel_id=1, source_target_pairs={{0,7},{1,0},{2,1},{3,2},{4,3},{5,4},{6,5},{7,6},{8,15},{9,8},{10,9... | collective-permute-start | bytes 405512 | tf_op jit(solution)/shard_map/ppermute | solution.py:345
  7.5 5.7 %collective-permute-start = (bf16[33,16,128]{2,1,0:T(8,128)(2,1)S(1)}, bf16[33,16,128]{2,1,0:T(8,128)(2,1)S(1)}, u32[]{:S(2)}, u32[]{:S(2)}) collective-permute-start(bf16[33,16,128]{2,1,0:T(8,128)(2,1)S(1)} %shard_map.55.refs_0_), channel_id=1, source_target_pairs={{0,1},{1,2},{2,3},{3,4},{4,5},{5,6},{6,7},{7,0},{8,9},{9,10},{10,1... | collective-permute-start | bytes 405512 | tf_op jit(solution)/shard_map/ppermute | solution.py:344
  9.7 5.4 %collective-permute-start.3 = (bf16[33,16,128]{2,1,0:T(8,128)(2,1)S(1)}, bf16[33,16,128]{2,1,0:T(8,128)(2,1)S(1)}, u32[]{:S(2)}, u32[]{:S(2)}) collective-permute-start(bf16[33,16,128]{2,1,0:T(8,128)(2,1)S(1)} %collective-permute-done.1.refs_2_), channel_id=1, source_target_pairs={{0,7},{1,0},{2,1},{3,2},{4,3},{5,4},{6,5},{7,6},{8,15},{9,8},{10,9... | collective-permute-start | bytes 405512 | tf_op jit(solution)/shard_map/ppermute | solution.py:345
  13.1 10.3 %collective-permute-start.2 = (bf16[33,16,128]{2,1,0:T(8,128)(2,1)S(1)}, bf16[33,16,128]{2,1,0:T(8,128)(2,1)S(1)}, u32[]{:S(2)}, u32[]{:S(2)}) collective-permute-start(bf16[33,16,128]{2,1,0:T(8,128)(2,1)S(1)} %collective-permute-done.refs_1_), channel_id=1, source_target_pairs={{0,1},{1,2},{2,3},{3,4},{4,5},{5,6},{6,7},{7,0},{8,9},{9,10},{10,1... | collective-permute-start | bytes 405512 | tf_op jit(solution)/shard_map/ppermute | solution.py:344
  13.1 10.3 %collective-permute-start.6 = (bf16[33,16,128]{2,1,0:T(8,128)(2,1)S(1)}, bf16[33,16,128]{2,1,0:T(8,128)(2,1)S(1)}, u32[]{:S(2)}, u32[]{:S(2)}) collective-permute-start(bf16[33,16,128]{2,1,0:T(8,128)(2,1)S(1)} %shard_map.55.refs_0_), channel_id=1, source_target_pairs={{0,4},{1,5},{2,6},{3,7},{4,0},{5,1},{6,2},{7,3},{8,12},{9,13},{10,... | collective-permute-start | bytes 405512 | tf_op jit(solution)/shard_map/ppermute | solution.py:348
  15.1 8.5 %collective-permute-start.5 = (bf16[33,16,128]{2,1,0:T(8,128)(2,1)S(1)}, bf16[33,16,128]{2,1,0:T(8,128)(2,1)S(1)}, u32[]{:S(2)}, u32[]{:S(2)}) collective-permute-start(bf16[33,16,128]{2,1,0:T(8,128)(2,1)S(1)} %collective-permute-done.3.refs_4_), channel_id=1, source_target_pairs={{0,7},{1,0},{2,1},{3,2},{4,3},{5,4},{6,5},{7,6},{8,15},{9,8},{10,9... | collective-permute-start | bytes 405512 | tf_op jit(solution)/shard_map/ppermute | solution.py:345
  23.4 5.1 %collective-permute-start.4 = (bf16[33,16,128]{2,1,0:T(8,128)(2,1)S(1)}, bf16[33,16,128]{2,1,0:T(8,128)(2,1)S(1)}, u32[]{:S(2)}, u32[]{:S(2)}) collective-permute-start(bf16[33,16,128]{2,1,0:T(8,128)(2,1)S(1)} %collective-permute-done.2.refs_3_), channel_id=1, source_target_pairs={{0,1},{1,2},{2,3},{3,4},{4,5},{5,6},{6,7},{7,0},{8,9},{9,10},{10,1... | collective-permute-start | bytes 405512 | tf_op jit(solution)/shard_map/ppermute | solution.py:344

commit v6 on v5

--- a/solution.py
+++ b/solution.py
@@ -21,7 +21,7 @@
 CELL = VIS * 2 + 1
 TILE = 8
 TILES = 384
-UNROLL = 72
+UNROLL = 96
 VMEM_LIMIT = 16 * 1024 * 1024
 
 
@@ -134,7 +134,7 @@
 
 
 def score_kernel(
-    got, cells_ref, passage_ref, length_ref, out_ref, held, lengths, plan_v, plan_s, best, sems
+    got, cells_ref, passage_ref, length_ref, out_ref, held, lengths, plan_v, plan_s, best, moves_v, sems
 ):
     load = pltpu.make_async_copy(passage_ref, held, sems.at[0])
     load.start()
@@ -197,6 +197,11 @@
     first = first_wide[:, 0:1]
     t = iota((LOCAL, TILES), 1)
     owned = jnp.where((first <= t) & (t < first + tiles), 1.0, 0.0).astype(bf16)
+    x = x >> 9
+    for b in (7, 6, 5, 4, 3, 2, 1, 0):
+        moves = ((x >> b) & 1) == 1
+        moves_v[b] = jnp.where(moves, 1.0, 0.0)
+        x = jnp.where(moves, 0, x) + pltpu.roll(jnp.where(moves, x, 0), 1 << b, 1)
     to_scalar.wait()
     load_lengths.wait()
     load.wait()
@@ -225,11 +230,9 @@
     sums = jnp.where(here, jnp.concatenate([sums, sums], 1), 0.0)
     y = dot_n(jnp.concatenate([owned] * 3, 1), jnp.concatenate(split3(sums), 0))
     y = jnp.where(slot < count, y, 0.0)
-    x = x >> 9
     for b in (7, 6, 5, 4, 3, 2, 1, 0):
-        moves = ((x >> b) & 1) == 1
-        y = jnp.where(moves, 0.0, y) + pltpu.roll(jnp.where(moves, y, 0.0), 1 << b, 1)
-        x = jnp.where(moves, 0, x) + pltpu.roll(jnp.where(moves, x, 0), 1 << b, 1)
+        moved = y * moves_v[b]
+        y = (y - moved) + pltpu.roll(moved, 1 << b, 1)
     scores = jnp.concatenate(
         [
             jnp.sum(jnp.where(cands[k : k + 1, :] == passage, y, 0.0), axis=0, keepdims=True)
@@ -314,6 +317,7 @@
             pltpu.VMEM((16, TILES), i32),
             pltpu.SMEM((16, TILES), i32),
             pltpu.VMEM((TILES, SLOTS), f32),
+            pltpu.VMEM((8, LOCAL, SLOTS), f32),
             pltpu.SemaphoreType.DMA((3,)),
         ],
         compiler_params=PARAMS,

time: 101 us -> 100 us (0.990)
  Pallas kernels: 14.1 us -> 12 us
    pallas_call x1, Pallas kernels: 9.9 us -> 7.83 us  [score(): pl.pallas_call(score_kernel, out_shape=jax.ShapeDtypeStruct((COLS, ROWS,...]
where the time goes in v6:
time: 100 us; the launch traced here: 99.4 us
  blocking collectives  59.9 us (60%)
  starting transfers between devices  14.6 us (15%)
  waiting for transfers between devices  12.9 us (13%)
  Pallas kernels  12 us (12%)
    all_to_all x1, blocking collectives, shards(): lax.all_to_all(send, 'corpus', split_axis=0, concat_axis=0, tiled=True)  40.2 us
    all_to_all x1, blocking collectives, shards(): lax.all_to_all(scored.reshape(OWNERS, 1, FEAT), ('corpus', 'qbatch'), spl...  19.7 us
    ppermute x3, starting transfers between devices, shards(): right = lax.ppermute(right, 'qbatch', down)  13 us
    ppermute x3, waiting for transfers between devices, shards(): left = lax.ppermute(left, 'qbatch', up)  10 us
    pallas_call x1, Pallas kernels, score(): pl.pallas_call(score_kernel, out_shape=jax.ShapeDtypeStruct((COLS, ROWS,...  7.83 us
    ppermute x3, waiting for transfers between devices, shards(): right = lax.ppermute(right, 'qbatch', down)  2.89 us
    pallas_call x1, Pallas kernels, build(): pl.pallas_call(build_kernel, out_shape=(jax.ShapeDtypeStruct((COLS, CELL,...  2.1 us
  transfers between devices with their start and end apart: 7, of which 5 were waited for; matrix products, arithmetic and copies ran while one was open for 0% of the time, Pallas kernels for 0%

profile of v6, /device:TPU:1, one launch (start us, length us, event | category | flops | bytes accessed | tf_op | source)
XLA Modules:
  0.0 99.4 jit_solution(11636230561266421052)
XLA Ops:
  0.0 1.0 shard_map.55.refs_0_
  1.0 6.5 %collective-permute-start.1 = (bf16[33,16,128]{2,1,0:T(8,128)(2,1)S(1)}, bf16[33,16,128]{2,1,0:T(8,128)(2,1)S(1)}, u32[]{:S(2)}, u32[]{:S(2)}) collective-permute-start(bf16[33,16,128]{2,1,0:T(8,128)(2,1)S(1)} %shard_map.55.refs_0_), channel_id=1, source_target_pairs={{0,7},{1,0},{2,1},{3,2},{4,3},{5,4},{6,5},{7,6},{8,15},{9,8},{10,9... | collective-permute-start | bytes 405512 | tf_op jit(solution)/shard_map/ppermute | solution.py:349
  7.5 0.0 collective-permute-start
  7.5 2.2 %collective-permute-done.1.refs_2_ = bf16[33,16,128]{2,1,0:T(8,128)(2,1)S(1)} collective-permute-done((bf16[33,16,128]{2,1,0:T(8,128)(2,1)S(1)}, bf16[33,16,128]{2,1,0:T(8,128)(2,1)S(1)}, u32[]{:S(2)}, u32[]{:S(2)}) %collective-permute-start.1) | collective-permute-done | bytes 135200 | tf_op jit(solution)/shard_map/ppermute | solution.py:349
  9.7 3.4 %collective-permute-start.3 = (bf16[33,16,128]{2,1,0:T(8,128)(2,1)S(1)}, bf16[33,16,128]{2,1,0:T(8,128)(2,1)S(1)}, u32[]{:S(2)}, u32[]{:S(2)}) collective-permute-start(bf16[33,16,128]{2,1,0:T(8,128)(2,1)S(1)} %collective-permute-done.1.refs_2_), channel_id=1, source_target_pairs={{0,7},{1,0},{2,1},{3,2},{4,3},{5,4},{6,5},{7,6},{8,15},{9,8},{10,9... | collective-permute-start | bytes 405512 | tf_op jit(solution)/shard_map/ppermute | solution.py:349
  13.1 0.0 collective-permute-done.refs_1_
  13.1 0.0 collective-permute-start.2
  13.1 1.6 %collective-permute-start.6 = (bf16[33,16,128]{2,1,0:T(8,128)(2,1)S(1)}, bf16[33,16,128]{2,1,0:T(8,128)(2,1)S(1)}, u32[]{:S(2)}, u32[]{:S(2)}) collective-permute-start(bf16[33,16,128]{2,1,0:T(8,128)(2,1)S(1)} %shard_map.55.refs_0_), channel_id=1, source_target_pairs={{0,4},{1,5},{2,6},{3,7},{4,0},{5,1},{6,2},{7,3},{8,12},{9,13},{10,... | collective-permute-start | bytes 405512 | tf_op jit(solution)/shard_map/ppermute | solution.py:352
  14.7 0.4 collective-permute-done.3.refs_4_
  15.1 3.1 %collective-permute-start.5 = (bf16[33,16,128]{2,1,0:T(8,128)(2,1)S(1)}, bf16[33,16,128]{2,1,0:T(8,128)(2,1)S(1)}, u32[]{:S(2)}, u32[]{:S(2)}) collective-permute-start(bf16[33,16,128]{2,1,0:T(8,128)(2,1)S(1)} %collective-permute-done.3.refs_4_), channel_id=1, source_target_pairs={{0,7},{1,0},{2,1},{3,2},{4,3},{5,4},{6,5},{7,6},{8,15},{9,8},{10,9... | collective-permute-start | bytes 405512 | tf_op jit(solution)/shard_map/ppermute | solution.py:349
  18.2 5.2 %collective-permute-done.2.refs_3_ = bf16[33,16,128]{2,1,0:T(8,128)(2,1)S(1)} collective-permute-done((bf16[33,16,128]{2,1,0:T(8,128)(2,1)S(1)}, bf16[33,16,128]{2,1,0:T(8,128)(2,1)S(1)}, u32[]{:S(2)}, u32[]{:S(2)}) %collective-permute-start.2) | collective-permute-done | bytes 135200 | tf_op jit(solution)/shard_map/ppermute | solution.py:348
  23.4 0.0 collective-permute-start.4
  23.4 0.0 collective-permute-done.6.refs_7_
  23.4 0.2 collective-permute-done.5.refs_6_
  23.6 4.8 %collective-permute-done.4.refs_5_ = bf16[33,16,128]{2,1,0:T(8,128)(2,1)S(1)} collective-permute-done((bf16[33,16,128]{2,1,0:T(8,128)(2,1)S(1)}, bf16[33,16,128]{2,1,0:T(8,128)(2,1)S(1)}, u32[]{:S(2)}, u32[]{:S(2)}) %collective-permute-start.4) | collective-permute-done | bytes 135200 | tf_op jit(solution)/shard_map/ppermute | solution.py:348
  28.5 2.1 %shard_map.56 = (bf16[32,17,16,128]{3,2,1,0:T(8,128)(2,1)S(1)}, bf16[128,256]{1,0:T(8,128)(2,1)S(1)}, f32[128,128]{1,0:T(8,128)S(1)}) custom-call(bf16[33,16,128]{2,1,0:T(8,128)(2,1)S(1)} %shard_map.55.refs_0_, bf16[33,16,128]{2,1,0:T(8,128)(2,1)S(1)} %collective-permute-done.refs_1_, bf16[33,16,128]{2,1,0:T(8,128)(2,1)S(1)} %collective-permute-done.1.refs_2_, ...), custom_call_target="tpu_custom_call" | custom-call | tf_op jit(solution)/shard_map/pallas_call | solution.py:289
  30.6 40.2 %all_to_all.10.cells_ref = bf16[32,17,16,128]{3,2,1,0:T(8,128)(2,1)S(1)} all-to-all(bf16[32,17,16,128]{3,2,1,0:T(8,128)(2,1)S(1)} %get-tuple-element.14), channel_id=1, replica_groups=mesh['corpus'=32,'qbatch'=8] {'corpus'}, dimensions={0} | all-to-all | bytes 4456448 | tf_op jit(solution)/shard_map/all_to_all | solution.py:356
  70.7 7.8 %shard_map.57 = f32[32,8,1,128]{3,2,1,0:T(1,128)S(1)} custom-call(bf16[544,16,128]{2,1,0:T(8,128)(2,1)S(1)} %bitcast.10, bf16[32,17,16,128]{3,2,1,0:T(8,128)(2,1)S(1)} %all_to_all.10.cells_ref, bf16[64,128,128]{2,1,0:T(8,128)(2,1)} %passage_ref.1, s32[64]{0:T(128)} %length_ref.1), custom_call_target="tpu_custom_call" | custom-call | tf_op jit(solution)/shard_map/pallas_call | solution.py:309
  78.6 19.7 %all_to_all.11 = f32[256,1,128]{2,1,0:T(1,128)S(1)} all-to-all(f32[256,1,128]{2,1,0:T(1,128)S(1)} %bitcast.11), channel_id=1, replica_groups=mesh['corpus'=32,'qbatch'=8] {'corpus','qbatch'}, dimensions={0} | all-to-all | bytes 262144 | tf_op jit(solution)/shard_map/all_to_all | solution.py:358
  98.3 1.1 %shard_map.58 = f32[16,64]{1,0:T(8,128)} custom-call(bf16[128,256]{1,0:T(8,128)(2,1)S(1)} %get-tuple-element.12.pick_ref, f32[128,128]{1,0:T(8,128)S(1)} %get-tuple-element.13.mask_ref, f32[256,128]{1,0:T(8,128)S(1)} %bitcast.12), custom_call_target="tpu_custom_call" | custom-call | tf_op jit(solution)/shard_map/pallas_call | solution.py:328
Async XLA Ops:
  1.0 8.7 %collective-permute-start.1 = (bf16[33,16,128]{2,1,0:T(8,128)(2,1)S(1)}, bf16[33,16,128]{2,1,0:T(8,128)(2,1)S(1)}, u32[]{:S(2)}, u32[]{:S(2)}) collective-permute-start(bf16[33,16,128]{2,1,0:T(8,128)(2,1)S(1)} %shard_map.55.refs_0_), channel_id=1, source_target_pairs={{0,7},{1,0},{2,1},{3,2},{4,3},{5,4},{6,5},{7,6},{8,15},{9,8},{10,9... | collective-permute-start | bytes 405512 | tf_op jit(solution)/shard_map/ppermute | solution.py:349
  7.5 5.7 %collective-permute-start = (bf16[33,16,128]{2,1,0:T(8,128)(2,1)S(1)}, bf16[33,16,128]{2,1,0:T(8,128)(2,1)S(1)}, u32[]{:S(2)}, u32[]{:S(2)}) collective-permute-start(bf16[33,16,128]{2,1,0:T(8,128)(2,1)S(1)} %shard_map.55.refs_0_), channel_id=1, source_target_pairs={{0,1},{1,2},{2,3},{3,4},{4,5},{5,6},{6,7},{7,0},{8,9},{9,10},{10,1... | collective-permute-start | bytes 405512 | tf_op jit(solution)/shard_map/ppermute | solution.py:348
  9.7 5.4 %collective-permute-start.3 = (bf16[33,16,128]{2,1,0:T(8,128)(2,1)S(1)}, bf16[33,16,128]{2,1,0:T(8,128)(2,1)S(1)}, u32[]{:S(2)}, u32[]{:S(2)}) collective-permute-start(bf16[33,16,128]{2,1,0:T(8,128)(2,1)S(1)} %collective-permute-done.1.refs_2_), channel_id=1, source_target_pairs={{0,7},{1,0},{2,1},{3,2},{4,3},{5,4},{6,5},{7,6},{8,15},{9,8},{10,9... | collective-permute-start | bytes 405512 | tf_op jit(solution)/shard_map/ppermute | solution.py:349
  13.1 10.3 %collective-permute-start.2 = (bf16[33,16,128]{2,1,0:T(8,128)(2,1)S(1)}, bf16[33,16,128]{2,1,0:T(8,128)(2,1)S(1)}, u32[]{:S(2)}, u32[]{:S(2)}) collective-permute-start(bf16[33,16,128]{2,1,0:T(8,128)(2,1)S(1)} %collective-permute-done.refs_1_), channel_id=1, source_target_pairs={{0,1},{1,2},{2,3},{3,4},{4,5},{5,6},{6,7},{7,0},{8,9},{9,10},{10,1... | collective-permute-start | bytes 405512 | tf_op jit(solution)/shard_map/ppermute | solution.py:348
  13.1 10.3 %collective-permute-start.6 = (bf16[33,16,128]{2,1,0:T(8,128)(2,1)S(1)}, bf16[33,16,128]{2,1,0:T(8,128)(2,1)S(1)}, u32[]{:S(2)}, u32[]{:S(2)}) collective-permute-start(bf16[33,16,128]{2,1,0:T(8,128)(2,1)S(1)} %shard_map.55.refs_0_), channel_id=1, source_target_pairs={{0,4},{1,5},{2,6},{3,7},{4,0},{5,1},{6,2},{7,3},{8,12},{9,13},{10,... | collective-permute-start | bytes 405512 | tf_op jit(solution)/shard_map/ppermute | solution.py:352
  15.1 8.5 %collective-permute-start.5 = (bf16[33,16,128]{2,1,0:T(8,128)(2,1)S(1)}, bf16[33,16,128]{2,1,0:T(8,128)(2,1)S(1)}, u32[]{:S(2)}, u32[]{:S(2)}) collective-permute-start(bf16[33,16,128]{2,1,0:T(8,128)(2,1)S(1)} %collective-permute-done.3.refs_4_), channel_id=1, source_target_pairs={{0,7},{1,0},{2,1},{3,2},{4,3},{5,4},{6,5},{7,6},{8,15},{9,8},{10,9... | collective-permute-start | bytes 405512 | tf_op jit(solution)/shard_map/ppermute | solution.py:349
  23.4 5.1 %collective-permute-start.4 = (bf16[33,16,128]{2,1,0:T(8,128)(2,1)S(1)}, bf16[33,16,128]{2,1,0:T(8,128)(2,1)S(1)}, u32[]{:S(2)}, u32[]{:S(2)}) collective-permute-start(bf16[33,16,128]{2,1,0:T(8,128)(2,1)S(1)} %collective-permute-done.2.refs_3_), channel_id=1, source_target_pairs={{0,1},{1,2},{2,3},{3,4},{4,5},{5,6},{6,7},{7,0},{8,9},{9,10},{10,1... | collective-permute-start | bytes 405512 | tf_op jit(solution)/shard_map/ppermute | solution.py:348

commit v7 on v6

--- a/solution.py
+++ b/solution.py
@@ -21,7 +21,7 @@
 CELL = VIS * 2 + 1
 TILE = 8
 TILES = 384
-UNROLL = 96
+UNROLL = 72
 VMEM_LIMIT = 16 * 1024 * 1024
 
 

time: 100 us -> 101 us (1.010)
  blocking collectives: 59.9 us -> 61.7 us
    all_to_all x1, blocking collectives: 19.7 us -> 21.6 us  [shards(): lax.all_to_all(scored.reshape(OWNERS, 1, FEAT), ('corpus', 'qbatch'), spl...]
where the time goes in v7:
time: 101 us; the launch traced here: 100 us
  blocking collectives  61.7 us (61%)
  starting transfers between devices  14.6 us (14%)
  waiting for transfers between devices  12.9 us (13%)
  Pallas kernels  11.1 us (11%)
    all_to_all x1, blocking collectives, shards(): lax.all_to_all(send, 'corpus', split_axis=0, concat_axis=0, tiled=True)  40.2 us
    all_to_all x1, blocking collectives, shards(): lax.all_to_all(scored.reshape(OWNERS, 1, FEAT), ('corpus', 'qbatch'), spl...  21.6 us
    ppermute x3, starting transfers between devices, shards(): right = lax.ppermute(right, 'qbatch', down)  13 us
    ppermute x3, waiting for transfers between devices, shards(): left = lax.ppermute(left, 'qbatch', up)  10 us
    pallas_call x1, Pallas kernels, score(): pl.pallas_call(score_kernel, out_shape=jax.ShapeDtypeStruct((COLS, ROWS,...  6.95 us
    ppermute x3, waiting for transfers between devices, shards(): right = lax.ppermute(right, 'qbatch', down)  2.89 us
    pallas_call x1, Pallas kernels, build(): pl.pallas_call(build_kernel, out_shape=(jax.ShapeDtypeStruct((COLS, CELL,...  2.1 us
  transfers between devices with their start and end apart: 7, of which 5 were waited for; matrix products, arithmetic and copies ran while one was open for 0% of the time, Pallas kernels for 0%

profile of v7, /device:TPU:1, one launch (start us, length us, event | category | flops | bytes accessed | tf_op | source)
XLA Modules:
  0.0 100.3 jit_solution(4029468340123817115)
XLA Ops:
  0.0 1.0 shard_map.55.refs_0_
  1.0 6.5 %collective-permute-start.1 = (bf16[33,16,128]{2,1,0:T(8,128)(2,1)S(1)}, bf16[33,16,128]{2,1,0:T(8,128)(2,1)S(1)}, u32[]{:S(2)}, u32[]{:S(2)}) collective-permute-start(bf16[33,16,128]{2,1,0:T(8,128)(2,1)S(1)} %shard_map.55.refs_0_), channel_id=1, source_target_pairs={{0,7},{1,0},{2,1},{3,2},{4,3},{5,4},{6,5},{7,6},{8,15},{9,8},{10,9... | collective-permute-start | bytes 405512 | tf_op jit(solution)/shard_map/ppermute | solution.py:349
  7.5 0.0 collective-permute-start
  7.5 2.2 %collective-permute-done.1.refs_2_ = bf16[33,16,128]{2,1,0:T(8,128)(2,1)S(1)} collective-permute-done((bf16[33,16,128]{2,1,0:T(8,128)(2,1)S(1)}, bf16[33,16,128]{2,1,0:T(8,128)(2,1)S(1)}, u32[]{:S(2)}, u32[]{:S(2)}) %collective-permute-start.1) | collective-permute-done | bytes 135200 | tf_op jit(solution)/shard_map/ppermute | solution.py:349
  9.7 3.4 %collective-permute-start.3 = (bf16[33,16,128]{2,1,0:T(8,128)(2,1)S(1)}, bf16[33,16,128]{2,1,0:T(8,128)(2,1)S(1)}, u32[]{:S(2)}, u32[]{:S(2)}) collective-permute-start(bf16[33,16,128]{2,1,0:T(8,128)(2,1)S(1)} %collective-permute-done.1.refs_2_), channel_id=1, source_target_pairs={{0,7},{1,0},{2,1},{3,2},{4,3},{5,4},{6,5},{7,6},{8,15},{9,8},{10,9... | collective-permute-start | bytes 405512 | tf_op jit(solution)/shard_map/ppermute | solution.py:349
  13.1 0.0 collective-permute-done.refs_1_
  13.1 0.0 collective-permute-start.2
  13.1 1.6 %collective-permute-start.6 = (bf16[33,16,128]{2,1,0:T(8,128)(2,1)S(1)}, bf16[33,16,128]{2,1,0:T(8,128)(2,1)S(1)}, u32[]{:S(2)}, u32[]{:S(2)}) collective-permute-start(bf16[33,16,128]{2,1,0:T(8,128)(2,1)S(1)} %shard_map.55.refs_0_), channel_id=1, source_target_pairs={{0,4},{1,5},{2,6},{3,7},{4,0},{5,1},{6,2},{7,3},{8,12},{9,13},{10,... | collective-permute-start | bytes 405512 | tf_op jit(solution)/shard_map/ppermute | solution.py:352
  14.7 0.4 collective-permute-done.3.refs_4_
  15.1 3.1 %collective-permute-start.5 = (bf16[33,16,128]{2,1,0:T(8,128)(2,1)S(1)}, bf16[33,16,128]{2,1,0:T(8,128)(2,1)S(1)}, u32[]{:S(2)}, u32[]{:S(2)}) collective-permute-start(bf16[33,16,128]{2,1,0:T(8,128)(2,1)S(1)} %collective-permute-done.3.refs_4_), channel_id=1, source_target_pairs={{0,7},{1,0},{2,1},{3,2},{4,3},{5,4},{6,5},{7,6},{8,15},{9,8},{10,9... | collective-permute-start | bytes 405512 | tf_op jit(solution)/shard_map/ppermute | solution.py:349
  18.2 5.2 %collective-permute-done.2.refs_3_ = bf16[33,16,128]{2,1,0:T(8,128)(2,1)S(1)} collective-permute-done((bf16[33,16,128]{2,1,0:T(8,128)(2,1)S(1)}, bf16[33,16,128]{2,1,0:T(8,128)(2,1)S(1)}, u32[]{:S(2)}, u32[]{:S(2)}) %collective-permute-start.2) | collective-permute-done | bytes 135200 | tf_op jit(solution)/shard_map/ppermute | solution.py:348
  23.4 0.0 collective-permute-start.4
  23.4 0.0 collective-permute-done.6.refs_7_
  23.4 0.2 collective-permute-done.5.refs_6_
  23.6 4.8 %collective-permute-done.4.refs_5_ = bf16[33,16,128]{2,1,0:T(8,128)(2,1)S(1)} collective-permute-done((bf16[33,16,128]{2,1,0:T(8,128)(2,1)S(1)}, bf16[33,16,128]{2,1,0:T(8,128)(2,1)S(1)}, u32[]{:S(2)}, u32[]{:S(2)}) %collective-permute-start.4) | collective-permute-done | bytes 135200 | tf_op jit(solution)/shard_map/ppermute | solution.py:348
  28.5 2.1 %shard_map.56 = (bf16[32,17,16,128]{3,2,1,0:T(8,128)(2,1)S(1)}, bf16[128,256]{1,0:T(8,128)(2,1)S(1)}, f32[128,128]{1,0:T(8,128)S(1)}) custom-call(bf16[33,16,128]{2,1,0:T(8,128)(2,1)S(1)} %shard_map.55.refs_0_, bf16[33,16,128]{2,1,0:T(8,128)(2,1)S(1)} %collective-permute-done.refs_1_, bf16[33,16,128]{2,1,0:T(8,128)(2,1)S(1)} %collective-permute-done.1.refs_2_, ...), custom_call_target="tpu_custom_call" | custom-call | tf_op jit(solution)/shard_map/pallas_call | solution.py:289
  30.6 40.2 %all_to_all.10.cells_ref = bf16[32,17,16,128]{3,2,1,0:T(8,128)(2,1)S(1)} all-to-all(bf16[32,17,16,128]{3,2,1,0:T(8,128)(2,1)S(1)} %get-tuple-element.14), channel_id=1, replica_groups=mesh['corpus'=32,'qbatch'=8] {'corpus'}, dimensions={0} | all-to-all | bytes 4456448 | tf_op jit(solution)/shard_map/all_to_all | solution.py:356
  70.7 6.9 %shard_map.57 = f32[32,8,1,128]{3,2,1,0:T(1,128)S(1)} custom-call(bf16[544,16,128]{2,1,0:T(8,128)(2,1)S(1)} %bitcast.10, bf16[32,17,16,128]{3,2,1,0:T(8,128)(2,1)S(1)} %all_to_all.10.cells_ref, bf16[64,128,128]{2,1,0:T(8,128)(2,1)} %passage_ref.1, s32[64]{0:T(128)} %length_ref.1), custom_call_target="tpu_custom_call" | custom-call | tf_op jit(solution)/shard_map/pallas_call | solution.py:309
  77.7 21.6 %all_to_all.11 = f32[256,1,128]{2,1,0:T(1,128)S(1)} all-to-all(f32[256,1,128]{2,1,0:T(1,128)S(1)} %bitcast.11), channel_id=1, replica_groups=mesh['corpus'=32,'qbatch'=8] {'corpus','qbatch'}, dimensions={0} | all-to-all | bytes 262144 | tf_op jit(solution)/shard_map/all_to_all | solution.py:358
  99.2 1.1 %shard_map.58 = f32[16,64]{1,0:T(8,128)} custom-call(bf16[128,256]{1,0:T(8,128)(2,1)S(1)} %get-tuple-element.12.pick_ref, f32[128,128]{1,0:T(8,128)S(1)} %get-tuple-element.13.mask_ref, f32[256,128]{1,0:T(8,128)S(1)} %bitcast.12), custom_call_target="tpu_custom_call" | custom-call | tf_op jit(solution)/shard_map/pallas_call | solution.py:328
Async XLA Ops:
  1.0 8.7 %collective-permute-start.1 = (bf16[33,16,128]{2,1,0:T(8,128)(2,1)S(1)}, bf16[33,16,128]{2,1,0:T(8,128)(2,1)S(1)}, u32[]{:S(2)}, u32[]{:S(2)}) collective-permute-start(bf16[33,16,128]{2,1,0:T(8,128)(2,1)S(1)} %shard_map.55.refs_0_), channel_id=1, source_target_pairs={{0,7},{1,0},{2,1},{3,2},{4,3},{5,4},{6,5},{7,6},{8,15},{9,8},{10,9... | collective-permute-start | bytes 405512 | tf_op jit(solution)/shard_map/ppermute | solution.py:349
  7.5 5.7 %collective-permute-start = (bf16[33,16,128]{2,1,0:T(8,128)(2,1)S(1)}, bf16[33,16,128]{2,1,0:T(8,128)(2,1)S(1)}, u32[]{:S(2)}, u32[]{:S(2)}) collective-permute-start(bf16[33,16,128]{2,1,0:T(8,128)(2,1)S(1)} %shard_map.55.refs_0_), channel_id=1, source_target_pairs={{0,1},{1,2},{2,3},{3,4},{4,5},{5,6},{6,7},{7,0},{8,9},{9,10},{10,1... | collective-permute-start | bytes 405512 | tf_op jit(solution)/shard_map/ppermute | solution.py:348
  9.7 5.4 %collective-permute-start.3 = (bf16[33,16,128]{2,1,0:T(8,128)(2,1)S(1)}, bf16[33,16,128]{2,1,0:T(8,128)(2,1)S(1)}, u32[]{:S(2)}, u32[]{:S(2)}) collective-permute-start(bf16[33,16,128]{2,1,0:T(8,128)(2,1)S(1)} %collective-permute-done.1.refs_2_), channel_id=1, source_target_pairs={{0,7},{1,0},{2,1},{3,2},{4,3},{5,4},{6,5},{7,6},{8,15},{9,8},{10,9... | collective-permute-start | bytes 405512 | tf_op jit(solution)/shard_map/ppermute | solution.py:349
  13.1 10.3 %collective-permute-start.2 = (bf16[33,16,128]{2,1,0:T(8,128)(2,1)S(1)}, bf16[33,16,128]{2,1,0:T(8,128)(2,1)S(1)}, u32[]{:S(2)}, u32[]{:S(2)}) collective-permute-start(bf16[33,16,128]{2,1,0:T(8,128)(2,1)S(1)} %collective-permute-done.refs_1_), channel_id=1, source_target_pairs={{0,1},{1,2},{2,3},{3,4},{4,5},{5,6},{6,7},{7,0},{8,9},{9,10},{10,1... | collective-permute-start | bytes 405512 | tf_op jit(solution)/shard_map/ppermute | solution.py:348
  13.1 10.3 %collective-permute-start.6 = (bf16[33,16,128]{2,1,0:T(8,128)(2,1)S(1)}, bf16[33,16,128]{2,1,0:T(8,128)(2,1)S(1)}, u32[]{:S(2)}, u32[]{:S(2)}) collective-permute-start(bf16[33,16,128]{2,1,0:T(8,128)(2,1)S(1)} %shard_map.55.refs_0_), channel_id=1, source_target_pairs={{0,4},{1,5},{2,6},{3,7},{4,0},{5,1},{6,2},{7,3},{8,12},{9,13},{10,... | collective-permute-start | bytes 405512 | tf_op jit(solution)/shard_map/ppermute | solution.py:352
  15.1 8.5 %collective-permute-start.5 = (bf16[33,16,128]{2,1,0:T(8,128)(2,1)S(1)}, bf16[33,16,128]{2,1,0:T(8,128)(2,1)S(1)}, u32[]{:S(2)}, u32[]{:S(2)}) collective-permute-start(bf16[33,16,128]{2,1,0:T(8,128)(2,1)S(1)} %collective-permute-done.3.refs_4_), channel_id=1, source_target_pairs={{0,7},{1,0},{2,1},{3,2},{4,3},{5,4},{6,5},{7,6},{8,15},{9,8},{10,9... | collective-permute-start | bytes 405512 | tf_op jit(solution)/shard_map/ppermute | solution.py:349
  23.4 5.1 %collective-permute-start.4 = (bf16[33,16,128]{2,1,0:T(8,128)(2,1)S(1)}, bf16[33,16,128]{2,1,0:T(8,128)(2,1)S(1)}, u32[]{:S(2)}, u32[]{:S(2)}) collective-permute-start(bf16[33,16,128]{2,1,0:T(8,128)(2,1)S(1)} %collective-permute-done.2.refs_3_), channel_id=1, source_target_pairs={{0,1},{1,2},{2,3},{3,4},{4,5},{5,6},{6,7},{7,0},{8,9},{9,10},{10,1... | collective-permute-start | bytes 405512 | tf_op jit(solution)/shard_map/ppermute | solution.py:348
